TPU v7x, 512 devices: a whole 4x8x8 slice. The times are simulated.
512 devices in a mesh: rng: 32 (over z, x), az: 16 (over y, core).
Axes of the slice: x: 4, y: 8, z: 8, core: 2. Of those that a mesh axis runs over, the one named last changes fastest.
Arguments:
- sar_image: float32 [2, 2048, 16384], P(None, 'rng', 'az'), may hold values from -6 to 6
- strong_index: int32 [1024], P('rng'), may hold values from 0 to 2047, as said below
- shifts: int32 [1024], P('rng'), may hold values from 0 to 16383
- widths: int32 [1024], P('rng'), may hold values from 256 to 2048
Outputs:
- focused_image: float32 [2, 2048, 16384], P(None, 'rng', 'az')
- phase_error: float32 [16384], P('az')
Inputs may be any that keep to these rules, and one draw needn't show every extreme that they name: `strong_index`: entries r * 32 to (r + 1) * 32 - 1 are distinct range bins of the block r * 64 to (r + 1) * 64 - 1.
All inputs are finite; a program needn't handle non-finite values.
Results may differ from a plain program's by a relative error of at most 0.0003.
Values sent between devices are 32-bit elements; how exact they have to be, the bound alone decides.
No kernel may reach another device: no remote copies, remote signals or barrier semaphores. Data moves between devices by JAX's collectives and lax.ppermute only.
A program may use at most 64 MiB of HBM per device.

v0:
```python
import math

import jax
import jax.numpy as jnp
from jax import lax
from jax.sharding import PartitionSpec as P

ITERS = 2


epsilon = 1e-06


def make_tables(pulses):
    first = max((factor for factor in range(1, math.isqrt(pulses) + 1) if pulses % factor == 0))
    second = pulses // first

    def table(count_rows, count_cols, modulus):
        product = (
            jnp.arange(count_rows, dtype=jnp.int32)[:, None]
            * jnp.arange(count_cols, dtype=jnp.int32)[None, :]
            % modulus
        )
        angle = -2.0 * math.pi / modulus * product.astype(jnp.float32)
        return (jnp.cos(angle), jnp.sin(angle))

    return (
        first,
        second,
        table(second, second, second),
        table(second, first, pulses),
        table(first, first, first),
    )


def complex_product(real_part, imag_part, matrix, form):

    def single(left, right):
        return jnp.einsum(form, left, right, precision=lax.Precision.HIGHEST)

    return (
        single(real_part, matrix[0]) - single(imag_part, matrix[1]),
        single(real_part, matrix[1]) + single(imag_part, matrix[0]),
    )


def forward(real_part, imag_part, tables):
    first, second, outer, twist, inner = tables
    count = real_part.shape[0]
    pulses = real_part.shape[1]
    section_r, section_i = complex_product(
        real_part.reshape(count, second, first),
        imag_part.reshape(count, second, first),
        outer,
        "rab,ak->rkb",
    )
    turned_r = section_r * twist[0] - section_i * twist[1]
    turned_i = section_r * twist[1] + section_i * twist[0]
    final_r, final_i = complex_product(turned_r, turned_i, inner, "rkb,bj->rjk")
    factor = 1.0 / math.sqrt(pulses)
    return (final_r.reshape(count, pulses) * factor, final_i.reshape(count, pulses) * factor)


def inverse(real_part, imag_part, tables):
    out_r, out_i = forward(real_part, -imag_part, tables)
    return (out_r, -out_i)


def correct(hist_r, hist_i, total):
    cosine = jnp.cos(total)[None, :]
    sine = jnp.sin(total)[None, :]
    return (hist_r * cosine + hist_i * sine, hist_i * cosine - hist_r * sine)


def center_window(real_part, imag_part, line_shift, line_width):
    pulses = real_part.shape[1]
    cells = jnp.arange(pulses, dtype=jnp.int32)
    starts = (line_shift - pulses // 2) % pulses
    lower = pulses // 2 - line_width // 2
    inside = (
        (cells[None, :] >= lower[:, None]) & (cells[None, :] < (lower + line_width)[:, None])
    ).astype(jnp.float32)
    stacked = jnp.stack([real_part, imag_part])
    doubled = jnp.concatenate([stacked, stacked], axis=2)

    def roll_row(row, begin):
        return lax.dynamic_slice_in_dim(row, begin, pulses, 1)

    moved = jax.vmap(roll_row, in_axes=(1, 0), out_axes=1)(doubled, starts)
    return (moved[0] * inside, moved[1] * inside)


def gradient_terms(spec_r, spec_i):
    cross = jnp.sum(spec_r[:, :-1] * spec_i[:, 1:] - spec_i[:, :-1] * spec_r[:, 1:], axis=0)
    numerator = jnp.concatenate([jnp.zeros((1,), jnp.float32), cross])
    denominator = jnp.sum(spec_r * spec_r + spec_i * spec_i, axis=0)
    return (numerator, denominator)


def phase_step(numerator, denominator):
    summed_num, summed_den = lax.psum((numerator, denominator), ("rng", "az"))
    return jnp.cumsum(summed_num / (summed_den + epsilon))


def local(sar_image, strong_index, shifts, widths):
    bins_local = sar_image.shape[1]
    pulses_local = sar_image.shape[2]
    rows = lax.all_to_all(sar_image, "az", split_axis=1, concat_axis=2, tiled=True)
    pulses = rows.shape[2]
    tables = make_tables(pulses)
    hist_r, hist_i = forward(rows[0], rows[1], tables)
    local_strong = strong_index % bins_local
    total = jnp.zeros((pulses,), jnp.float32)
    count = rows.shape[1]
    row_ids = lax.axis_index("az") * count + jnp.arange(count, dtype=jnp.int32)
    matches = (row_ids[:, None] == local_strong[None, :]).astype(jnp.int32)
    line_shift = jnp.sum(matches * shifts[None, :], axis=1)
    line_width = jnp.sum(matches * widths[None, :], axis=1)
    for step in range(ITERS):
        if step == 0:
            lines_r, lines_i = (rows[0], rows[1])
        else:
            lines_r, lines_i = inverse(*correct(hist_r, hist_i, total), tables)
        centered_r, centered_i = center_window(lines_r, lines_i, line_shift, line_width)
        spec_r, spec_i = forward(centered_r, centered_i, tables)
        total = total + phase_step(*gradient_terms(spec_r, spec_i))
    final_r, final_i = inverse(*correct(hist_r, hist_i, total), tables)
    focused_image = lax.all_to_all(
        jnp.stack([final_r, final_i]), "az", split_axis=2, concat_axis=1, tiled=True
    )
    phase_error = lax.dynamic_slice_in_dim(total, lax.axis_index("az") * pulses_local, pulses_local)
    return (focused_image, phase_error)


def solution(mesh):
    placed = (P(None, "rng", "az"), P("rng"), P("rng"), P("rng"))
    return jax.shard_map(
        local,
        mesh=mesh,
        in_specs=placed,
        out_specs=(P(None, "rng", "az"), P("az")),
        check_vma=False,
    )
```

profile of v0, /device:TPU:1, one launch (start us, length us, event | category | flops | bytes accessed | tf_op | source)
XLA Modules:
  0.0 739.3 jit_solution(12912270436124720808)
XLA Ops:
  7.2 2.2 copy.80
  9.4 10.2 %all-to-all-start = ((f32[2,64,1024]{2,0,1:T(2,128)}), f32[2,64,1024]{2,0,1:T(2,128)S(1)}, u32[]{:S(2)}, u32[]{:S(2)}) async-start(f32[2,64,1024]{2,0,1:T(2,128)} %copy.80), calls=%async_computation | async-start | bytes 1048576 | tf_op jit(solution)/shard_map/all_to_all | solution.py:108
  20.4 0.9 fusion.175
  22.2 14.8 %all-to-all-done = f32[2,64,1024]{2,0,1:T(2,128)S(1)} async-done(((f32[2,64,1024]{2,0,1:T(2,128)}), f32[2,64,1024]{2,0,1:T(2,128)S(1)}, u32[]{:S(2)}, u32[]{:S(2)}) %all-to-all-start) | async-done | bytes 524320 | tf_op jit(solution)/shard_map/all_to_all | solution.py:108
  42.0 0.9 maximum_bitcast_fusion
  43.1 8.6 %while.2 = (s32[]{:T(128)}, f32[4,2,32768]{2,1,0:T(2,128)S(1)}, s32[4,3]{1,0:T(4,128)S(1)}, f32[4,2,16384]{2,1,0:T(2,128)S(1)}, s32[]{:T(128)}) while((s32[]{:T(128)}, f32[4,2,32768]{2,1,0:T(2,128)S(1)}, s32[4,3]{1,0:T(4,128)S(1)}, f32[4,2,16384]{2,1,0:T(2,128)S(1)}, s32[]{:T(128)}) %tuple.57), condition=%wide.while_cond, body=%wide.while_body.sunk | while | flops 2 | bytes 262269 | solution.py:87
  44.0 1.5 dynamic-slice_dynamic-update-slice_fusion.4
  46.1 1.5 dynamic-slice_dynamic-update-slice_fusion.4
  48.2 1.5 dynamic-slice_dynamic-update-slice_fusion.4
  50.3 1.5 dynamic-slice_dynamic-update-slice_fusion.4
  52.2 0.7 fusion.66
  52.9 0.7 fusion.68
  53.6 0.7 convolution_add_fusion.8
  54.3 0.7 convolution_subtract_fusion.7
  55.0 0.7 fusion.48
  57.1 0.7 fusion.11
  57.8 1.3 add_reduce_fusion.1
  59.8 0.7 pad_maximum_fusion.2
  61.8 259.7 %all-reduce.8.cloned.1.call-done = (f32[16384]{0:T(1024)}, f32[16384]{0:T(1024)}) async-done(((f32[16384]{0:T(1024)}, f32[16384]{0:T(1024)}), (f32[16384]{0:T(1024)}, f32[16384]{0:T(1024)})) %all-reduce.8.cloned.1.call-update) | async-done | bytes 131088 | tf_op jit(solution)/shard_map/psum | solution.py:101
  321.5 0.9 divide_bitcast_fusion.1
  324.9 0.7 convolution_add_fusion.5
  327.7 0.7 fusion.8
  328.3 0.7 fusion.9
  329.0 0.9 maximum_bitcast_fusion.1
  330.1 9.0 %while.3 = (s32[]{:T(128)}, f32[4,2,32768]{2,1,0:T(2,128)S(1)}, s32[4,3]{1,0:T(4,128)S(1)}, f32[4,2,16384]{2,1,0:T(2,128)S(1)}, s32[]{:T(128)}) while((s32[]{:T(128)}, f32[4,2,32768]{2,1,0:T(2,128)S(1)}, s32[4,3]{1,0:T(4,128)S(1)}, f32[4,2,16384]{2,1,0:T(2,128)S(1)}, s32[]{:T(128)}) %tuple.69), condition=%wide.while_cond.1, body=%wide.while_body.1.sunk | while | flops 2 | bytes 262269 | solution.py:87
  330.9 1.6 dynamic-slice_dynamic-update-slice_fusion.5
  333.2 1.6 dynamic-slice_dynamic-update-slice_fusion.5
  335.4 1.6 dynamic-slice_dynamic-update-slice_fusion.5
  337.6 1.6 dynamic-slice_dynamic-update-slice_fusion.5
  339.6 0.7 fusion.60
  340.3 0.7 fusion.62
  341.0 0.7 convolution_add_fusion.3
  341.7 0.7 convolution_subtract_fusion.3
  342.5 0.7 fusion.30
  343.9 0.7 fusion.6
  344.5 1.4 add_reduce_fusion
  346.6 0.7 pad_maximum_fusion.1
  347.3 255.9 %all-reduce.6.cloned.1.call-done = (f32[16384]{0:T(1024)}, f32[16384]{0:T(1024)}) async-done(((f32[16384]{0:T(1024)}, f32[16384]{0:T(1024)}), (f32[16384]{0:T(1024)}, f32[16384]{0:T(1024)})) %all-reduce.6.cloned.1.call-update) | async-done | bytes 131088 | tf_op jit(solution)/shard_map/psum | solution.py:101
  603.3 0.9 divide_bitcast_fusion
  606.9 0.7 convolution_add_fusion.1
  611.3 14.8 %copy.97 = f32[2,4,16384]{1,0,2:T(2,128)} copy(f32[2,4,16384]{2,1,0:T(4,128)S(1)} %pad_maximum_fusion) | data formatting | bytes 1048576 | tf_op jit(solution)/shard_map/stack | solution.py:129
  626.2 27.8 %reshape.443 = f32[16,1,8192]{2,1,0:T(1,128)} reshape(f32[16384,2,4]{2,1,0:T(2,128)} %bitcast.240) | data formatting | bytes 1048576
  654.0 5.0 all-to-all-start.1
  659.7 16.6 %all-to-all-done.1 = f32[16,1,8192]{2,1,0:T(1,128)S(1)} async-done(((f32[16,1,8192]{2,1,0:T(1,128)}), f32[16,1,8192]{2,1,0:T(1,128)S(1)}, u32[]{:S(2)}, u32[]{:S(2)}) %all-to-all-start.1) | async-done | bytes 524320 | tf_op jit(solution)/shard_map/all_to_all | solution.py:128
  676.8 1.9 reduce.8
  678.7 32.0 %reshape.444 = f32[16384,2,4]{2,1,0:T(2,128)} reshape(f32[16,8192]{1,0:T(8,128)S(1)} %reduce.8) | data formatting | bytes 1048576
  710.7 20.6 %copy.98 = f32[2,16,4,1024]{3,2,1,0:T(4,128)S(1)} copy(f32[2,16,4,1024]{2,0,3,1:T(2,128)} %bitcast.241) | data formatting | bytes 1048576 | tf_op jit(solution)/shard_map/all_to_all | solution.py:128
  731.2 1.0 all_to_all.30
  (95 shorter events, 29.2 us)
Async XLA Ops:
  9.4 27.6 %all-to-all-start = ((f32[2,64,1024]{2,0,1:T(2,128)}), f32[2,64,1024]{2,0,1:T(2,128)S(1)}, u32[]{:S(2)}, u32[]{:S(2)}) async-start(f32[2,64,1024]{2,0,1:T(2,128)} %copy.80), calls=%async_computation | async-start | bytes 1048576 | tf_op jit(solution)/shard_map/all_to_all | solution.py:108
  19.6 301.9 %all-reduce.8.cloned.1.call-start = ((), (), s32[]{:S(2)}) async-start(), calls=%async_computation.3 | async-start | bytes 262144 | tf_op jit(solution)/shard_map/psum | solution.py:101
  60.6 542.7 %all-reduce.6.cloned.1.call-start = ((), (), s32[]{:S(2)}) async-start(), calls=%async_computation.2 | async-start | bytes 262144 | tf_op jit(solution)/shard_map/psum | solution.py:101
  654.0 22.3 %all-to-all-start.1 = ((f32[16,1,8192]{2,1,0:T(1,128)}), f32[16,1,8192]{2,1,0:T(1,128)S(1)}, u32[]{:S(2)}, u32[]{:S(2)}) async-start(f32[16,1,8192]{2,1,0:T(1,128)} %reshape.443), calls=%async_computation.1 | async-start | bytes 1048576 | tf_op jit(solution)/shard_map/all_to_all | solution.py:128
Sparse Core Ops, SparseCore 0:
  60.7 260.7 all-reduce.7
  347.5 255.7 all-reduce.5
where the time goes:
time: 746 us; the launch traced here: 739 us
  waiting for transfers between devices  547 us (73%)
  local copies, waits for them, and re-layouts  121 us (16%)
  matrix products  28.6 us (4%)
  starting transfers between devices  15.8 us (2%)
  between operations  14.9 us (2%)
  other arithmetic  11.3 us (2%)
    psum x2, waiting for transfers between devices, phase_step(): summed_num, summed_den = lax.psum((numerator, denominator), ('rng', 'az'))  516 us
    unnamed x9, local copies, waits for them, and re-layouts  62.7 us
    dot_general x40, matrix products, single(): return jnp.einsum(form, left, right, precision=lax.Precision.HIGHEST)  28.6 us
    all_to_all x3, local copies, waits for them, and re-layouts, local(): lax.all_to_all(jnp.stack([final_r, final_i]), 'az', split_axis=2, concat_...  22.1 us
    gather x24, local copies, waits for them, and re-layouts  17 us
    all_to_all x1, waiting for transfers between devices, local(): lax.all_to_all(jnp.stack([final_r, final_i]), 'az', split_axis=2, concat_...  16.6 us
  transfers between devices with their start and end apart: 4, of which 4 were waited for; matrix products, arithmetic and copies ran while one was open for 1% of the time, Pallas kernels for 0%

commit v1 on v0

v1 whole, which is shorter than its diff:
```python
import math

import jax
import jax.numpy as jnp
import numpy as np
from jax import lax
from jax.experimental import pallas as pl
from jax.experimental.pallas import tpu as pltpu
from jax.sharding import PartitionSpec as P

EPSILON = 1e-06
SIDE = 128
SUB = 8
HIGHEST = lax.Precision.HIGHEST


def tables():
    grid = np.arange(SIDE)
    product = grid[:, None] * grid[None, :]
    angle = 2.0 * np.pi * (product % SIDE) / SIDE
    cosine, sine = np.cos(angle), np.sin(angle)
    right = np.block([[cosine, -sine], [sine, cosine]])
    twist = 2.0 * np.pi * product / (SIDE * SIDE)
    twist = np.stack([np.cos(twist), np.sin(twist)]) / SIDE
    return right.astype(np.float32), np.ascontiguousarray(right.T).astype(np.float32), twist.astype(np.float32)


def multiply(left, right):
    return jnp.dot(left, right, precision=HIGHEST, preferred_element_type=jnp.float32)


def forward(lines, right, right_t, twist):
    cosine, sine = twist
    stacked = jnp.concatenate([jnp.concatenate(line, axis=0) for line in lines], axis=1)
    first = multiply(right_t, stacked)
    turned = []
    for at in range(len(lines)):
        real = first[:SIDE, at * SIDE : (at + 1) * SIDE]
        imag = first[SIDE:, at * SIDE : (at + 1) * SIDE]
        turned.append(jnp.concatenate([real * cosine + imag * sine, imag * cosine - real * sine], axis=1))
    second = multiply(jnp.concatenate(turned, axis=0), right)
    return [
        (second[at * SIDE : (at + 1) * SIDE, :SIDE], second[at * SIDE : (at + 1) * SIDE, SIDE:])
        for at in range(len(lines))
    ]


def inverse(lines, right, right_t, twist):
    cosine, sine = twist
    stacked = jnp.concatenate([jnp.concatenate(line, axis=1) for line in lines], axis=0)
    first = multiply(stacked, right_t)
    turned = []
    for at in range(len(lines)):
        real = first[at * SIDE : (at + 1) * SIDE, :SIDE]
        imag = first[at * SIDE : (at + 1) * SIDE, SIDE:]
        turned.append(jnp.concatenate([real * cosine - imag * sine, imag * cosine + real * sine], axis=0))
    second = multiply(right, jnp.concatenate(turned, axis=1))
    return [
        (second[:SIDE, at * SIDE : (at + 1) * SIDE], second[SIDE:, at * SIDE : (at + 1) * SIDE])
        for at in range(len(lines))
    ]


def running_sum(gradient):
    rows = lax.broadcasted_iota(jnp.int32, (SIDE, SIDE), 0)
    cols = lax.broadcasted_iota(jnp.int32, (SIDE, SIDE), 1)
    within = multiply((cols <= rows).astype(jnp.float32), gradient)
    sums = jnp.broadcast_to(within[SIDE - 1 :, :], (SUB, SIDE))
    before = multiply(sums, (rows < cols).astype(jnp.float32))
    return within + before[:1, :]


def window_lines(lines, a_index, shifts_ref, widths_ref):
    rows = lax.broadcasted_iota(jnp.int32, (SIDE, SIDE), 0)
    cols = lax.broadcasted_iota(jnp.int32, (SIDE, SIDE), 1)
    cells = rows * SIDE + cols
    pulses = SIDE * SIDE
    out = []
    for at, (real, imag) in enumerate(lines):
        line = a_index * len(lines) + at
        width = widths_ref[line]
        start = shifts_ref[line] - width // 2
        inside = ((cells - start) & (pulses - 1)) < width
        out.append((jnp.where(inside, real, 0.0), jnp.where(inside, imag, 0.0)))
    return out


def gradient_sums(lines, a_index, shifts_ref):
    rows = lax.broadcasted_iota(jnp.int32, (SIDE, SIDE), 0)
    cols = lax.broadcasted_iota(jnp.int32, (SIDE, SIDE), 1)
    pulses = SIDE * SIDE
    numerator = jnp.zeros((SIDE, SIDE), jnp.float32)
    denominator = jnp.zeros((SIDE, SIDE), jnp.float32)

    def before(part):
        down = pltpu.roll(part, 1, 0)
        return jnp.where(rows == 0, pltpu.roll(down, 1, 1), down)

    for at, (real, imag) in enumerate(lines):
        shift = shifts_ref[a_index * len(lines) + at] - pulses // 2
        angle = jnp.full((SUB, SIDE), shift, jnp.int32).astype(jnp.float32) * (2.0 * math.pi / pulses)
        turn_r, turn_i = jnp.cos(angle)[:1, :], jnp.sin(angle)[:1, :]
        real_b, imag_b = before(real), before(imag)
        cross_r = real_b * real + imag_b * imag
        cross_i = real_b * imag - imag_b * real
        numerator = numerator + (cross_i * turn_r + cross_r * turn_i)
        denominator = denominator + (real * real + imag * imag)
    first = jnp.logical_and(rows == 0, cols == 0)
    return jnp.where(first, 0.0, numerator), denominator


def turn_back(lines, total):
    cosine, sine = jnp.cos(total), jnp.sin(total)
    return [(real * cosine + imag * sine, imag * cosine - real * sine) for real, imag in lines]


def square(ref, *at):
    return ref[(slice(None),) + at].reshape(SIDE, SIDE)


def store_sums(out_ref, numerator, denominator):
    out_ref[:, 0] = numerator.reshape(SIDE // SUB, SUB, SIDE)
    out_ref[:, 1] = denominator.reshape(SIDE // SUB, SUB, SIDE)


def pack_kernel(strong_ref, image_ref, out_ref, place_ref, tiles_ref):
    bins = image_ref.shape[1]
    strong = strong_ref.shape[0]

    def clear(at, carry):
        place_ref[at] = -1
        return carry

    def mark(at, carry):
        place_ref[strong_ref[at] % bins] = at
        return carry

    def count(at, others):
        held = place_ref[at]
        other = held < 0
        here = jnp.where(other, others, held)
        slot = here % 2 + jnp.where(other, 2, 0)
        place_ref[at] = (here // 2) * 4 + slot
        return others + jnp.where(other, 1, 0)

    lax.fori_loop(0, bins, clear, 0)
    lax.fori_loop(0, strong, mark, 0)
    lax.fori_loop(0, bins, count, 0)
    for part in range(2):
        for group in range(bins // SUB):
            for block in range(SUB):
                at = ((part * (bins // SUB) + group) * SUB + block) * SUB
                tiles_ref[pl.ds(at, SUB), :] = image_ref[
                    part, group * SUB : (group + 1) * SUB, block * SIDE : (block + 1) * SIDE
                ]
    for row in range(bins):
        place = place_ref[row]
        device, slot = place // 4, place % 4
        for part in range(2):
            at = (part * (bins // SUB) + row // SUB) * SUB * SUB + row % SUB
            out_ref[device, part * 4 + slot] = tiles_ref[pl.ds(at, SUB, stride=SUB), :]


def unpack_kernel(place_ref, rows_ref, image_ref, tiles_ref):
    bins = image_ref.shape[1]
    for row in range(bins):
        place = place_ref[row]
        device, slot = place // 4, place % 4
        for part in range(2):
            at = (part * (bins // SUB) + row // SUB) * SUB * SUB + row % SUB
            tiles_ref[pl.ds(at, SUB, stride=SUB), :] = rows_ref[device, part * 4 + slot]
    for part in range(2):
        for group in range(bins // SUB):
            for block in range(SUB):
                at = ((part * (bins // SUB) + group) * SUB + block) * SUB
                image_ref[part, group * SUB : (group + 1) * SUB, block * SIDE : (block + 1) * SIDE] = tiles_ref[
                    pl.ds(at, SUB), :
                ]


def first_kernel(a_ref, shifts_ref, widths_ref, rows_ref, right_ref, right_t_ref, twist_ref, out_ref):
    a_index = a_ref[0]
    consts = (right_ref[...], right_t_ref[...], (twist_ref[0], twist_ref[1]))
    lines = [(square(rows_ref, at), square(rows_ref, 4 + at)) for at in range(2)]
    spectra = forward(window_lines(lines, a_index, shifts_ref, widths_ref), *consts)
    store_sums(out_ref, *gradient_sums(spectra, a_index, shifts_ref))


def history_kernel(rows_ref, right_ref, right_t_ref, twist_ref, out_ref):
    consts = (right_ref[...], right_t_ref[...], (twist_ref[0], twist_ref[1]))
    lines = [(square(rows_ref, at), square(rows_ref, 4 + at)) for at in range(4)]
    for at, (real, imag) in enumerate(forward(lines, *consts)):
        out_ref[at, 0] = real
        out_ref[at, 1] = imag


def gather_sums_kernel(in_ref, out_ref):
    out_ref[...] = jnp.broadcast_to(jnp.sum(in_ref[...], axis=0)[None], out_ref.shape)


def gradient_kernel(in_ref, out_ref):
    sums = jnp.sum(in_ref[...], axis=0)
    gradient = sums[0] / (sums[1] + EPSILON)
    out_ref[...] = jnp.broadcast_to(gradient[None], out_ref.shape)


def second_kernel(
    a_ref, shifts_ref, widths_ref, gradient_ref, history_ref, right_ref, right_t_ref, twist_ref, out_ref, total_ref
):
    a_index = a_ref[0]
    consts = (right_ref[...], right_t_ref[...], (twist_ref[0], twist_ref[1]))
    total = running_sum(gradient_ref[...].reshape(SIDE, SIDE))
    total_ref[...] = total
    lines = [(history_ref[at, 0], history_ref[at, 1]) for at in range(2)]
    lines = inverse(turn_back(lines, total), *consts)
    spectra = forward(window_lines(lines, a_index, shifts_ref, widths_ref), *consts)
    store_sums(out_ref, *gradient_sums(spectra, a_index, shifts_ref))


def final_kernel(
    a_ref, gradient_ref, total_ref, history_ref, right_ref, right_t_ref, twist_ref, out_ref, phase_ref, turned_ref
):
    a_index = a_ref[0]
    consts = (right_ref[...], right_t_ref[...], (twist_ref[0], twist_ref[1]))
    total = total_ref[...] + running_sum(gradient_ref[...].reshape(SIDE, SIDE))
    turned_ref[...] = total.T
    phase_ref[...] = turned_ref[pl.ds(pl.multiple_of(a_index * SUB, SUB), SUB), :]
    lines = [(history_ref[at, 0], history_ref[at, 1]) for at in range(4)]
    for at, (real, imag) in enumerate(inverse(turn_back(lines, total), *consts)):
        out_ref[:, at] = real.reshape(SIDE // SUB, SUB, SIDE)
        out_ref[:, 4 + at] = imag.reshape(SIDE // SUB, SUB, SIDE)


SMEM = pl.BlockSpec(memory_space=pltpu.SMEM)
VMEM = pl.BlockSpec(memory_space=pltpu.VMEM)


def call(kernel, shapes, specs, *operands, scratch=(), out_specs=None):
    out_shape = [jax.ShapeDtypeStruct(*shape) for shape in shapes]
    out = pl.pallas_call(
        kernel,
        out_shape=out_shape,
        in_specs=list(specs),
        out_specs=out_specs or [VMEM] * len(out_shape),
        scratch_shapes=list(scratch),
        compiler_params=pltpu.CompilerParams(vmem_limit_bytes=32 * 1024 * 1024),
    )(*operands)
    return out if len(out) > 1 else out[0]


def exchange(array, axis):
    return lax.all_to_all(array, axis, split_axis=0, concat_axis=0, tiled=True)


def local(sar_image, strong_index, shifts, widths):
    f32 = jnp.float32
    az, rng = lax.axis_size("az"), lax.axis_size("rng")
    bins, pulses_local = sar_image.shape[1:]
    consts = tuple(jnp.asarray(table) for table in tables())
    a_index = lax.axis_index("az").astype(jnp.int32).reshape(1)
    tile = (SUB, SIDE)

    packed, place = call(
        pack_kernel,
        [((az, 8) + tile, f32), ((bins,), jnp.int32)],
        [SMEM, VMEM],
        strong_index,
        sar_image,
        scratch=[pltpu.VMEM((2 * bins * SUB, SIDE), f32)],
        out_specs=[VMEM, SMEM],
    )
    rows = exchange(packed, "az")
    sums = call(
        first_kernel,
        [((az, 2) + tile, f32)],
        [SMEM, SMEM, SMEM, VMEM, VMEM, VMEM, VMEM],
        a_index,
        shifts,
        widths,
        rows,
        *consts,
    )
    history = call(history_kernel, [((4, 2, SIDE, SIDE), f32)], [VMEM] * 4, rows, *consts)

    def all_gradient(sums):
        scattered = exchange(sums, "az")
        partial = call(gather_sums_kernel, [((rng, 2) + tile, f32)], [VMEM], scattered)
        everyone = exchange(partial, "rng")
        gradient = call(gradient_kernel, [((az,) + tile, f32)], [VMEM], everyone)
        return exchange(gradient, "az")

    gradient = all_gradient(sums)
    sums, total = call(
        second_kernel,
        [((az, 2) + tile, f32), ((SIDE, SIDE), f32)],
        [SMEM, SMEM, SMEM, VMEM, VMEM, VMEM, VMEM, VMEM],
        a_index,
        shifts,
        widths,
        gradient,
        history,
        *consts,
    )
    gradient = all_gradient(sums)
    corrected, phase = call(
        final_kernel,
        [((az, 8) + tile, f32), (tile, f32)],
        [SMEM] + [VMEM] * 6,
        a_index,
        gradient,
        total,
        history,
        *consts,
        scratch=[pltpu.VMEM((SIDE, SIDE), f32)],
    )
    returned = exchange(corrected, "az")
    focused = call(
        unpack_kernel,
        [(sar_image.shape, f32)],
        [SMEM, VMEM],
        place,
        returned,
        scratch=[pltpu.VMEM((2 * bins * SUB, SIDE), f32)],
    )
    return focused, phase.reshape(pulses_local)


def solution(mesh):
    placed = (P(None, "rng", "az"), P("rng"), P("rng"), P("rng"))
    return jax.shard_map(
        local,
        mesh=mesh,
        in_specs=placed,
        out_specs=(P(None, "rng", "az"), P("az")),
        check_vma=False,
    )
```

time: 746 us -> 152 us (0.20)
  waiting for transfers between devices: 547 us -> 24 us
  local copies, waits for them, and re-layouts: 121 us -> 1.72 us
  blocking collectives: 0 us -> 94.3 us
  matrix products: 28.6 us -> 0 us
  Pallas kernels: 0 us -> 15.4 us
  between operations: 14.9 us -> 0.73 us
  other arithmetic: 11.3 us -> 0 us
    psum x2 -> x0, waiting for transfers between devices: 516 us -> none  [phase_step(): summed_num, summed_den = lax.psum((numerator, denominator), ('rng', 'az'))]
    all_to_all x0 -> x6, blocking collectives: none -> 94.3 us  [exchange(): return lax.all_to_all(array, axis, split_axis=0, concat_axis=0, tiled=True)]
    unnamed x9 -> x14, local copies, waits for them, and re-layouts: 62.7 us -> 1.72 us
    dot_general x40 -> x0, matrix products: 28.6 us -> none  [single(): return jnp.einsum(form, left, right, precision=lax.Precision.HIGHEST)]
    all_to_all x4 -> x0, local copies, waits for them, and re-layouts: 22.4 us -> none  [the longest x3 22.1 us: local(): lax.all_to_all(jnp.stack([final_r, final_i]), 'az', split_axis=2, concat_...]
    gather x24 -> x0, local copies, waits for them, and re-layouts: 17 us -> none
    pallas_call x0 -> x10, Pallas kernels: none -> 15.4 us  [call(): pl.pallas_call(kernel, out_shape=out_shape, in_specs=list(specs), out_spe...]
    another operation x8 -> x0, local copies, waits for them, and re-layouts: 15.3 us -> none  [the longest x1 14.8 us: local(): jnp.stack([final_r, final_i])]
  transfers between devices with their start and end apart: 4 -> 2, of which waited for: 4 -> 2; matrix products, arithmetic and copies ran while one was open for 1% -> 0% of each run, Pallas kernels for 0% -> 1%
where the time goes in v1:
time: 152 us; the launch traced here: 151 us
  blocking collectives  94.3 us (62%)
  waiting for transfers between devices  24 us (16%)
  Pallas kernels  15.4 us (10%)
  starting transfers between devices  15.2 us (10%)
  local copies, waits for them, and re-layouts  1.72 us (1%)
    all_to_all x6, blocking collectives, exchange(): return lax.all_to_all(array, axis, split_axis=0, concat_axis=0, tiled=True)  94.3 us
    all_to_all x2, waiting for transfers between devices, exchange(): return lax.all_to_all(array, axis, split_axis=0, concat_axis=0, tiled=True)  24 us
    pallas_call x10, Pallas kernels, call(): pl.pallas_call(kernel, out_shape=out_shape, in_specs=list(specs), out_spe...  15.4 us
    all_to_all x2, starting transfers between devices, exchange(): return lax.all_to_all(array, axis, split_axis=0, concat_axis=0, tiled=True)  15.2 us
  transfers between devices with their start and end apart: 2, of which 2 were waited for; matrix products, arithmetic and copies ran while one was open for 0% of the time, Pallas kernels for 1%

profile of v1, /device:TPU:1, one launch (start us, length us, event | category | flops | bytes accessed | tf_op | source)
XLA Modules:
  0.0 151.4 jit_solution(709200163645301994)
XLA Ops:
  0.6 0.0 copy-start.3
  0.6 1.0 copy-done.3
  1.7 0.0 copy-start.6
  1.7 0.7 copy-done.6
  2.3 3.5 %shard_map.86 = (f32[16,8,8,128]{3,2,1,0:T(8,128)}, s32[64]{0:T(128)S(1)}) custom-call(s32[32]{0:T(128)S(1)} %copy-done.6, f32[2,64,1024]{2,1,0:T(8,128)S(1)} %copy-done.3), custom_call_target="tpu_custom_call" | custom-call | tf_op jit(solution)/shard_map/pallas_call | solution.py:240
  5.8 0.0 copy-start
  5.9 0.0 copy-start.1
  5.9 0.0 copy-start.2
  5.9 10.4 %all-to-all-start = ((f32[16,8,8,128]{3,2,1,0:T(8,128)}), f32[16,8,8,128]{3,2,1,0:T(8,128)S(1)}, u32[]{:S(2)}, u32[]{:S(2)}) async-start(f32[16,8,8,128]{3,2,1,0:T(8,128)} %get-tuple-element.9), calls=%async_computation | async-start | bytes 1048576 | tf_op jit(solution)/shard_map/all_to_all | solution.py:252
  16.3 0.0 copy-start.4
  16.3 0.0 copy-start.5
  16.3 17.3 %all-to-all-done.rows_ref = f32[16,8,8,128]{3,2,1,0:T(8,128)S(1)} async-done(((f32[16,8,8,128]{3,2,1,0:T(8,128)}), f32[16,8,8,128]{3,2,1,0:T(8,128)S(1)}, u32[]{:S(2)}, u32[]{:S(2)}) %all-to-all-start) | async-done | bytes 524320 | tf_op jit(solution)/shard_map/all_to_all | solution.py:252
  33.6 0.0 copy-done
  33.6 0.0 copy-done.1
  33.6 0.0 copy-done.2
  33.6 0.0 copy-done.4
  33.6 0.0 copy-done.5
  33.6 1.7 %shard_map.87 = f32[16,2,8,128]{3,2,1,0:T(8,128)S(1)} custom-call(s32[1]{0:T(128)} %bitcast.a_ref, s32[32]{0:T(128)S(1)} %copy-done.4, s32[32]{0:T(128)S(1)} %copy-done.5, f32[16,8,8,128]{3,2,1,0:T(8,128)S(1)} %all-to-all-done.rows_ref, f32[256,256]{1,0:T(8,128)S(1)} %copy-done.1, f32[256,256]{1,0:T(8,128)S(1)} %copy-done, f32[2,128,128]{2,1,0:T(8,128)S(1)} %copy-done.2), custom_call_target="tpu_custom_call" | custom-call | tf_op jit(solution)/shard_map/pallas_call | solution.py:240
  35.4 11.9 %all_to_all.40.in_ref = f32[16,2,8,128]{3,2,1,0:T(8,128)S(1)} all-to-all(f32[16,2,8,128]{3,2,1,0:T(8,128)S(1)} %shard_map.87), channel_id=1, replica_groups=mesh['rng'=32,'az'=16] {'az'}, dimensions={0} | all-to-all | bytes 262144 | tf_op jit(solution)/shard_map/all_to_all | solution.py:252
  47.3 23.3 %all_to_all.41.in_ref = f32[32,2,8,128]{3,2,1,0:T(8,128)S(1)} all-to-all(f32[32,2,8,128]{3,2,1,0:T(8,128)S(1)} %shard_map.88), channel_id=1, replica_groups=mesh['rng'=32,'az'=16] {'rng'}, dimensions={0} | all-to-all | bytes 524288 | tf_op jit(solution)/shard_map/all_to_all | solution.py:252
  70.6 0.7 shard_map.89
  71.2 4.9 %all-to-all-start.3 = ((f32[16,8,128]{2,1,0:T(8,128)}), f32[16,8,128]{2,1,0:T(8,128)S(1)}, u32[]{:S(2)}, u32[]{:S(2)}) async-start(f32[16,8,128]{2,1,0:T(8,128)} %shard_map.89), calls=%async_computation.3 | async-start | bytes 131072 | tf_op jit(solution)/shard_map/all_to_all | solution.py:252
  76.1 1.2 shard_map.90.history_ref
  77.3 6.7 %all-to-all-done.3.gradient_ref = f32[16,8,128]{2,1,0:T(8,128)S(1)} async-done(((f32[16,8,128]{2,1,0:T(8,128)}), f32[16,8,128]{2,1,0:T(8,128)S(1)}, u32[]{:S(2)}, u32[]{:S(2)}) %all-to-all-start.3) | async-done | bytes 65568 | tf_op jit(solution)/shard_map/all_to_all | solution.py:252
  83.9 3.4 %shard_map.91 = (f32[16,2,8,128]{3,2,1,0:T(8,128)S(1)}, f32[128,128]{1,0:T(8,128)S(1)}) custom-call(s32[1]{0:T(128)} %bitcast.a_ref, s32[32]{0:T(128)S(1)} %copy-done.4, s32[32]{0:T(128)S(1)} %copy-done.5, f32[16,8,128]{2,1,0:T(8,128)S(1)} %all-to-all-done.3.gradient_ref, f32[4,2,128,128]{3,2,1,0:T(8,128)S(1)} %shard_map.90.history_ref, ...), custom_call_target="tpu_custom_call" | custom-call | tf_op jit(solution)/shard_map/pallas_call | solution.py:240
  87.4 11.8 %all_to_all.42.in_ref = f32[16,2,8,128]{3,2,1,0:T(8,128)S(1)} all-to-all(f32[16,2,8,128]{3,2,1,0:T(8,128)S(1)} %get-tuple-element.10), channel_id=1, replica_groups=mesh['rng'=32,'az'=16] {'az'}, dimensions={0} | all-to-all | bytes 262144 | tf_op jit(solution)/shard_map/all_to_all | solution.py:252
  99.2 15.7 %all_to_all.43.in_ref = f32[32,2,8,128]{3,2,1,0:T(8,128)S(1)} all-to-all(f32[32,2,8,128]{3,2,1,0:T(8,128)S(1)} %shard_map.92), channel_id=1, replica_groups=mesh['rng'=32,'az'=16] {'rng'}, dimensions={0} | all-to-all | bytes 524288 | tf_op jit(solution)/shard_map/all_to_all | solution.py:252
  114.9 11.8 %all_to_all.44.gradient_ref = f32[16,8,128]{2,1,0:T(8,128)S(1)} all-to-all(f32[16,8,128]{2,1,0:T(8,128)S(1)} %shard_map.93), channel_id=1, replica_groups=mesh['rng'=32,'az'=16] {'az'}, dimensions={0} | all-to-all | bytes 131072 | tf_op jit(solution)/shard_map/all_to_all | solution.py:252
  126.7 3.0 %shard_map.94 = (f32[16,8,8,128]{3,2,1,0:T(8,128)S(1)}, f32[8,128]{1,0:T(8,128)}) custom-call(s32[1]{0:T(128)} %bitcast.a_ref, f32[16,8,128]{2,1,0:T(8,128)S(1)} %all_to_all.44.gradient_ref, f32[128,128]{1,0:T(8,128)S(1)} %get-tuple-element.11.total_ref, f32[4,2,128,128]{3,2,1,0:T(8,128)S(1)} %shard_map.90.history_ref, f32[256,256]{1,0:T(8,128)S(1)} %copy-done.1, ...), custom_call_target="tpu_custom_call" | custom-call | tf_op jit(solution)/shard_map/pallas_call | solution.py:240
  129.7 19.9 %all_to_all.45.rows_ref = f32[16,8,8,128]{3,2,1,0:T(8,128)S(1)} all-to-all(f32[16,8,8,128]{3,2,1,0:T(8,128)S(1)} %get-tuple-element.12), channel_id=1, replica_groups=mesh['rng'=32,'az'=16] {'az'}, dimensions={0} | all-to-all | bytes 1048576 | tf_op jit(solution)/shard_map/all_to_all | solution.py:252
  149.6 1.8 %shard_map.95 = f32[2,64,1024]{2,1,0:T(8,128)} custom-call(s32[64]{0:T(128)S(1)} %get-tuple-element.8.place_ref, f32[16,8,8,128]{3,2,1,0:T(8,128)S(1)} %all_to_all.45.rows_ref), custom_call_target="tpu_custom_call" | custom-call | tf_op jit(solution)/shard_map/pallas_call | solution.py:240
  (3 shorter events, 0.1 us)
Async XLA Ops:
  0.6 1.0 copy-start.3
  1.7 0.7 copy-start.6
  5.8 27.8 %copy-start = (f32[256,256]{1,0:T(8,128)S(1)}, f32[256,256]{1,0:T(8,128)}, u32[]{:S(2)}) copy-start(f32[256,256]{1,0:T(8,128)} %constant.11.clone.right_t_ref) | copy-start | bytes 786436
  5.9 27.8 %copy-start.1 = (f32[256,256]{1,0:T(8,128)S(1)}, f32[256,256]{1,0:T(8,128)}, u32[]{:S(2)}) copy-start(f32[256,256]{1,0:T(8,128)} %constant.10.clone.right_ref) | copy-start | bytes 786436
  5.9 27.8 %copy-start.2 = (f32[2,128,128]{2,1,0:T(8,128)S(1)}, f32[2,128,128]{2,1,0:T(8,128)}, u32[]{:S(2)}) copy-start(f32[2,128,128]{2,1,0:T(8,128)} %constant.12.clone.twist_ref) | copy-start | bytes 393220
  5.9 27.7 %all-to-all-start = ((f32[16,8,8,128]{3,2,1,0:T(8,128)}), f32[16,8,8,128]{3,2,1,0:T(8,128)S(1)}, u32[]{:S(2)}, u32[]{:S(2)}) async-start(f32[16,8,8,128]{3,2,1,0:T(8,128)} %get-tuple-element.9), calls=%async_computation | async-start | bytes 1048576 | tf_op jit(solution)/shard_map/all_to_all | solution.py:252
  16.3 17.4 %copy-start.4 = (s32[32]{0:T(128)S(1)}, s32[32]{0:T(128)}, u32[]{:S(2)}) copy-start(s32[32]{0:T(128)} %shifts_ref.3) | copy-start | bytes 388
  16.3 17.4 %copy-start.5 = (s32[32]{0:T(128)S(1)}, s32[32]{0:T(128)}, u32[]{:S(2)}) copy-start(s32[32]{0:T(128)} %widths_ref.3) | copy-start | bytes 388
  71.2 12.7 %all-to-all-start.3 = ((f32[16,8,128]{2,1,0:T(8,128)}), f32[16,8,128]{2,1,0:T(8,128)S(1)}, u32[]{:S(2)}, u32[]{:S(2)}) async-start(f32[16,8,128]{2,1,0:T(8,128)} %shard_map.89), calls=%async_computation.3 | async-start | bytes 131072 | tf_op jit(solution)/shard_map/all_to_all | solution.py:252

commit v2 on v1

v2 whole, which is shorter than its diff:
```python
import jax
import jax.numpy as jnp
import numpy as np
from jax import lax
from jax.experimental import pallas as pl
from jax.experimental.pallas import tpu as pltpu
from jax.sharding import Mesh, PartitionSpec as P

EPSILON = 1e-06
SIDE = 128
SUB = 8
TILES = SIDE // SUB
WINDOW = 16
FIRST = SIDE // 2 - WINDOW // 2
LOAD = 24
HIGHEST = lax.Precision.HIGHEST


def tables():
    grid = np.arange(SIDE)
    product = grid[:, None] * grid[None, :]
    angle = 2.0 * np.pi * (product % SIDE) / SIDE
    cosine, sine = np.cos(angle), np.sin(angle)
    right = np.block([[cosine, -sine], [sine, cosine]])
    rows = slice(FIRST, FIRST + WINDOW)
    window = np.block([[cosine[:, rows], sine[:, rows]], [-sine[:, rows], cosine[:, rows]]])
    around = np.arange(SIDE + LOAD) % SIDE
    ring = np.stack([cosine[around], sine[around]])
    twist = 2.0 * np.pi * product / (SIDE * SIDE)
    twist = np.stack([np.cos(twist), np.sin(twist)]) / SIDE
    made = dict(right=right, right_t=right.T, window=window, ring=ring, twist=twist)
    return {name: jnp.asarray(np.ascontiguousarray(table).astype(np.float32)) for name, table in made.items()}


def multiply(left, right):
    return jnp.dot(left, right, precision=HIGHEST, preferred_element_type=jnp.float32)


def forward(lines, left, right, twist_ref):
    cosine, sine = twist_ref[0], twist_ref[1]
    stacked = jnp.concatenate([jnp.concatenate(line, axis=0) for line in lines], axis=1)
    first = multiply(left, stacked)
    turned = []
    for at in range(len(lines)):
        real = first[:SIDE, at * SIDE : (at + 1) * SIDE]
        imag = first[SIDE:, at * SIDE : (at + 1) * SIDE]
        turned.append(jnp.concatenate([real * cosine + imag * sine, imag * cosine - real * sine], axis=1))
    second = multiply(jnp.concatenate(turned, axis=0), right)
    return [
        (second[at * SIDE : (at + 1) * SIDE, :SIDE], second[at * SIDE : (at + 1) * SIDE, SIDE:])
        for at in range(len(lines))
    ]


def inverse_start(lines, right_t, twist_ref):
    cosine, sine = twist_ref[0], twist_ref[1]
    stacked = jnp.concatenate([jnp.concatenate(line, axis=1) for line in lines], axis=0)
    first = multiply(stacked, right_t)
    turned = []
    for at in range(len(lines)):
        real = first[at * SIDE : (at + 1) * SIDE, :SIDE]
        imag = first[at * SIDE : (at + 1) * SIDE, SIDE:]
        turned.append(jnp.concatenate([real * cosine - imag * sine, imag * cosine + real * sine], axis=0))
    return turned


def grid_of(rows):
    return (
        lax.broadcasted_iota(jnp.int32, (rows, SIDE), 0),
        lax.broadcasted_iota(jnp.int32, (rows, SIDE), 1),
    )


def running_sum(gradient):
    rows, cols = grid_of(SIDE)
    within = multiply((cols <= rows).astype(jnp.float32), gradient)
    sums = jnp.broadcast_to(jnp.sum(gradient, axis=0, keepdims=True), (SUB, SIDE))
    before = multiply(sums, (rows < cols).astype(jnp.float32))
    return within + before[:1, :]


def phase_of(sums_ref):
    gradient = sums_ref[:TILES] / (sums_ref[TILES:] + EPSILON)
    return running_sum(gradient.reshape(SIDE, SIDE))


def cosine_sine(angle):
    quarters = jnp.floor(angle * (2.0 / np.pi) + 0.5)
    rest = angle - quarters * 1.5703125
    rest = rest - quarters * 4.837512969970703125e-4
    rest = rest - quarters * 7.54978995489188216e-8
    square = rest * rest
    sine = ((-1.9515295891e-4 * square + 8.3321608736e-3) * square - 1.6666654611e-1) * square * rest + rest
    cosine = (2.443315711809948e-5 * square - 1.388731625493765e-3) * square + 4.166664568298827e-2
    cosine = cosine * square * square - 0.5 * square + 1.0
    turn = quarters.astype(jnp.int32)
    odd = (turn & 1) == 1
    sine, cosine = jnp.where(odd, cosine, sine), jnp.where(odd, sine, cosine)
    return jnp.where(((turn + 1) & 2) == 2, -cosine, cosine), jnp.where((turn & 2) == 2, -sine, sine)


def turn_back(lines, total):
    cosine, sine = cosine_sine(total)
    return [(real * cosine + imag * sine, imag * cosine - real * sine) for real, imag in lines]


def row_offset(shift):
    begin = (shift + SIDE * SIDE // 2) & (SIDE * SIDE - 1)
    return ((begin >> 7) + FIRST) & (SIDE - 1), begin & (SIDE - 1)


def center(upper, lower, lane, width):
    rows, cols = grid_of(WINDOW)
    turn = (SIDE - lane) & (SIDE - 1)
    moved = jnp.where(cols >= SIDE - lane, pltpu.roll(lower, turn, 1), pltpu.roll(upper, turn, 1))
    cells = (rows + FIRST) * SIDE + cols
    least = SIDE * SIDE // 2 - width // 2
    return jnp.where((cells >= least) & (cells < least + width), moved, 0.0)


def gradient_sums(lines, out_ref):
    rows, cols = grid_of(SIDE)
    numerator = jnp.zeros((SIDE, SIDE), jnp.float32)
    denominator = jnp.zeros((SIDE, SIDE), jnp.float32)

    def before(part):
        down = pltpu.roll(part, 1, 0)
        return jnp.where(rows == 0, pltpu.roll(down, 1, 1), down)

    for real, imag in lines:
        numerator = numerator + (before(real) * imag - before(imag) * real)
        denominator = denominator + (real * real + imag * imag)
    numerator = jnp.where((rows == 0) & (cols == 0), 0.0, numerator)
    out_ref[:TILES] = numerator.reshape(TILES, SUB, SIDE)
    out_ref[TILES:] = denominator.reshape(TILES, SUB, SIDE)


def tile_at(bins, part, row):
    return (part * (bins // SUB) + row // SUB) * SUB * SUB + row % SUB


def pack_kernel(strong_hbm, image_hbm, out_ref, place_ref, strong_ref, image_ref, tiles_ref, small_sem, sems):
    bins = image_ref.shape[1]
    strong = strong_ref.shape[0]
    indices = pltpu.make_async_copy(strong_hbm, strong_ref, small_sem)
    indices.start()
    parts = [pltpu.make_async_copy(image_hbm.at[part], image_ref.at[part], sems.at[part]) for part in range(2)]
    for part in parts:
        part.start()
    for row in range(bins):
        place_ref[row] = -1
    indices.wait()
    for at in range(strong):
        place_ref[strong_ref[at] % bins] = at // 2 * 8 + at % 2
    others = jnp.int32(0)
    for row in range(bins):
        held = place_ref[row]
        place_ref[row] = jnp.where(held < 0, others // 2 * 8 + others % 2 + 2, held)
        others = others + jnp.where(held < 0, 1, 0)
    for part in range(2):
        parts[part].wait()
        for group in range(bins // SUB):
            for block in range(SUB):
                at = ((part * (bins // SUB) + group) * SUB + block) * SUB
                tiles_ref[at : at + SUB, :] = image_ref[
                    part, group * SUB : (group + 1) * SUB, block * SIDE : (block + 1) * SIDE
                ]
        for row in range(bins):
            out_ref[place_ref[row] + part * 4] = tiles_ref[pl.ds(tile_at(bins, part, row), SUB, stride=SUB), :]


def unpack_kernel(place_ref, rows_ref, image_hbm, image_ref, tiles_ref, sems):
    bins = image_ref.shape[1]
    copies = []
    for part in range(2):
        for row in range(bins):
            tiles_ref[pl.ds(tile_at(bins, part, row), SUB, stride=SUB), :] = rows_ref[place_ref[row] + part * 4]
        for half in range(2):
            span = slice(half * bins // 2, (half + 1) * bins // 2)
            for group in range(half * bins // 2 // SUB, (half + 1) * bins // 2 // SUB):
                for block in range(SUB):
                    at = ((part * (bins // SUB) + group) * SUB + block) * SUB
                    image_ref[part, group * SUB : (group + 1) * SUB, block * SIDE : (block + 1) * SIDE] = tiles_ref[
                        at : at + SUB, :
                    ]
            copies.append(
                pltpu.make_async_copy(
                    image_ref.at[part, span], image_hbm.at[part, span], sems.at[part * 2 + half]
                )
            )
            copies[-1].start()
    for copy in copies:
        copy.wait()


def first_kernel(a_ref, shifts_ref, widths_ref, rows_ref, window_ref, right_ref, twist_ref, out_ref, ring_ref):
    lines = []
    for at in range(2):
        line = a_ref[0] * 2 + at
        row, lane = row_offset(shifts_ref[line])
        parts = []
        for part in range(2):
            ring = ring_ref.at[at * 2 + part]
            ring[:SIDE, :] = rows_ref[:, part * 4 + at].reshape(SIDE, SIDE)
            ring[SIDE:, :] = rows_ref[: LOAD // SUB, part * 4 + at].reshape(LOAD, SIDE)
            parts.append(center(ring[pl.ds(row, WINDOW), :], ring[pl.ds(row + 1, WINDOW), :], lane, widths_ref[line]))
        lines.append(parts)
    gradient_sums(forward(lines, window_ref[...], right_ref[...], twist_ref), out_ref)


def history_kernel(rows_ref, right_ref, right_t_ref, twist_ref, out_ref):
    lines = [[rows_ref[:, part * 4 + at].reshape(SIDE, SIDE) for part in range(2)] for at in range(4)]
    for at, (real, imag) in enumerate(forward(lines, right_t_ref[...], right_ref[...], twist_ref)):
        out_ref[at, 0] = real
        out_ref[at, 1] = imag


def share_kernel(in_ref, out_ref):
    out_ref[...] = jnp.broadcast_to(jnp.sum(in_ref[...], axis=0)[None], out_ref.shape)


def second_kernel(
    a_ref, shifts_ref, widths_ref, sums_ref, history_ref, window_ref, ring_ref, right_ref, right_t_ref, twist_ref,
    out_ref, total_ref,
):
    total = phase_of(sums_ref)
    total_ref[...] = total
    lines = turn_back([(history_ref[at, 0], history_ref[at, 1]) for at in range(2)], total)
    centered = []
    for at, started in enumerate(inverse_start(lines, right_t_ref[...], twist_ref)):
        line = a_ref[0] * 2 + at
        row, lane = row_offset(shifts_ref[line])
        cosine, sine = ring_ref[0, pl.ds(row, LOAD), :], ring_ref[1, pl.ds(row, LOAD), :]
        left = [jnp.concatenate([cosine, -sine], axis=1), jnp.concatenate([sine, cosine], axis=1)]
        found = multiply(jnp.concatenate(left, axis=0), started)
        centered.append(
            [
                center(found[from_row : from_row + WINDOW], found[from_row + 1 : from_row + 1 + WINDOW], lane, widths_ref[line])
                for from_row in (0, LOAD)
            ]
        )
    gradient_sums(forward(centered, window_ref[...], right_ref[...], twist_ref), out_ref)


def final_kernel(
    a_ref, sums_ref, total_ref, history_ref, right_ref, right_t_ref, twist_ref, out_ref, phase_ref, turned_ref
):
    total = total_ref[...] + phase_of(sums_ref)
    lines = turn_back([(history_ref[at, 0], history_ref[at, 1]) for at in range(4)], total)
    found = multiply(right_ref[...], jnp.concatenate(inverse_start(lines, right_t_ref[...], twist_ref), axis=1))
    for at in range(4):
        for part in range(2):
            line = found[part * SIDE : (part + 1) * SIDE, at * SIDE : (at + 1) * SIDE]
            out_ref[:, part * 4 + at] = line.reshape(TILES, SUB, SIDE)
    turned_ref[...] = total.T
    phase_ref[...] = turned_ref[pl.ds(pl.multiple_of(a_ref[0] * SUB, SUB), SUB), :]


SMEM = pl.BlockSpec(memory_space=pltpu.SMEM)
VMEM = pl.BlockSpec(memory_space=pltpu.VMEM)
HBM = pl.BlockSpec(memory_space=pltpu.HBM)


def call(kernel, shapes, specs, *operands, scratch=(), out_specs=None):
    out = pl.pallas_call(
        kernel,
        out_shape=[jax.ShapeDtypeStruct(*shape) for shape in shapes],
        in_specs=list(specs),
        out_specs=out_specs or [VMEM] * len(shapes),
        scratch_shapes=list(scratch),
        compiler_params=pltpu.CompilerParams(vmem_limit_bytes=32 * 1024 * 1024),
    )(*operands)
    return out if len(out) > 1 else out[0]


def exchange(array, axes):
    return lax.all_to_all(array, axes, split_axis=0, concat_axis=0, tiled=True)


RNG = ("zh", "zl", "x")
AZ = ("yh", "yl", "core")
NEAR = ("zl", "x", "yl", "core")
FAR = ("zh", "yh")


def local(sar_image, strong_index, shifts, widths):
    f32, i32 = jnp.float32, jnp.int32
    az, near, far = lax.axis_size(AZ), lax.axis_size(NEAR), lax.axis_size(FAR)
    bins, pulses_local = sar_image.shape[1:]
    table = tables()
    a_index = lax.axis_index(AZ).astype(i32).reshape(1)
    tile = (SUB, SIDE)
    moved_tiles = pltpu.VMEM((2 * bins * SUB, SIDE), f32)

    packed, place = call(
        pack_kernel,
        [((az * 8,) + tile, f32), ((bins,), i32)],
        [HBM, HBM],
        strong_index,
        sar_image,
        scratch=[
            pltpu.SMEM(strong_index.shape, i32),
            pltpu.VMEM(sar_image.shape, f32),
            moved_tiles,
            pltpu.SemaphoreType.DMA,
            pltpu.SemaphoreType.DMA((2,)),
        ],
        out_specs=[VMEM, SMEM],
    )
    rows = exchange(packed.reshape((az, 8) + tile), AZ)
    sums = call(
        first_kernel,
        [((2 * TILES,) + tile, f32)],
        [SMEM] * 3 + [VMEM] * 4,
        a_index,
        shifts,
        widths,
        rows,
        table["window"],
        table["right"],
        table["twist"],
        scratch=[pltpu.VMEM((4, SIDE + LOAD, SIDE), f32)],
    )
    history = call(
        history_kernel,
        [((4, 2, SIDE, SIDE), f32)],
        [VMEM] * 4,
        rows,
        table["right"],
        table["right_t"],
        table["twist"],
    )

    def all_sums(sums):
        each = 2 * TILES // near
        scattered = exchange(sums.reshape((near, each) + tile), NEAR)
        partial = call(share_kernel, [((far, each) + tile, f32)], [VMEM], scattered)
        everyone = exchange(partial, FAR)
        whole = call(share_kernel, [((near, each) + tile, f32)], [VMEM], everyone)
        return exchange(whole, NEAR).reshape((2 * TILES,) + tile)

    summed = all_sums(sums)
    sums, total = call(
        second_kernel,
        [((2 * TILES,) + tile, f32), ((SIDE, SIDE), f32)],
        [SMEM] * 3 + [VMEM] * 7,
        a_index,
        shifts,
        widths,
        summed,
        history,
        table["window"],
        table["ring"],
        table["right"],
        table["right_t"],
        table["twist"],
    )
    summed = all_sums(sums)
    corrected, phase = call(
        final_kernel,
        [((az, 8) + tile, f32), (tile, f32)],
        [SMEM] + [VMEM] * 6,
        a_index,
        summed,
        total,
        history,
        table["right"],
        table["right_t"],
        table["twist"],
        scratch=[pltpu.VMEM((SIDE, SIDE), f32)],
    )
    returned = exchange(corrected, AZ)
    focused = call(
        unpack_kernel,
        [(sar_image.shape, f32)],
        [SMEM, VMEM],
        place,
        returned.reshape((az * 8,) + tile),
        scratch=[pltpu.VMEM(sar_image.shape, f32), moved_tiles, pltpu.SemaphoreType.DMA((4,))],
        out_specs=[HBM],
    )
    return focused, phase.reshape(pulses_local)


def solution(mesh):
    rng, az = mesh.devices.shape
    along_x = max(1, min(4, rng // 2))
    split = Mesh(
        mesh.devices.reshape(rng // (2 * along_x), 2, along_x, az // 4, 2, 2), RNG + AZ
    )
    placed = (P(None, RNG, AZ), P(RNG), P(RNG), P(RNG))
    return jax.shard_map(
        local,
        mesh=split,
        in_specs=placed,
        out_specs=(P(None, RNG, AZ), P(AZ)),
        check_vma=False,
    )
```

time: 152 us -> 144 us (0.947)
  blocking collectives: 94.3 us -> 89.4 us
  Pallas kernels: 15.4 us -> 12.6 us
    all_to_all x6, blocking collectives: 94.3 us -> 89.4 us  [exchange(): return lax.all_to_all(array, axes, split_axis=0, concat_axis=0, tiled=True)]
    pallas_call x10, Pallas kernels: 15.4 us -> 12.6 us  [call(): pl.pallas_call(kernel, out_shape=[jax.ShapeDtypeStruct(*shape) for shape...]
where the time goes in v2:
time: 144 us; the launch traced here: 143 us
  blocking collectives  89.4 us (62%)
  waiting for transfers between devices  23.2 us (16%)
  starting transfers between devices  15.7 us (11%)
  Pallas kernels  12.6 us (9%)
  local copies, waits for them, and re-layouts  1.73 us (1%)
    all_to_all x6, blocking collectives, exchange(): return lax.all_to_all(array, axes, split_axis=0, concat_axis=0, tiled=True)  89.4 us
    all_to_all x2, waiting for transfers between devices, exchange(): return lax.all_to_all(array, axes, split_axis=0, concat_axis=0, tiled=True)  23.2 us
    all_to_all x2, starting transfers between devices, exchange(): return lax.all_to_all(array, axes, split_axis=0, concat_axis=0, tiled=True)  15.7 us
    pallas_call x10, Pallas kernels, call(): pl.pallas_call(kernel, out_shape=[jax.ShapeDtypeStruct(*shape) for shape...  12.6 us
  transfers between devices with their start and end apart: 2, of which 2 were waited for; matrix products, arithmetic and copies ran while one was open for 0% of the time, Pallas kernels for 1%

profile of v2, /device:TPU:1, one launch (start us, length us, event | category | flops | bytes accessed | tf_op | source)
XLA Modules:
  0.0 143.4 jit_solution(9497975159414444108)
XLA Ops:
  0.6 0.0 copy-start.4
  0.6 1.0 copy-done.4
  1.7 0.0 copy-start.8
  1.7 0.7 copy-done.8
  2.3 2.0 %shard_map.104 = (f32[128,8,128]{2,1,0:T(8,128)}, s32[64]{0:T(128)S(1)}) custom-call(s32[32]{0:T(128)S(1)} %copy-done.8, f32[2,64,1024]{2,1,0:T(8,128)S(1)} %copy-done.4), custom_call_target="tpu_custom_call" | custom-call | tf_op jit(solution)/shard_map/pallas_call | solution.py:265
  4.3 0.0 copy-start
  4.3 0.0 copy-start.2
  4.4 0.0 copy-start.3
  4.4 10.4 %all-to-all-start = ((f32[16,8,8,128]{3,2,1,0:T(8,128)}), f32[16,8,8,128]{3,2,1,0:T(8,128)S(1)}, u32[]{:S(2)}, u32[]{:S(2)}) async-start(f32[16,8,8,128]{3,2,1,0:T(8,128)} %bitcast.1), calls=%async_computation | async-start | bytes 1048576 | tf_op jit(solution)/shard_map/all_to_all | solution.py:277
  14.8 0.0 copy-start.6
  14.8 0.0 copy-start.7
  14.8 17.3 %all-to-all-done.rows_ref = f32[16,8,8,128]{3,2,1,0:T(8,128)S(1)} async-done(((f32[16,8,8,128]{3,2,1,0:T(8,128)}), f32[16,8,8,128]{3,2,1,0:T(8,128)S(1)}, u32[]{:S(2)}, u32[]{:S(2)}) %all-to-all-start) | async-done | bytes 524320 | tf_op jit(solution)/shard_map/all_to_all | solution.py:277
  32.1 0.0 copy-done
  32.1 0.0 copy-done.2
  32.1 0.0 copy-done.3
  32.1 0.0 copy-done.6
  32.1 0.0 copy-done.7
  32.1 1.8 %shard_map.105 = f32[32,8,128]{2,1,0:T(8,128)S(1)} custom-call(s32[1]{0:T(128)} %bitcast.a_ref, s32[32]{0:T(128)S(1)} %copy-done.6, s32[32]{0:T(128)S(1)} %copy-done.7, f32[16,8,8,128]{3,2,1,0:T(8,128)S(1)} %all-to-all-done.rows_ref, f32[256,32]{1,0:T(8,128)S(1)} %copy-done.3, f32[256,256]{1,0:T(8,128)S(1)} %copy-done, f32[2,128,128]{2,1,0:T(8,128)S(1)} %copy-done.2), custom_call_target="tpu_custom_call" | custom-call | tf_op jit(solution)/shard_map/pallas_call | solution.py:265
  33.9 11.4 %all_to_all.40.in_ref = f32[32,1,8,128]{3,2,1,0:T(8,128)S(1)} all-to-all(f32[32,1,8,128]{3,2,1,0:T(8,128)S(1)} %bitcast.11), channel_id=1, replica_groups=mesh['zh'=4,'zl'=2,'x'=4,'yh'=4,'yl'=2,'core'=2] {'zl','x','yl','core'}, dimensions={0} | all-to-all | bytes 262144 | tf_op jit(solution)/shard_map/all_to_all | solution.py:277
  45.4 0.0 copy-start.1
  45.4 22.3 %all_to_all.41.in_ref = f32[16,1,8,128]{3,2,1,0:T(8,128)S(1)} all-to-all(f32[16,1,8,128]{3,2,1,0:T(8,128)S(1)} %shard_map.106), channel_id=1, replica_groups=mesh['zh'=4,'zl'=2,'x'=4,'yh'=4,'yl'=2,'core'=2] {'zh','yh'}, dimensions={0} | all-to-all | bytes 131072 | tf_op jit(solution)/shard_map/all_to_all | solution.py:277
  67.7 0.7 shard_map.107
  68.4 5.3 %all-to-all-start.3 = ((f32[32,1,8,128]{3,2,1,0:T(8,128)}), f32[32,1,8,128]{3,2,1,0:T(8,128)S(1)}, u32[]{:S(2)}, u32[]{:S(2)}) async-start(f32[32,1,8,128]{3,2,1,0:T(8,128)} %shard_map.107), calls=%async_computation.3 | async-start | bytes 262144 | tf_op jit(solution)/shard_map/all_to_all | solution.py:277
  73.7 0.0 copy-done.1
  73.7 0.0 copy-start.5
  73.8 1.2 shard_map.108.history_ref
  74.9 5.8 %all-to-all-done.3 = f32[32,1,8,128]{3,2,1,0:T(8,128)S(1)} async-done(((f32[32,1,8,128]{3,2,1,0:T(8,128)}), f32[32,1,8,128]{3,2,1,0:T(8,128)S(1)}, u32[]{:S(2)}, u32[]{:S(2)}) %all-to-all-start.3) | async-done | bytes 131104 | tf_op jit(solution)/shard_map/all_to_all | solution.py:277
  80.8 0.0 copy-done.5
  80.8 2.8 %shard_map.109 = (f32[32,8,128]{2,1,0:T(8,128)S(1)}, f32[128,128]{1,0:T(8,128)S(1)}) custom-call(s32[1]{0:T(128)} %bitcast.a_ref, s32[32]{0:T(128)S(1)} %copy-done.6, s32[32]{0:T(128)S(1)} %copy-done.7, f32[32,8,128]{2,1,0:T(8,128)S(1)} %bitcast.9, f32[4,2,128,128]{3,2,1,0:T(8,128)S(1)} %shard_map.108.history_ref, f32[256,32]{1,0:T(8,128)S(1)} %copy-done.3, ...), custom_call_target="tpu_custom_call" | custom-call | tf_op jit(solution)/shard_map/pallas_call | solution.py:265
  83.5 10.3 %all_to_all.42.in_ref = f32[32,1,8,128]{3,2,1,0:T(8,128)S(1)} all-to-all(f32[32,1,8,128]{3,2,1,0:T(8,128)S(1)} %bitcast.12), channel_id=1, replica_groups=mesh['zh'=4,'zl'=2,'x'=4,'yh'=4,'yl'=2,'core'=2] {'zl','x','yl','core'}, dimensions={0} | all-to-all | bytes 262144 | tf_op jit(solution)/shard_map/all_to_all | solution.py:277
  93.8 13.8 %all_to_all.43.in_ref = f32[16,1,8,128]{3,2,1,0:T(8,128)S(1)} all-to-all(f32[16,1,8,128]{3,2,1,0:T(8,128)S(1)} %shard_map.110), channel_id=1, replica_groups=mesh['zh'=4,'zl'=2,'x'=4,'yh'=4,'yl'=2,'core'=2] {'zh','yh'}, dimensions={0} | all-to-all | bytes 131072 | tf_op jit(solution)/shard_map/all_to_all | solution.py:277
  107.7 11.4 %all_to_all.44 = f32[32,1,8,128]{3,2,1,0:T(8,128)S(1)} all-to-all(f32[32,1,8,128]{3,2,1,0:T(8,128)S(1)} %shard_map.111), channel_id=1, replica_groups=mesh['zh'=4,'zl'=2,'x'=4,'yh'=4,'yl'=2,'core'=2] {'zl','x','yl','core'}, dimensions={0} | all-to-all | bytes 262144 | tf_op jit(solution)/shard_map/all_to_all | solution.py:277
  119.1 2.7 %shard_map.112 = (f32[16,8,8,128]{3,2,1,0:T(8,128)S(1)}, f32[8,128]{1,0:T(8,128)}) custom-call(s32[1]{0:T(128)} %bitcast.a_ref, f32[32,8,128]{2,1,0:T(8,128)S(1)} %bitcast.10, f32[128,128]{1,0:T(8,128)S(1)} %get-tuple-element.11.total_ref, f32[4,2,128,128]{3,2,1,0:T(8,128)S(1)} %shard_map.108.history_ref, f32[256,256]{1,0:T(8,128)S(1)} %copy-done, ...), custom_call_target="tpu_custom_call" | custom-call | tf_op jit(solution)/shard_map/pallas_call | solution.py:265
  121.8 20.2 %all_to_all.45 = f32[16,8,8,128]{3,2,1,0:T(8,128)S(1)} all-to-all(f32[16,8,8,128]{3,2,1,0:T(8,128)S(1)} %get-tuple-element.12), channel_id=1, replica_groups=mesh['zh'=4,'zl'=2,'x'=4,'yh'=4,'yl'=2,'core'=2] {'yh','yl','core'}, dimensions={0} | all-to-all | bytes 1048576 | tf_op jit(solution)/shard_map/all_to_all | solution.py:277
  142.0 1.4 %shard_map.113 = f32[2,64,1024]{2,1,0:T(8,128)} custom-call(s32[64]{0:T(128)S(1)} %get-tuple-element.8.place_ref, f32[128,8,128]{2,1,0:T(8,128)S(1)} %bitcast.8), custom_call_target="tpu_custom_call" | custom-call | tf_op jit(solution)/shard_map/pallas_call | solution.py:265
  (3 shorter events, 0.1 us)
Async XLA Ops:
  0.6 1.0 copy-start.4
  1.7 0.7 copy-start.8
  4.3 27.8 %copy-start = (f32[256,256]{1,0:T(8,128)S(1)}, f32[256,256]{1,0:T(8,128)}, u32[]{:S(2)}) copy-start(f32[256,256]{1,0:T(8,128)} %constant.25.clone.right_ref) | copy-start | bytes 786436
  4.3 27.8 %copy-start.2 = (f32[2,128,128]{2,1,0:T(8,128)S(1)}, f32[2,128,128]{2,1,0:T(8,128)}, u32[]{:S(2)}) copy-start(f32[2,128,128]{2,1,0:T(8,128)} %constant.29.clone.twist_ref) | copy-start | bytes 393220
  4.4 27.8 %copy-start.3 = (f32[256,32]{1,0:T(8,128)S(1)}, f32[256,32]{1,0:T(8,128)}, u32[]{:S(2)}) copy-start(f32[256,32]{1,0:T(8,128)} %constant.27.clone.window_ref) | copy-start | bytes 98308
  4.4 27.7 %all-to-all-start = ((f32[16,8,8,128]{3,2,1,0:T(8,128)}), f32[16,8,8,128]{3,2,1,0:T(8,128)S(1)}, u32[]{:S(2)}, u32[]{:S(2)}) async-start(f32[16,8,8,128]{3,2,1,0:T(8,128)} %bitcast.1), calls=%async_computation | async-start | bytes 1048576 | tf_op jit(solution)/shard_map/all_to_all | solution.py:277
  14.8 17.4 %copy-start.6 = (s32[32]{0:T(128)S(1)}, s32[32]{0:T(128)}, u32[]{:S(2)}) copy-start(s32[32]{0:T(128)} %shifts_ref.3) | copy-start | bytes 388
  14.8 17.4 %copy-start.7 = (s32[32]{0:T(128)S(1)}, s32[32]{0:T(128)}, u32[]{:S(2)}) copy-start(s32[32]{0:T(128)} %widths_ref.3) | copy-start | bytes 388
  45.4 28.4 %copy-start.1 = (f32[256,256]{1,0:T(8,128)S(1)}, f32[256,256]{1,0:T(8,128)}, u32[]{:S(2)}) copy-start(f32[256,256]{1,0:T(8,128)} %constant.26.clone.right_t_ref) | copy-start | bytes 786436
  68.4 12.4 %all-to-all-start.3 = ((f32[32,1,8,128]{3,2,1,0:T(8,128)}), f32[32,1,8,128]{3,2,1,0:T(8,128)S(1)}, u32[]{:S(2)}, u32[]{:S(2)}) async-start(f32[32,1,8,128]{3,2,1,0:T(8,128)} %shard_map.107), calls=%async_computation.3 | async-start | bytes 262144 | tf_op jit(solution)/shard_map/all_to_all | solution.py:277
  73.7 7.0 %copy-start.5 = (f32[2,152,128]{2,1,0:T(8,128)S(1)}, f32[2,152,128]{2,1,0:T(8,128)}, u32[]{:S(2)}) copy-start(f32[2,152,128]{2,1,0:T(8,128)} %constant.28.clone.ring_ref) | copy-start | bytes 466948

commit v3 on v2

--- a/solution.py
+++ b/solution.py
@@ -139,14 +139,23 @@
     return (part * (bins // SUB) + row // SUB) * SUB * SUB + row % SUB
 
 
-def pack_kernel(strong_hbm, image_hbm, out_ref, place_ref, strong_ref, image_ref, tiles_ref, small_sem, sems):
+def pack_kernel(
+    strong_hbm, shifts_hbm, widths_hbm, image_hbm, out_hbm, at_ref,
+    place_ref, strong_ref, shifts_ref, widths_ref, image_ref, tiles_ref, out_ref, small_sems, sems, out_sems,
+):
     bins = image_ref.shape[1]
     strong = strong_ref.shape[0]
-    indices = pltpu.make_async_copy(strong_hbm, strong_ref, small_sem)
+    indices = pltpu.make_async_copy(strong_hbm, strong_ref, small_sems.at[0])
     indices.start()
     parts = [pltpu.make_async_copy(image_hbm.at[part], image_ref.at[part], sems.at[part]) for part in range(2)]
     for part in parts:
         part.start()
+    others_in = [
+        pltpu.make_async_copy(shifts_hbm, shifts_ref, small_sems.at[1]),
+        pltpu.make_async_copy(widths_hbm, widths_ref, small_sems.at[2]),
+    ]
+    for copy in others_in:
+        copy.start()
     for row in range(bins):
         place_ref[row] = -1
     indices.wait()
@@ -155,8 +164,17 @@
     others = jnp.int32(0)
     for row in range(bins):
         held = place_ref[row]
-        place_ref[row] = jnp.where(held < 0, others // 2 * 8 + others % 2 + 2, held)
+        place = jnp.where(held < 0, others // 2 * 8 + others % 2 + 2, held)
+        place_ref[row] = place
+        at_ref[SUB + row : SUB + row + 1, :] = jnp.full((1, SIDE), place, jnp.int32)
         others = others + jnp.where(held < 0, 1, 0)
+    for copy in others_in:
+        copy.wait()
+    for at in range(2):
+        line = lax.axis_index(AZ) * 2 + at
+        for where, value in enumerate(row_offset(shifts_ref[line]) + (widths_ref[line],)):
+            at_ref[4 * at + where : 4 * at + where + 1, :] = jnp.full((1, SIDE), value, jnp.int32)
+    copies = []
     for part in range(2):
         parts[part].wait()
         for group in range(bins // SUB):
@@ -166,15 +184,25 @@
                     part, group * SUB : (group + 1) * SUB, block * SIDE : (block + 1) * SIDE
                 ]
         for row in range(bins):
-            out_ref[place_ref[row] + part * 4] = tiles_ref[pl.ds(tile_at(bins, part, row), SUB, stride=SUB), :]
-
-
-def unpack_kernel(place_ref, rows_ref, image_hbm, image_ref, tiles_ref, sems):
+            out_ref[part, place_ref[row] // 8, place_ref[row] % 8] = tiles_ref[
+                pl.ds(tile_at(bins, part, row), SUB, stride=SUB), :
+            ]
+        copies.append(
+            pltpu.make_async_copy(out_ref.at[part], out_hbm.at[:, pl.ds(part * 4, 4)], out_sems.at[part])
+        )
+        copies[-1].start()
+    for copy in copies:
+        copy.wait()
+
+
+def unpack_kernel(at_ref, rows_ref, phase_ref, image_hbm, phase_hbm, image_ref, tiles_ref, sems):
     bins = image_ref.shape[1]
-    copies = []
+    copies = [pltpu.make_async_copy(phase_ref, phase_hbm, sems.at[4])]
+    copies[0].start()
+    places = [at_ref[SUB + row, 0] for row in range(bins)]
     for part in range(2):
         for row in range(bins):
-            tiles_ref[pl.ds(tile_at(bins, part, row), SUB, stride=SUB), :] = rows_ref[place_ref[row] + part * 4]
+            tiles_ref[pl.ds(tile_at(bins, part, row), SUB, stride=SUB), :] = rows_ref[places[row] + part * 4]
         for half in range(2):
             span = slice(half * bins // 2, (half + 1) * bins // 2)
             for group in range(half * bins // 2 // SUB, (half + 1) * bins // 2 // SUB):
@@ -193,17 +221,20 @@
         copy.wait()
 
 
-def first_kernel(a_ref, shifts_ref, widths_ref, rows_ref, window_ref, right_ref, twist_ref, out_ref, ring_ref):
+def offsets(at_ref, line):
+    return [at_ref[4 * line + where, 0] for where in range(3)]
+
+
+def first_kernel(at_ref, rows_ref, window_ref, right_ref, twist_ref, out_ref, ring_ref):
     lines = []
     for at in range(2):
-        line = a_ref[0] * 2 + at
-        row, lane = row_offset(shifts_ref[line])
+        row, lane, width = offsets(at_ref, at)
         parts = []
         for part in range(2):
             ring = ring_ref.at[at * 2 + part]
             ring[:SIDE, :] = rows_ref[:, part * 4 + at].reshape(SIDE, SIDE)
             ring[SIDE:, :] = rows_ref[: LOAD // SUB, part * 4 + at].reshape(LOAD, SIDE)
-            parts.append(center(ring[pl.ds(row, WINDOW), :], ring[pl.ds(row + 1, WINDOW), :], lane, widths_ref[line]))
+            parts.append(center(ring[pl.ds(row, WINDOW), :], ring[pl.ds(row + 1, WINDOW), :], lane, width))
         lines.append(parts)
     gradient_sums(forward(lines, window_ref[...], right_ref[...], twist_ref), out_ref)
 
@@ -220,7 +251,7 @@
 
 
 def second_kernel(
-    a_ref, shifts_ref, widths_ref, sums_ref, history_ref, window_ref, ring_ref, right_ref, right_t_ref, twist_ref,
+    at_ref, sums_ref, history_ref, window_ref, ring_ref, right_ref, right_t_ref, twist_ref,
     out_ref, total_ref,
 ):
     total = phase_of(sums_ref)
@@ -228,14 +259,13 @@
     lines = turn_back([(history_ref[at, 0], history_ref[at, 1]) for at in range(2)], total)
     centered = []
     for at, started in enumerate(inverse_start(lines, right_t_ref[...], twist_ref)):
-        line = a_ref[0] * 2 + at
-        row, lane = row_offset(shifts_ref[line])
+        row, lane, width = offsets(at_ref, at)
         cosine, sine = ring_ref[0, pl.ds(row, LOAD), :], ring_ref[1, pl.ds(row, LOAD), :]
         left = [jnp.concatenate([cosine, -sine], axis=1), jnp.concatenate([sine, cosine], axis=1)]
         found = multiply(jnp.concatenate(left, axis=0), started)
         centered.append(
             [
-                center(found[from_row : from_row + WINDOW], found[from_row + 1 : from_row + 1 + WINDOW], lane, widths_ref[line])
+                center(found[from_row : from_row + WINDOW], found[from_row + 1 : from_row + 1 + WINDOW], lane, width)
                 for from_row in (0, LOAD)
             ]
         )
@@ -243,7 +273,7 @@
 
 
 def final_kernel(
-    a_ref, sums_ref, total_ref, history_ref, right_ref, right_t_ref, twist_ref, out_ref, phase_ref, turned_ref
+    sums_ref, total_ref, history_ref, right_ref, right_t_ref, twist_ref, out_ref, phase_ref, turned_ref
 ):
     total = total_ref[...] + phase_of(sums_ref)
     lines = turn_back([(history_ref[at, 0], history_ref[at, 1]) for at in range(4)], total)
@@ -253,22 +283,23 @@
             line = found[part * SIDE : (part + 1) * SIDE, at * SIDE : (at + 1) * SIDE]
             out_ref[:, part * 4 + at] = line.reshape(TILES, SUB, SIDE)
     turned_ref[...] = total.T
-    phase_ref[...] = turned_ref[pl.ds(pl.multiple_of(a_ref[0] * SUB, SUB), SUB), :]
+    phase_ref[...] = turned_ref[pl.ds(pl.multiple_of(lax.axis_index(AZ) * SUB, SUB), SUB), :]
 
 
 SMEM = pl.BlockSpec(memory_space=pltpu.SMEM)
 VMEM = pl.BlockSpec(memory_space=pltpu.VMEM)
 HBM = pl.BlockSpec(memory_space=pltpu.HBM)
-
-
-def call(kernel, shapes, specs, *operands, scratch=(), out_specs=None):
+PACK_VMEM = 60 * 1024 * 1024
+
+
+def call(kernel, shapes, specs, *operands, scratch=(), out_specs=None, vmem=32 * 1024 * 1024):
     out = pl.pallas_call(
         kernel,
         out_shape=[jax.ShapeDtypeStruct(*shape) for shape in shapes],
         in_specs=list(specs),
         out_specs=out_specs or [VMEM] * len(shapes),
         scratch_shapes=list(scratch),
-        compiler_params=pltpu.CompilerParams(vmem_limit_bytes=32 * 1024 * 1024),
+        compiler_params=pltpu.CompilerParams(vmem_limit_bytes=vmem),
     )(*operands)
     return out if len(out) > 1 else out[0]
 
@@ -288,33 +319,36 @@
     az, near, far = lax.axis_size(AZ), lax.axis_size(NEAR), lax.axis_size(FAR)
     bins, pulses_local = sar_image.shape[1:]
     table = tables()
-    a_index = lax.axis_index(AZ).astype(i32).reshape(1)
     tile = (SUB, SIDE)
     moved_tiles = pltpu.VMEM((2 * bins * SUB, SIDE), f32)
 
-    packed, place = call(
+    packed, places = call(
         pack_kernel,
-        [((az * 8,) + tile, f32), ((bins,), i32)],
-        [HBM, HBM],
+        [((az, 8) + tile, f32), ((SUB + bins, SIDE), i32)],
+        [HBM] * 4,
         strong_index,
+        shifts,
+        widths,
         sar_image,
-        scratch=[
-            pltpu.SMEM(strong_index.shape, i32),
+        scratch=[pltpu.SMEM((bins,), i32)]
+        + [pltpu.SMEM(strong_index.shape, i32) for _ in range(3)]
+        + [
             pltpu.VMEM(sar_image.shape, f32),
             moved_tiles,
-            pltpu.SemaphoreType.DMA,
+            pltpu.VMEM((2, az, 4) + tile, f32),
+            pltpu.SemaphoreType.DMA((3,)),
+            pltpu.SemaphoreType.DMA((2,)),
             pltpu.SemaphoreType.DMA((2,)),
         ],
-        out_specs=[VMEM, SMEM],
-    )
-    rows = exchange(packed.reshape((az, 8) + tile), AZ)
+        out_specs=[HBM, VMEM],
+        vmem=PACK_VMEM,
+    )
+    rows = exchange(packed, AZ)
     sums = call(
         first_kernel,
         [((2 * TILES,) + tile, f32)],
-        [SMEM] * 3 + [VMEM] * 4,
-        a_index,
-        shifts,
-        widths,
+        [VMEM] * 5,
+        places,
         rows,
         table["window"],
         table["right"],
@@ -343,10 +377,8 @@
     sums, total = call(
         second_kernel,
         [((2 * TILES,) + tile, f32), ((SIDE, SIDE), f32)],
-        [SMEM] * 3 + [VMEM] * 7,
-        a_index,
-        shifts,
-        widths,
+        [VMEM] * 8,
+        places,
         summed,
         history,
         table["window"],
@@ -359,8 +391,7 @@
     corrected, phase = call(
         final_kernel,
         [((az, 8) + tile, f32), (tile, f32)],
-        [SMEM] + [VMEM] * 6,
-        a_index,
+        [VMEM] * 6,
         summed,
         total,
         history,
@@ -370,14 +401,15 @@
         scratch=[pltpu.VMEM((SIDE, SIDE), f32)],
     )
     returned = exchange(corrected, AZ)
-    focused = call(
+    focused, phase = call(
         unpack_kernel,
-        [(sar_image.shape, f32)],
-        [SMEM, VMEM],
-        place,
+        [(sar_image.shape, f32), (tile, f32)],
+        [VMEM, VMEM, VMEM],
+        places,
         returned.reshape((az * 8,) + tile),
-        scratch=[pltpu.VMEM(sar_image.shape, f32), moved_tiles, pltpu.SemaphoreType.DMA((4,))],
-        out_specs=[HBM],
+        phase,
+        scratch=[pltpu.VMEM(sar_image.shape, f32), moved_tiles, pltpu.SemaphoreType.DMA((5,))],
+        out_specs=[HBM, HBM],
     )
     return focused, phase.reshape(pulses_local)
 

time: 144 us -> 142 us (0.986)
  blocking collectives: 89.4 us -> 117 us
  waiting for transfers between devices: 23.2 us -> 5.84 us
  starting transfers between devices: 15.7 us -> 5.33 us
  local copies, waits for them, and re-layouts: 1.73 us -> 0.04 us
    all_to_all x6 -> x7, blocking collectives: 89.4 us -> 117 us  [exchange(): return lax.all_to_all(array, axes, split_axis=0, concat_axis=0, tiled=True)]
    all_to_all x2 -> x1, waiting for transfers between devices: 23.2 us -> 5.84 us  [exchange(): return lax.all_to_all(array, axes, split_axis=0, concat_axis=0, tiled=True)]
    all_to_all x2 -> x1, starting transfers between devices: 15.7 us -> 5.33 us  [exchange(): return lax.all_to_all(array, axes, split_axis=0, concat_axis=0, tiled=True)]
    unnamed x18 -> x12, local copies, waits for them, and re-layouts: 1.73 us -> 0.04 us
  transfers between devices with their start and end apart: 2 -> 1, of which waited for: 2 -> 1; matrix products, arithmetic and copies ran while one was open for 0% -> 0% of each run, Pallas kernels for 1% -> 1%
where the time goes in v3:
time: 142 us; the launch traced here: 141 us
  blocking collectives  117 us (82%)
  Pallas kernels  12 us (8%)
  waiting for transfers between devices  5.84 us (4%)
  starting transfers between devices  5.33 us (4%)
    all_to_all x7, blocking collectives, exchange(): return lax.all_to_all(array, axes, split_axis=0, concat_axis=0, tiled=True)  117 us
    pallas_call x10, Pallas kernels, call(): pl.pallas_call(kernel, out_shape=[jax.ShapeDtypeStruct(*shape) for shape...  12 us
    all_to_all x1, waiting for transfers between devices, exchange(): return lax.all_to_all(array, axes, split_axis=0, concat_axis=0, tiled=True)  5.84 us
    all_to_all x1, starting transfers between devices, exchange(): return lax.all_to_all(array, axes, split_axis=0, concat_axis=0, tiled=True)  5.33 us
  transfers between devices with their start and end apart: 1, of which 1 were waited for; matrix products, arithmetic and copies ran while one was open for 0% of the time, Pallas kernels for 1%

profile of v3, /device:TPU:1, one launch (start us, length us, event | category | flops | bytes accessed | tf_op | source)
XLA Modules:
  0.0 141.1 jit_solution(11479304046738625227)
XLA Ops:
  0.6 3.4 %shard_map.104 = (f32[16,8,8,128]{3,2,1,0:T(8,128)}, s32[72,128]{1,0:T(8,128)}) custom-call(s32[32]{0:T(128)} %strong_hbm.1, s32[32]{0:T(128)} %shifts_hbm.1, s32[32]{0:T(128)} %widths_hbm.1, f32[2,64,1024]{2,1,0:T(8,128)} %image_hbm.1), custom_call_target="tpu_custom_call" | custom-call | tf_op jit(solution)/shard_map/pallas_call | solution.py:296
  4.0 0.0 copy-start
  4.0 0.0 copy-start.2
  4.0 0.0 copy-start.3
  4.0 0.0 copy-start.4
  4.0 27.7 %all_to_all.40.rows_ref = f32[16,8,8,128]{3,2,1,0:T(8,128)S(1)} all-to-all(f32[16,8,8,128]{3,2,1,0:T(8,128)} %get-tuple-element.11), channel_id=1, replica_groups=mesh['zh'=4,'zl'=2,'x'=4,'yh'=4,'yl'=2,'core'=2] {'yh','yl','core'}, dimensions={0} | all-to-all | bytes 1048576 | tf_op jit(solution)/shard_map/all_to_all | solution.py:308
  31.8 0.0 copy-done
  31.8 0.0 copy-done.2
  31.8 0.0 copy-done.3
  31.8 0.0 copy-done.4
  31.8 1.2 shard_map.105
  33.0 11.5 %all_to_all.41.in_ref = f32[32,1,8,128]{3,2,1,0:T(8,128)S(1)} all-to-all(f32[32,1,8,128]{3,2,1,0:T(8,128)S(1)} %bitcast.8), channel_id=1, replica_groups=mesh['zh'=4,'zl'=2,'x'=4,'yh'=4,'yl'=2,'core'=2] {'zl','x','yl','core'}, dimensions={0} | all-to-all | bytes 262144 | tf_op jit(solution)/shard_map/all_to_all | solution.py:308
  44.5 0.0 copy-start.1
  44.5 22.3 %all_to_all.42.in_ref = f32[16,1,8,128]{3,2,1,0:T(8,128)S(1)} all-to-all(f32[16,1,8,128]{3,2,1,0:T(8,128)S(1)} %shard_map.106), channel_id=1, replica_groups=mesh['zh'=4,'zl'=2,'x'=4,'yh'=4,'yl'=2,'core'=2] {'zh','yh'}, dimensions={0} | all-to-all | bytes 131072 | tf_op jit(solution)/shard_map/all_to_all | solution.py:308
  66.8 0.7 shard_map.107
  67.5 5.3 %all-to-all-start.3 = ((f32[32,1,8,128]{3,2,1,0:T(8,128)}), f32[32,1,8,128]{3,2,1,0:T(8,128)S(1)}, u32[]{:S(2)}, u32[]{:S(2)}) async-start(f32[32,1,8,128]{3,2,1,0:T(8,128)} %shard_map.107), calls=%async_computation.3 | async-start | bytes 262144 | tf_op jit(solution)/shard_map/all_to_all | solution.py:308
  72.9 0.0 copy-done.1
  72.9 0.0 copy-start.5
  72.9 1.2 shard_map.108.history_ref
  74.1 5.8 %all-to-all-done.3 = f32[32,1,8,128]{3,2,1,0:T(8,128)S(1)} async-done(((f32[32,1,8,128]{3,2,1,0:T(8,128)}), f32[32,1,8,128]{3,2,1,0:T(8,128)S(1)}, u32[]{:S(2)}, u32[]{:S(2)}) %all-to-all-start.3) | async-done | bytes 131104 | tf_op jit(solution)/shard_map/all_to_all | solution.py:308
  79.9 0.0 copy-done.5
  79.9 2.2 %shard_map.109 = (f32[32,8,128]{2,1,0:T(8,128)S(1)}, f32[128,128]{1,0:T(8,128)S(1)}) custom-call(s32[72,128]{1,0:T(8,128)S(1)} %copy-done.4, f32[32,8,128]{2,1,0:T(8,128)S(1)} %bitcast.7, f32[4,2,128,128]{3,2,1,0:T(8,128)S(1)} %shard_map.108.history_ref, f32[256,32]{1,0:T(8,128)S(1)} %copy-done.3, f32[2,152,128]{2,1,0:T(8,128)S(1)} %copy-done.5, ...), custom_call_target="tpu_custom_call" | custom-call | tf_op jit(solution)/shard_map/pallas_call | solution.py:296
  82.1 10.3 %all_to_all.43.in_ref = f32[32,1,8,128]{3,2,1,0:T(8,128)S(1)} all-to-all(f32[32,1,8,128]{3,2,1,0:T(8,128)S(1)} %bitcast.10), channel_id=1, replica_groups=mesh['zh'=4,'zl'=2,'x'=4,'yh'=4,'yl'=2,'core'=2] {'zl','x','yl','core'}, dimensions={0} | all-to-all | bytes 262144 | tf_op jit(solution)/shard_map/all_to_all | solution.py:308
  92.4 13.8 %all_to_all.44.in_ref = f32[16,1,8,128]{3,2,1,0:T(8,128)S(1)} all-to-all(f32[16,1,8,128]{3,2,1,0:T(8,128)S(1)} %shard_map.110), channel_id=1, replica_groups=mesh['zh'=4,'zl'=2,'x'=4,'yh'=4,'yl'=2,'core'=2] {'zh','yh'}, dimensions={0} | all-to-all | bytes 131072 | tf_op jit(solution)/shard_map/all_to_all | solution.py:308
  106.3 11.4 %all_to_all.45 = f32[32,1,8,128]{3,2,1,0:T(8,128)S(1)} all-to-all(f32[32,1,8,128]{3,2,1,0:T(8,128)S(1)} %shard_map.111), channel_id=1, replica_groups=mesh['zh'=4,'zl'=2,'x'=4,'yh'=4,'yl'=2,'core'=2] {'zl','x','yl','core'}, dimensions={0} | all-to-all | bytes 262144 | tf_op jit(solution)/shard_map/all_to_all | solution.py:308
  117.7 2.2 %shard_map.112 = (f32[16,8,8,128]{3,2,1,0:T(8,128)S(1)}, f32[8,128]{1,0:T(8,128)S(1)}) custom-call(f32[32,8,128]{2,1,0:T(8,128)S(1)} %bitcast.9, f32[128,128]{1,0:T(8,128)S(1)} %get-tuple-element.13.total_ref, f32[4,2,128,128]{3,2,1,0:T(8,128)S(1)} %shard_map.108.history_ref, f32[256,256]{1,0:T(8,128)S(1)} %copy-done, f32[256,256]{1,0:T(8,128)S(1)} %copy-done.1, ...), custom_call_target="tpu_custom_call" | custom-call | tf_op jit(solution)/shard_map/pallas_call | solution.py:296
  120.0 20.2 %all_to_all.46 = f32[16,8,8,128]{3,2,1,0:T(8,128)S(1)} all-to-all(f32[16,8,8,128]{3,2,1,0:T(8,128)S(1)} %get-tuple-element.14), channel_id=1, replica_groups=mesh['zh'=4,'zl'=2,'x'=4,'yh'=4,'yl'=2,'core'=2] {'yh','yl','core'}, dimensions={0} | all-to-all | bytes 1048576 | tf_op jit(solution)/shard_map/all_to_all | solution.py:308
  140.1 1.0 shard_map.113
  (3 shorter events, 0.1 us)
Async XLA Ops:
  4.0 27.8 %copy-start = (f32[256,256]{1,0:T(8,128)S(1)}, f32[256,256]{1,0:T(8,128)}, u32[]{:S(2)}) copy-start(f32[256,256]{1,0:T(8,128)} %constant.10.clone.right_ref) | copy-start | bytes 786436
  4.0 27.8 %copy-start.2 = (f32[2,128,128]{2,1,0:T(8,128)S(1)}, f32[2,128,128]{2,1,0:T(8,128)}, u32[]{:S(2)}) copy-start(f32[2,128,128]{2,1,0:T(8,128)} %constant.14.clone.twist_ref) | copy-start | bytes 393220
  4.0 27.7 %copy-start.3 = (f32[256,32]{1,0:T(8,128)S(1)}, f32[256,32]{1,0:T(8,128)}, u32[]{:S(2)}) copy-start(f32[256,32]{1,0:T(8,128)} %constant.12.clone.window_ref) | copy-start | bytes 98308
  4.0 27.7 %copy-start.4 = (s32[72,128]{1,0:T(8,128)S(1)}, s32[72,128]{1,0:T(8,128)}, u32[]{:S(2)}) copy-start(s32[72,128]{1,0:T(8,128)} %get-tuple-element.10.at_ref) | copy-start | bytes 110596
  44.5 28.3 %copy-start.1 = (f32[256,256]{1,0:T(8,128)S(1)}, f32[256,256]{1,0:T(8,128)}, u32[]{:S(2)}) copy-start(f32[256,256]{1,0:T(8,128)} %constant.11.clone.right_t_ref) | copy-start | bytes 786436
  67.5 12.4 %all-to-all-start.3 = ((f32[32,1,8,128]{3,2,1,0:T(8,128)}), f32[32,1,8,128]{3,2,1,0:T(8,128)S(1)}, u32[]{:S(2)}, u32[]{:S(2)}) async-start(f32[32,1,8,128]{3,2,1,0:T(8,128)} %shard_map.107), calls=%async_computation.3 | async-start | bytes 262144 | tf_op jit(solution)/shard_map/all_to_all | solution.py:308
  72.9 7.0 %copy-start.5 = (f32[2,152,128]{2,1,0:T(8,128)S(1)}, f32[2,152,128]{2,1,0:T(8,128)}, u32[]{:S(2)}) copy-start(f32[2,152,128]{2,1,0:T(8,128)} %constant.13.clone.ring_ref) | copy-start | bytes 466948

commit v4 on v3

--- a/solution.py
+++ b/solution.py
@@ -13,7 +13,6 @@
 WINDOW = 16
 FIRST = SIDE // 2 - WINDOW // 2
 LOAD = 24
-HIGHEST = lax.Precision.HIGHEST
 
 
 def tables():
@@ -28,34 +27,75 @@
     ring = np.stack([cosine[around], sine[around]])
     twist = 2.0 * np.pi * product / (SIDE * SIDE)
     twist = np.stack([np.cos(twist), np.sin(twist)]) / SIDE
-    made = dict(right=right, right_t=right.T, window=window, ring=ring, twist=twist)
-    return {name: jnp.asarray(np.ascontiguousarray(table).astype(np.float32)) for name, table in made.items()}
+    made = dict(ring=ring, twist=twist)
+    made = {name: jnp.asarray(table.astype(np.float32)) for name, table in made.items()}
+    for name, table in dict(right=right, right_t=right.T, window=window).items():
+        parts, rest = [], table.astype(np.float32)
+        for _ in range(3):
+            parts.append(rest.astype(jnp.bfloat16))
+            rest = rest - parts[-1].astype(np.float32)
+        if name == "window":
+            made[name] = jnp.asarray(np.concatenate([parts[at] for at in (0, 0, 1, 0, 1, 2)], axis=1))
+        else:
+            made[name] = jnp.asarray(np.concatenate(parts, axis=0))
+    return made
+
+
+def split(array, count):
+    parts = []
+    for _ in range(count):
+        parts.append(array.astype(jnp.bfloat16))
+        array = array - parts[-1].astype(jnp.float32)
+    return parts
+
+
+def dot(left, right):
+    return jnp.dot(left, right, preferred_element_type=jnp.float32)
+
+
+def stack(array, count=3):
+    return jnp.concatenate(split(array, count), axis=0)
 
 
 def multiply(left, right):
-    return jnp.dot(left, right, precision=HIGHEST, preferred_element_type=jnp.float32)
-
-
-def forward(lines, left, right, twist_ref):
+    count = len(right)
+    rows = left.shape[0] // count
+    by_order = [None] * count
+    for at in range(count):
+        product = dot(left[: (count - at) * rows], right[at])
+        for order in range(count - at):
+            term = product[order * rows : (order + 1) * rows]
+            by_order[at + order] = term if by_order[at + order] is None else by_order[at + order] + term
+    total = by_order[-1]
+    for term in reversed(by_order[:-1]):
+        total = total + term
+    return total
+
+
+def multiply_window(left, right):
+    first, second, third = split(right, 3)
+    return dot(left, jnp.concatenate([first, second, first, third, second, first], axis=0))
+
+
+def forward(lines, first_stage, right_ref, twist_ref):
     cosine, sine = twist_ref[0], twist_ref[1]
-    stacked = jnp.concatenate([jnp.concatenate(line, axis=0) for line in lines], axis=1)
-    first = multiply(left, stacked)
+    first = first_stage(jnp.concatenate([jnp.concatenate(line, axis=0) for line in lines], axis=1))
     turned = []
     for at in range(len(lines)):
         real = first[:SIDE, at * SIDE : (at + 1) * SIDE]
         imag = first[SIDE:, at * SIDE : (at + 1) * SIDE]
         turned.append(jnp.concatenate([real * cosine + imag * sine, imag * cosine - real * sine], axis=1))
-    second = multiply(jnp.concatenate(turned, axis=0), right)
+    second = multiply(stack(jnp.concatenate(turned, axis=0)), parts_of(right_ref))
     return [
         (second[at * SIDE : (at + 1) * SIDE, :SIDE], second[at * SIDE : (at + 1) * SIDE, SIDE:])
         for at in range(len(lines))
     ]
 
 
-def inverse_start(lines, right_t, twist_ref):
+def inverse_start(lines, right_t_ref, twist_ref, count=3):
     cosine, sine = twist_ref[0], twist_ref[1]
     stacked = jnp.concatenate([jnp.concatenate(line, axis=1) for line in lines], axis=0)
-    first = multiply(stacked, right_t)
+    first = multiply(stack(stacked, count), parts_of(right_t_ref, count))
     turned = []
     for at in range(len(lines)):
         real = first[at * SIDE : (at + 1) * SIDE, :SIDE]
@@ -64,6 +104,10 @@
     return turned
 
 
+def parts_of(table_ref, count=3):
+    return [table_ref[at * 2 * SIDE : (at + 1) * 2 * SIDE, :] for at in range(count)]
+
+
 def grid_of(rows):
     return (
         lax.broadcasted_iota(jnp.int32, (rows, SIDE), 0),
@@ -73,10 +117,15 @@
 
 def running_sum(gradient):
     rows, cols = grid_of(SIDE)
-    within = multiply((cols <= rows).astype(jnp.float32), gradient)
-    sums = jnp.broadcast_to(jnp.sum(gradient, axis=0, keepdims=True), (SUB, SIDE))
-    before = multiply(sums, (rows < cols).astype(jnp.float32))
-    return within + before[:1, :]
+    within = dot(
+        (cols <= rows).astype(jnp.float32).astype(jnp.bfloat16), jnp.concatenate(split(gradient, 3), axis=1)
+    )
+    sums = jnp.broadcast_to(jnp.sum(gradient, axis=0, keepdims=True), (16, SIDE))
+    before = dot(
+        jnp.concatenate(split(sums, 3), axis=0), (rows < cols).astype(jnp.float32).astype(jnp.bfloat16)
+    )
+    within = within[:, :SIDE] + (within[:, SIDE : 2 * SIDE] + within[:, 2 * SIDE :])
+    return within + (before[:1, :] + (before[16:17, :] + before[32:33, :]))
 
 
 def phase_of(sums_ref):
@@ -145,11 +194,17 @@
 ):
     bins = image_ref.shape[1]
     strong = strong_ref.shape[0]
+    half = bins // 2
     indices = pltpu.make_async_copy(strong_hbm, strong_ref, small_sems.at[0])
     indices.start()
-    parts = [pltpu.make_async_copy(image_hbm.at[part], image_ref.at[part], sems.at[part]) for part in range(2)]
-    for part in parts:
-        part.start()
+    chunks = []
+    for part in range(2):
+        for at in range(2):
+            span = slice(at * half, (at + 1) * half)
+            chunks.append(
+                pltpu.make_async_copy(image_hbm.at[part, span], image_ref.at[part, span], sems.at[part * 2 + at])
+            )
+            chunks[-1].start()
     others_in = [
         pltpu.make_async_copy(shifts_hbm, shifts_ref, small_sems.at[1]),
         pltpu.make_async_copy(widths_hbm, widths_ref, small_sems.at[2]),
@@ -160,37 +215,39 @@
         place_ref[row] = -1
     indices.wait()
     for at in range(strong):
-        place_ref[strong_ref[at] % bins] = at // 2 * 8 + at % 2
+        place_ref[strong_ref[at] & (bins - 1)] = at // 2 * 8 + at % 2
     others = jnp.int32(0)
+    places = []
     for row in range(bins):
         held = place_ref[row]
-        place = jnp.where(held < 0, others // 2 * 8 + others % 2 + 2, held)
-        place_ref[row] = place
+        place = jnp.where(held < 0, ((others >> 1) << 3) + (others & 1) + 2, held)
+        others = others + jnp.where(held < 0, 1, 0)
+        places.append(place)
         at_ref[SUB + row : SUB + row + 1, :] = jnp.full((1, SIDE), place, jnp.int32)
-        others = others + jnp.where(held < 0, 1, 0)
+    copies = []
+    for part in range(2):
+        for at in range(2):
+            chunks[part * 2 + at].wait()
+            for group in range(at * half // SUB, (at + 1) * half // SUB):
+                for block in range(SUB):
+                    tile = ((part * (bins // SUB) + group) * SUB + block) * SUB
+                    tiles_ref[tile : tile + SUB, :] = image_ref[
+                        part, group * SUB : (group + 1) * SUB, block * SIDE : (block + 1) * SIDE
+                    ]
+            for row in range(at * half, (at + 1) * half):
+                out_ref[part, places[row] >> 3, places[row] & 3] = tiles_ref[
+                    pl.ds(tile_at(bins, part, row), SUB, stride=SUB), :
+                ]
+        copies.append(
+            pltpu.make_async_copy(out_ref.at[part], out_hbm.at[:, pl.ds(part * 4, 4)], out_sems.at[part])
+        )
+        copies[-1].start()
     for copy in others_in:
         copy.wait()
     for at in range(2):
         line = lax.axis_index(AZ) * 2 + at
         for where, value in enumerate(row_offset(shifts_ref[line]) + (widths_ref[line],)):
             at_ref[4 * at + where : 4 * at + where + 1, :] = jnp.full((1, SIDE), value, jnp.int32)
-    copies = []
-    for part in range(2):
-        parts[part].wait()
-        for group in range(bins // SUB):
-            for block in range(SUB):
-                at = ((part * (bins // SUB) + group) * SUB + block) * SUB
-                tiles_ref[at : at + SUB, :] = image_ref[
-                    part, group * SUB : (group + 1) * SUB, block * SIDE : (block + 1) * SIDE
-                ]
-        for row in range(bins):
-            out_ref[part, place_ref[row] // 8, place_ref[row] % 8] = tiles_ref[
-                pl.ds(tile_at(bins, part, row), SUB, stride=SUB), :
-            ]
-        copies.append(
-            pltpu.make_async_copy(out_ref.at[part], out_hbm.at[:, pl.ds(part * 4, 4)], out_sems.at[part])
-        )
-        copies[-1].start()
     for copy in copies:
         copy.wait()
 
@@ -236,12 +293,12 @@
             ring[SIDE:, :] = rows_ref[: LOAD // SUB, part * 4 + at].reshape(LOAD, SIDE)
             parts.append(center(ring[pl.ds(row, WINDOW), :], ring[pl.ds(row + 1, WINDOW), :], lane, width))
         lines.append(parts)
-    gradient_sums(forward(lines, window_ref[...], right_ref[...], twist_ref), out_ref)
+    gradient_sums(forward(lines, lambda lines: multiply_window(window_ref[...], lines), right_ref, twist_ref), out_ref)
 
 
 def history_kernel(rows_ref, right_ref, right_t_ref, twist_ref, out_ref):
     lines = [[rows_ref[:, part * 4 + at].reshape(SIDE, SIDE) for part in range(2)] for at in range(4)]
-    for at, (real, imag) in enumerate(forward(lines, right_t_ref[...], right_ref[...], twist_ref)):
+    for at, (real, imag) in enumerate(forward(lines, lambda lines: multiply(right_t_ref[...], split(lines, 3)), right_ref, twist_ref)):
         out_ref[at, 0] = real
         out_ref[at, 1] = imag
 
@@ -258,18 +315,18 @@
     total_ref[...] = total
     lines = turn_back([(history_ref[at, 0], history_ref[at, 1]) for at in range(2)], total)
     centered = []
-    for at, started in enumerate(inverse_start(lines, right_t_ref[...], twist_ref)):
+    for at, started in enumerate(inverse_start(lines, right_t_ref, twist_ref)):
         row, lane, width = offsets(at_ref, at)
         cosine, sine = ring_ref[0, pl.ds(row, LOAD), :], ring_ref[1, pl.ds(row, LOAD), :]
         left = [jnp.concatenate([cosine, -sine], axis=1), jnp.concatenate([sine, cosine], axis=1)]
-        found = multiply(jnp.concatenate(left, axis=0), started)
+        found = multiply(stack(jnp.concatenate(left, axis=0)), split(started, 3))
         centered.append(
             [
                 center(found[from_row : from_row + WINDOW], found[from_row + 1 : from_row + 1 + WINDOW], lane, width)
                 for from_row in (0, LOAD)
             ]
         )
-    gradient_sums(forward(centered, window_ref[...], right_ref[...], twist_ref), out_ref)
+    gradient_sums(forward(centered, lambda lines: multiply_window(window_ref[...], lines), right_ref, twist_ref), out_ref)
 
 
 def final_kernel(
@@ -277,7 +334,8 @@
 ):
     total = total_ref[...] + phase_of(sums_ref)
     lines = turn_back([(history_ref[at, 0], history_ref[at, 1]) for at in range(4)], total)
-    found = multiply(right_ref[...], jnp.concatenate(inverse_start(lines, right_t_ref[...], twist_ref), axis=1))
+    started = inverse_start(lines, right_t_ref, twist_ref, 2)
+    found = multiply(right_ref[: 4 * SIDE, :], split(jnp.concatenate(started, axis=1), 2))
     for at in range(4):
         for part in range(2):
             line = found[part * SIDE : (part + 1) * SIDE, at * SIDE : (at + 1) * SIDE]
@@ -337,7 +395,7 @@
             moved_tiles,
             pltpu.VMEM((2, az, 4) + tile, f32),
             pltpu.SemaphoreType.DMA((3,)),
-            pltpu.SemaphoreType.DMA((2,)),
+            pltpu.SemaphoreType.DMA((4,)),
             pltpu.SemaphoreType.DMA((2,)),
         ],
         out_specs=[HBM, VMEM],

time: 142 us -> 139 us (0.979)
  Pallas kernels: 12 us -> 9.35 us
    pallas_call x10, Pallas kernels: 12 us -> 9.35 us  [call(): pl.pallas_call(kernel, out_shape=[jax.ShapeDtypeStruct(*shape) for shape...]
where the time goes in v4:
time: 139 us; the launch traced here: 138 us
  blocking collectives  117 us (84%)
  Pallas kernels  9.35 us (7%)
  waiting for transfers between devices  5.89 us (4%)
  starting transfers between devices  5.33 us (4%)
    all_to_all x7, blocking collectives, exchange(): return lax.all_to_all(array, axes, split_axis=0, concat_axis=0, tiled=True)  117 us
    pallas_call x10, Pallas kernels, call(): pl.pallas_call(kernel, out_shape=[jax.ShapeDtypeStruct(*shape) for shape...  9.35 us
    all_to_all x1, waiting for transfers between devices, exchange(): return lax.all_to_all(array, axes, split_axis=0, concat_axis=0, tiled=True)  5.89 us
    all_to_all x1, starting transfers between devices, exchange(): return lax.all_to_all(array, axes, split_axis=0, concat_axis=0, tiled=True)  5.33 us
  transfers between devices with their start and end apart: 1, of which 1 were waited for; matrix products, arithmetic and copies ran while one was open for 0% of the time, Pallas kernels for 1%

profile of v4, /device:TPU:1, one launch (start us, length us, event | category | flops | bytes accessed | tf_op | source)
XLA Modules:
  0.0 138.5 jit_solution(7186542524723113381)
XLA Ops:
  0.6 2.7 %shard_map.104 = (f32[16,8,8,128]{3,2,1,0:T(8,128)}, s32[72,128]{1,0:T(8,128)}) custom-call(s32[32]{0:T(128)} %strong_hbm.1, s32[32]{0:T(128)} %shifts_hbm.1, s32[32]{0:T(128)} %widths_hbm.1, f32[2,64,1024]{2,1,0:T(8,128)} %image_hbm.1), custom_call_target="tpu_custom_call" | custom-call | tf_op jit(solution)/shard_map/pallas_call | solution.py:354
  3.3 0.0 copy-start
  3.3 0.0 copy-start.2
  3.3 0.0 copy-start.3
  3.3 0.0 copy-start.4
  3.3 27.7 %all_to_all.40.rows_ref = f32[16,8,8,128]{3,2,1,0:T(8,128)S(1)} all-to-all(f32[16,8,8,128]{3,2,1,0:T(8,128)} %get-tuple-element.11), channel_id=1, replica_groups=mesh['zh'=4,'zl'=2,'x'=4,'yh'=4,'yl'=2,'core'=2] {'yh','yl','core'}, dimensions={0} | all-to-all | bytes 1048576 | tf_op jit(solution)/shard_map/all_to_all | solution.py:366
  31.1 0.0 copy-done
  31.1 0.0 copy-done.2
  31.1 0.0 copy-done.3
  31.1 0.0 copy-done.4
  31.1 0.8 shard_map.105
  31.8 11.5 %all_to_all.41.in_ref = f32[32,1,8,128]{3,2,1,0:T(8,128)S(1)} all-to-all(f32[32,1,8,128]{3,2,1,0:T(8,128)S(1)} %bitcast.8), channel_id=1, replica_groups=mesh['zh'=4,'zl'=2,'x'=4,'yh'=4,'yl'=2,'core'=2] {'zl','x','yl','core'}, dimensions={0} | all-to-all | bytes 262144 | tf_op jit(solution)/shard_map/all_to_all | solution.py:366
  43.3 0.0 copy-start.1
  43.3 22.3 %all_to_all.42.in_ref = f32[16,1,8,128]{3,2,1,0:T(8,128)S(1)} all-to-all(f32[16,1,8,128]{3,2,1,0:T(8,128)S(1)} %shard_map.106), channel_id=1, replica_groups=mesh['zh'=4,'zl'=2,'x'=4,'yh'=4,'yl'=2,'core'=2] {'zh','yh'}, dimensions={0} | all-to-all | bytes 131072 | tf_op jit(solution)/shard_map/all_to_all | solution.py:366
  65.7 0.7 shard_map.107
  66.3 5.3 %all-to-all-start.3 = ((f32[32,1,8,128]{3,2,1,0:T(8,128)}), f32[32,1,8,128]{3,2,1,0:T(8,128)S(1)}, u32[]{:S(2)}, u32[]{:S(2)}) async-start(f32[32,1,8,128]{3,2,1,0:T(8,128)} %shard_map.107), calls=%async_computation.3 | async-start | bytes 262144 | tf_op jit(solution)/shard_map/all_to_all | solution.py:366
  71.7 0.0 copy-done.1
  71.7 0.0 copy-start.5
  71.7 1.1 shard_map.108.history_ref
  72.8 5.9 %all-to-all-done.3 = f32[32,1,8,128]{3,2,1,0:T(8,128)S(1)} async-done(((f32[32,1,8,128]{3,2,1,0:T(8,128)}), f32[32,1,8,128]{3,2,1,0:T(8,128)S(1)}, u32[]{:S(2)}, u32[]{:S(2)}) %all-to-all-start.3) | async-done | bytes 131104 | tf_op jit(solution)/shard_map/all_to_all | solution.py:366
  78.7 0.0 copy-done.5
  78.7 1.8 %shard_map.109 = (f32[32,8,128]{2,1,0:T(8,128)S(1)}, f32[128,128]{1,0:T(8,128)S(1)}) custom-call(s32[72,128]{1,0:T(8,128)S(1)} %copy-done.4, f32[32,8,128]{2,1,0:T(8,128)S(1)} %bitcast.9, f32[4,2,128,128]{3,2,1,0:T(8,128)S(1)} %shard_map.108.history_ref, bf16[256,192]{1,0:T(8,128)(2,1)S(1)} %copy-done.3, f32[2,152,128]{2,1,0:T(8,128)S(1)} %copy-done.5, ...), custom_call_target="tpu_custom_call" | custom-call | tf_op jit(solution)/shard_map/pallas_call | solution.py:354
  80.5 10.3 %all_to_all.43.in_ref = f32[32,1,8,128]{3,2,1,0:T(8,128)S(1)} all-to-all(f32[32,1,8,128]{3,2,1,0:T(8,128)S(1)} %bitcast.10), channel_id=1, replica_groups=mesh['zh'=4,'zl'=2,'x'=4,'yh'=4,'yl'=2,'core'=2] {'zl','x','yl','core'}, dimensions={0} | all-to-all | bytes 262144 | tf_op jit(solution)/shard_map/all_to_all | solution.py:366
  90.8 13.8 %all_to_all.44.in_ref = f32[16,1,8,128]{3,2,1,0:T(8,128)S(1)} all-to-all(f32[16,1,8,128]{3,2,1,0:T(8,128)S(1)} %shard_map.110), channel_id=1, replica_groups=mesh['zh'=4,'zl'=2,'x'=4,'yh'=4,'yl'=2,'core'=2] {'zh','yh'}, dimensions={0} | all-to-all | bytes 131072 | tf_op jit(solution)/shard_map/all_to_all | solution.py:366
  104.7 11.4 %all_to_all.45 = f32[32,1,8,128]{3,2,1,0:T(8,128)S(1)} all-to-all(f32[32,1,8,128]{3,2,1,0:T(8,128)S(1)} %shard_map.111), channel_id=1, replica_groups=mesh['zh'=4,'zl'=2,'x'=4,'yh'=4,'yl'=2,'core'=2] {'zl','x','yl','core'}, dimensions={0} | all-to-all | bytes 262144 | tf_op jit(solution)/shard_map/all_to_all | solution.py:366
  116.1 1.3 shard_map.112
  117.4 20.2 %all_to_all.46 = f32[16,8,8,128]{3,2,1,0:T(8,128)S(1)} all-to-all(f32[16,8,8,128]{3,2,1,0:T(8,128)S(1)} %get-tuple-element.14), channel_id=1, replica_groups=mesh['zh'=4,'zl'=2,'x'=4,'yh'=4,'yl'=2,'core'=2] {'yh','yl','core'}, dimensions={0} | all-to-all | bytes 1048576 | tf_op jit(solution)/shard_map/all_to_all | solution.py:366
  137.5 1.0 shard_map.113
  (3 shorter events, 0.1 us)
Async XLA Ops:
  3.3 27.8 %copy-start = (bf16[768,256]{1,0:T(8,128)(2,1)S(1)}, bf16[768,256]{1,0:T(8,128)(2,1)}, u32[]{:S(2)}) copy-start(bf16[768,256]{1,0:T(8,128)(2,1)} %constant.12.clone.right_ref) | copy-start | bytes 1179652
  3.3 27.8 %copy-start.2 = (f32[2,128,128]{2,1,0:T(8,128)S(1)}, f32[2,128,128]{2,1,0:T(8,128)}, u32[]{:S(2)}) copy-start(f32[2,128,128]{2,1,0:T(8,128)} %constant.11.clone.twist_ref) | copy-start | bytes 393220
  3.3 27.7 %copy-start.3 = (bf16[256,192]{1,0:T(8,128)(2,1)S(1)}, bf16[256,192]{1,0:T(8,128)(2,1)}, u32[]{:S(2)}) copy-start(bf16[256,192]{1,0:T(8,128)(2,1)} %constant.14.clone.window_ref) | copy-start | bytes 294916
  3.3 27.7 %copy-start.4 = (s32[72,128]{1,0:T(8,128)S(1)}, s32[72,128]{1,0:T(8,128)}, u32[]{:S(2)}) copy-start(s32[72,128]{1,0:T(8,128)} %get-tuple-element.10.at_ref) | copy-start | bytes 110596
  43.3 28.4 %copy-start.1 = (bf16[768,256]{1,0:T(8,128)(2,1)S(1)}, bf16[768,256]{1,0:T(8,128)(2,1)}, u32[]{:S(2)}) copy-start(bf16[768,256]{1,0:T(8,128)(2,1)} %constant.13.clone.right_t_ref) | copy-start | bytes 1179652
  66.3 12.4 %all-to-all-start.3 = ((f32[32,1,8,128]{3,2,1,0:T(8,128)}), f32[32,1,8,128]{3,2,1,0:T(8,128)S(1)}, u32[]{:S(2)}, u32[]{:S(2)}) async-start(f32[32,1,8,128]{3,2,1,0:T(8,128)} %shard_map.107), calls=%async_computation.3 | async-start | bytes 262144 | tf_op jit(solution)/shard_map/all_to_all | solution.py:366
  71.7 7.0 %copy-start.5 = (f32[2,152,128]{2,1,0:T(8,128)S(1)}, f32[2,152,128]{2,1,0:T(8,128)}, u32[]{:S(2)}) copy-start(f32[2,152,128]{2,1,0:T(8,128)} %constant.10.clone.ring_ref) | copy-start | bytes 466948

commit v5 on v4

--- a/solution.py
+++ b/solution.py
@@ -12,6 +12,7 @@
 TILES = SIDE // SUB
 WINDOW = 16
 FIRST = SIDE // 2 - WINDOW // 2
+RIGHT, RIGHT_T = 0, 1
 LOAD = 24
 
 
@@ -29,15 +30,17 @@
     twist = np.stack([np.cos(twist), np.sin(twist)]) / SIDE
     made = dict(ring=ring, twist=twist)
     made = {name: jnp.asarray(table.astype(np.float32)) for name, table in made.items()}
-    for name, table in dict(right=right, right_t=right.T, window=window).items():
-        parts, rest = [], table.astype(np.float32)
+
+    def parts(table):
+        found, rest = [], table.astype(np.float32)
         for _ in range(3):
-            parts.append(rest.astype(jnp.bfloat16))
-            rest = rest - parts[-1].astype(np.float32)
-        if name == "window":
-            made[name] = jnp.asarray(np.concatenate([parts[at] for at in (0, 0, 1, 0, 1, 2)], axis=1))
-        else:
-            made[name] = jnp.asarray(np.concatenate(parts, axis=0))
+            found.append(rest.astype(jnp.bfloat16))
+            rest = rest - found[-1].astype(np.float32)
+        return found
+
+    window = parts(window)
+    made["window"] = jnp.asarray(np.concatenate([window[at] for at in (0, 0, 1, 0, 1, 2)], axis=1))
+    made["sides"] = jnp.asarray(np.concatenate(parts(right) + parts(right.T), axis=0))
     return made
 
 
@@ -77,7 +80,7 @@
     return dot(left, jnp.concatenate([first, second, first, third, second, first], axis=0))
 
 
-def forward(lines, first_stage, right_ref, twist_ref):
+def forward(lines, first_stage, sides_ref, twist_ref, count=3):
     cosine, sine = twist_ref[0], twist_ref[1]
     first = first_stage(jnp.concatenate([jnp.concatenate(line, axis=0) for line in lines], axis=1))
     turned = []
@@ -85,17 +88,17 @@
         real = first[:SIDE, at * SIDE : (at + 1) * SIDE]
         imag = first[SIDE:, at * SIDE : (at + 1) * SIDE]
         turned.append(jnp.concatenate([real * cosine + imag * sine, imag * cosine - real * sine], axis=1))
-    second = multiply(stack(jnp.concatenate(turned, axis=0)), parts_of(right_ref))
+    second = multiply(stack(jnp.concatenate(turned, axis=0), count), parts_of(sides_ref, RIGHT, count))
     return [
         (second[at * SIDE : (at + 1) * SIDE, :SIDE], second[at * SIDE : (at + 1) * SIDE, SIDE:])
         for at in range(len(lines))
     ]
 
 
-def inverse_start(lines, right_t_ref, twist_ref, count=3):
+def inverse_start(lines, sides_ref, twist_ref, count=3):
     cosine, sine = twist_ref[0], twist_ref[1]
     stacked = jnp.concatenate([jnp.concatenate(line, axis=1) for line in lines], axis=0)
-    first = multiply(stack(stacked, count), parts_of(right_t_ref, count))
+    first = multiply(stack(stacked, count), parts_of(sides_ref, RIGHT_T, count))
     turned = []
     for at in range(len(lines)):
         real = first[at * SIDE : (at + 1) * SIDE, :SIDE]
@@ -104,8 +107,12 @@
     return turned
 
 
-def parts_of(table_ref, count=3):
-    return [table_ref[at * 2 * SIDE : (at + 1) * 2 * SIDE, :] for at in range(count)]
+def stacked_of(sides_ref, which, count=3):
+    return sides_ref[which * 6 * SIDE : (which * 6 + 2 * count) * SIDE, :]
+
+
+def parts_of(sides_ref, which, count=3):
+    return [sides_ref[(which * 3 + at) * 2 * SIDE : (which * 3 + at + 1) * 2 * SIDE, :] for at in range(count)]
 
 
 def grid_of(rows):
@@ -189,8 +196,8 @@
 
 
 def pack_kernel(
-    strong_hbm, shifts_hbm, widths_hbm, image_hbm, out_hbm, at_ref,
-    place_ref, strong_ref, shifts_ref, widths_ref, image_ref, tiles_ref, out_ref, small_sems, sems, out_sems,
+    strong_hbm, shifts_hbm, widths_hbm, image_hbm, out_hbm, at_hbm,
+    place_ref, strong_ref, shifts_ref, widths_ref, image_ref, tiles_ref, out_ref, at_ref, small_sems, sems, out_sems,
 ):
     bins = image_ref.shape[1]
     strong = strong_ref.shape[0]
@@ -224,7 +231,14 @@
         others = others + jnp.where(held < 0, 1, 0)
         places.append(place)
         at_ref[SUB + row : SUB + row + 1, :] = jnp.full((1, SIDE), place, jnp.int32)
-    copies = []
+    for copy in others_in:
+        copy.wait()
+    for at in range(2):
+        line = lax.axis_index(AZ) * 2 + at
+        for where, value in enumerate(row_offset(shifts_ref[line]) + (widths_ref[line],)):
+            at_ref[4 * at + where : 4 * at + where + 1, :] = jnp.full((1, SIDE), value, jnp.int32)
+    copies = [pltpu.make_async_copy(at_ref, at_hbm, out_sems.at[2])]
+    copies[0].start()
     for part in range(2):
         for at in range(2):
             chunks[part * 2 + at].wait()
@@ -242,12 +256,6 @@
             pltpu.make_async_copy(out_ref.at[part], out_hbm.at[:, pl.ds(part * 4, 4)], out_sems.at[part])
         )
         copies[-1].start()
-    for copy in others_in:
-        copy.wait()
-    for at in range(2):
-        line = lax.axis_index(AZ) * 2 + at
-        for where, value in enumerate(row_offset(shifts_ref[line]) + (widths_ref[line],)):
-            at_ref[4 * at + where : 4 * at + where + 1, :] = jnp.full((1, SIDE), value, jnp.int32)
     for copy in copies:
         copy.wait()
 
@@ -282,25 +290,31 @@
     return [at_ref[4 * line + where, 0] for where in range(3)]
 
 
-def first_kernel(at_ref, rows_ref, window_ref, right_ref, twist_ref, out_ref, ring_ref):
+def first_kernel(
+    at_ref, rows_ref, window_ref, sides_ref, twist_ref, out_ref, history_ref, ring_ref
+):
     lines = []
     for at in range(2):
         row, lane, width = offsets(at_ref, at)
         parts = []
         for part in range(2):
             ring = ring_ref.at[at * 2 + part]
-            ring[:SIDE, :] = rows_ref[:, part * 4 + at].reshape(SIDE, SIDE)
+            ring[:SIDE, :] = square(rows_ref, part * 4 + at)
             ring[SIDE:, :] = rows_ref[: LOAD // SUB, part * 4 + at].reshape(LOAD, SIDE)
             parts.append(center(ring[pl.ds(row, WINDOW), :], ring[pl.ds(row + 1, WINDOW), :], lane, width))
         lines.append(parts)
-    gradient_sums(forward(lines, lambda lines: multiply_window(window_ref[...], lines), right_ref, twist_ref), out_ref)
-
-
-def history_kernel(rows_ref, right_ref, right_t_ref, twist_ref, out_ref):
-    lines = [[rows_ref[:, part * 4 + at].reshape(SIDE, SIDE) for part in range(2)] for at in range(4)]
-    for at, (real, imag) in enumerate(forward(lines, lambda lines: multiply(right_t_ref[...], split(lines, 3)), right_ref, twist_ref)):
-        out_ref[at, 0] = real
-        out_ref[at, 1] = imag
+    gradient_sums(forward(lines, lambda lines: multiply_window(window_ref[...], lines), sides_ref, twist_ref), out_ref)
+    for begin, count in ((0, 3), (2, 2)):
+        lines = [[square(rows_ref, part * 4 + begin + at) for part in range(2)] for at in range(2)]
+        whole = stacked_of(sides_ref, RIGHT_T, count)
+        spectra = forward(lines, lambda lines: multiply(whole, split(lines, count)), sides_ref, twist_ref, count)
+        for at in range(2):
+            for part in range(2):
+                history_ref[begin + at, part] = spectra[at][part]
+
+
+def square(rows_ref, slot):
+    return rows_ref[:, slot].reshape(SIDE, SIDE)
 
 
 def share_kernel(in_ref, out_ref):
@@ -308,14 +322,14 @@
 
 
 def second_kernel(
-    at_ref, sums_ref, history_ref, window_ref, ring_ref, right_ref, right_t_ref, twist_ref,
+    at_ref, sums_ref, history_ref, window_ref, ring_ref, sides_ref, twist_ref,
     out_ref, total_ref,
 ):
     total = phase_of(sums_ref)
     total_ref[...] = total
     lines = turn_back([(history_ref[at, 0], history_ref[at, 1]) for at in range(2)], total)
     centered = []
-    for at, started in enumerate(inverse_start(lines, right_t_ref, twist_ref)):
+    for at, started in enumerate(inverse_start(lines, sides_ref, twist_ref)):
         row, lane, width = offsets(at_ref, at)
         cosine, sine = ring_ref[0, pl.ds(row, LOAD), :], ring_ref[1, pl.ds(row, LOAD), :]
         left = [jnp.concatenate([cosine, -sine], axis=1), jnp.concatenate([sine, cosine], axis=1)]
@@ -326,16 +340,16 @@
                 for from_row in (0, LOAD)
             ]
         )
-    gradient_sums(forward(centered, lambda lines: multiply_window(window_ref[...], lines), right_ref, twist_ref), out_ref)
+    gradient_sums(forward(centered, lambda lines: multiply_window(window_ref[...], lines), sides_ref, twist_ref), out_ref)
 
 
 def final_kernel(
-    sums_ref, total_ref, history_ref, right_ref, right_t_ref, twist_ref, out_ref, phase_ref, turned_ref
+    sums_ref, total_ref, history_ref, sides_ref, twist_ref, out_ref, phase_ref, turned_ref
 ):
     total = total_ref[...] + phase_of(sums_ref)
     lines = turn_back([(history_ref[at, 0], history_ref[at, 1]) for at in range(4)], total)
-    started = inverse_start(lines, right_t_ref, twist_ref, 2)
-    found = multiply(right_ref[: 4 * SIDE, :], split(jnp.concatenate(started, axis=1), 2))
+    started = inverse_start(lines, sides_ref, twist_ref, 2)
+    found = multiply(stacked_of(sides_ref, RIGHT, 2), split(jnp.concatenate(started, axis=1), 2))
     for at in range(4):
         for part in range(2):
             line = found[part * SIDE : (part + 1) * SIDE, at * SIDE : (at + 1) * SIDE]
@@ -394,33 +408,25 @@
             pltpu.VMEM(sar_image.shape, f32),
             moved_tiles,
             pltpu.VMEM((2, az, 4) + tile, f32),
+            pltpu.VMEM((SUB + bins, SIDE), i32),
             pltpu.SemaphoreType.DMA((3,)),
             pltpu.SemaphoreType.DMA((4,)),
-            pltpu.SemaphoreType.DMA((2,)),
+            pltpu.SemaphoreType.DMA((3,)),
         ],
-        out_specs=[HBM, VMEM],
+        out_specs=[HBM, HBM],
         vmem=PACK_VMEM,
     )
     rows = exchange(packed, AZ)
-    sums = call(
+    sums, history = call(
         first_kernel,
-        [((2 * TILES,) + tile, f32)],
+        [((2 * TILES,) + tile, f32), ((4, 2, SIDE, SIDE), f32)],
         [VMEM] * 5,
         places,
         rows,
         table["window"],
-        table["right"],
+        table["sides"],
         table["twist"],
         scratch=[pltpu.VMEM((4, SIDE + LOAD, SIDE), f32)],
-    )
-    history = call(
-        history_kernel,
-        [((4, 2, SIDE, SIDE), f32)],
-        [VMEM] * 4,
-        rows,
-        table["right"],
-        table["right_t"],
-        table["twist"],
     )
 
     def all_sums(sums):
@@ -435,26 +441,24 @@
     sums, total = call(
         second_kernel,
         [((2 * TILES,) + tile, f32), ((SIDE, SIDE), f32)],
-        [VMEM] * 8,
+        [VMEM] * 7,
         places,
         summed,
         history,
         table["window"],
         table["ring"],
-        table["right"],
-        table["right_t"],
+        table["sides"],
         table["twist"],
     )
     summed = all_sums(sums)
     corrected, phase = call(
         final_kernel,
         [((az, 8) + tile, f32), (tile, f32)],
-        [VMEM] * 6,
+        [VMEM] * 5,
         summed,
         total,
         history,
-        table["right"],
-        table["right_t"],
+        table["sides"],
         table["twist"],
         scratch=[pltpu.VMEM((SIDE, SIDE), f32)],
     )

time: 139 us -> 138 us (level)
  blocking collectives: 117 us -> 129 us
  waiting for transfers between devices: 5.89 us -> 0 us
  starting transfers between devices: 5.33 us -> 0 us
  Pallas kernels: 9.35 us -> 7.52 us
    all_to_all x7 -> x8, blocking collectives: 117 us -> 129 us  [exchange(): return lax.all_to_all(array, axes, split_axis=0, concat_axis=0, tiled=True)]
    all_to_all x1 -> x0, waiting for transfers between devices: 5.89 us -> none  [exchange(): return lax.all_to_all(array, axes, split_axis=0, concat_axis=0, tiled=True)]
    all_to_all x1 -> x0, starting transfers between devices: 5.33 us -> none  [exchange(): return lax.all_to_all(array, axes, split_axis=0, concat_axis=0, tiled=True)]
    pallas_call x10 -> x9, Pallas kernels: 9.35 us -> 7.52 us  [call(): pl.pallas_call(kernel, out_shape=[jax.ShapeDtypeStruct(*shape) for shape...]
  transfers between devices with their start and end apart: 1 -> 0, of which waited for: 1 -> 0; matrix products, arithmetic and copies ran while one was open for 0% -> 0% of each run, Pallas kernels for 1% -> 0%
where the time goes in v5:
time: 138 us; the launch traced here: 137 us
  blocking collectives  129 us (93%)
  Pallas kernels  7.52 us (5%)
    all_to_all x8, blocking collectives, exchange(): return lax.all_to_all(array, axes, split_axis=0, concat_axis=0, tiled=True)  129 us
    pallas_call x9, Pallas kernels, call(): pl.pallas_call(kernel, out_shape=[jax.ShapeDtypeStruct(*shape) for shape...  7.52 us

profile of v5, /device:TPU:1, one launch (start us, length us, event | category | flops | bytes accessed | tf_op | source)
XLA Modules:
  0.0 137.1 jit_solution(18269735032779336585)
XLA Ops:
  0.6 0.0 copy-start
  0.6 2.1 %shard_map.95 = (f32[16,8,8,128]{3,2,1,0:T(8,128)}, s32[72,128]{1,0:T(8,128)}) custom-call(s32[32]{0:T(128)} %strong_hbm.1, s32[32]{0:T(128)} %shifts_hbm.1, s32[32]{0:T(128)} %widths_hbm.1, f32[2,64,1024]{2,1,0:T(8,128)} %image_hbm.1), custom_call_target="tpu_custom_call" | custom-call | tf_op jit(solution)/shard_map/pallas_call | solution.py:368
  2.8 0.0 copy-start.1
  2.8 0.0 copy-start.2
  2.8 0.0 copy-start.3
  2.8 27.7 %all_to_all.40.rows_ref = f32[16,8,8,128]{3,2,1,0:T(8,128)S(1)} all-to-all(f32[16,8,8,128]{3,2,1,0:T(8,128)} %get-tuple-element.13), channel_id=1, replica_groups=mesh['zh'=4,'zl'=2,'x'=4,'yh'=4,'yl'=2,'core'=2] {'yh','yl','core'}, dimensions={0} | all-to-all | bytes 1048576 | tf_op jit(solution)/shard_map/all_to_all | solution.py:380
  30.5 0.0 copy-done
  30.5 0.0 copy-done.1
  30.5 0.0 copy-done.2
  30.5 0.0 copy-done.3
  30.5 1.2 shard_map.96
  31.8 11.5 %all_to_all.41.in_ref = f32[32,1,8,128]{3,2,1,0:T(8,128)S(1)} all-to-all(f32[32,1,8,128]{3,2,1,0:T(8,128)S(1)} %bitcast.10), channel_id=1, replica_groups=mesh['zh'=4,'zl'=2,'x'=4,'yh'=4,'yl'=2,'core'=2] {'zl','x','yl','core'}, dimensions={0} | all-to-all | bytes 262144 | tf_op jit(solution)/shard_map/all_to_all | solution.py:380
  43.3 22.2 %all_to_all.42.in_ref = f32[16,1,8,128]{3,2,1,0:T(8,128)S(1)} all-to-all(f32[16,1,8,128]{3,2,1,0:T(8,128)S(1)} %shard_map.97), channel_id=1, replica_groups=mesh['zh'=4,'zl'=2,'x'=4,'yh'=4,'yl'=2,'core'=2] {'zh','yh'}, dimensions={0} | all-to-all | bytes 131072 | tf_op jit(solution)/shard_map/all_to_all | solution.py:380
  65.5 0.0 copy-start.4
  65.5 11.8 %all_to_all.43 = f32[32,1,8,128]{3,2,1,0:T(8,128)S(1)} all-to-all(f32[32,1,8,128]{3,2,1,0:T(8,128)S(1)} %shard_map.98), channel_id=1, replica_groups=mesh['zh'=4,'zl'=2,'x'=4,'yh'=4,'yl'=2,'core'=2] {'zl','x','yl','core'}, dimensions={0} | all-to-all | bytes 262144 | tf_op jit(solution)/shard_map/all_to_all | solution.py:380
  77.3 0.0 copy-done.4
  77.3 1.8 %shard_map.99 = (f32[32,8,128]{2,1,0:T(8,128)S(1)}, f32[128,128]{1,0:T(8,128)S(1)}) custom-call(s32[72,128]{1,0:T(8,128)S(1)} %copy-done.3, f32[32,8,128]{2,1,0:T(8,128)S(1)} %bitcast.8, f32[4,2,128,128]{3,2,1,0:T(8,128)S(1)} %get-tuple-element.15.history_ref, bf16[256,192]{1,0:T(8,128)(2,1)S(1)} %copy-done.2, f32[2,152,128]{2,1,0:T(8,128)S(1)} %copy-done.4, ...), custom_call_target="tpu_custom_call" | custom-call | tf_op jit(solution)/shard_map/pallas_call | solution.py:368
  79.2 10.3 %all_to_all.44.in_ref = f32[32,1,8,128]{3,2,1,0:T(8,128)S(1)} all-to-all(f32[32,1,8,128]{3,2,1,0:T(8,128)S(1)} %bitcast.9), channel_id=1, replica_groups=mesh['zh'=4,'zl'=2,'x'=4,'yh'=4,'yl'=2,'core'=2] {'zl','x','yl','core'}, dimensions={0} | all-to-all | bytes 262144 | tf_op jit(solution)/shard_map/all_to_all | solution.py:380
  89.4 13.8 %all_to_all.45.in_ref = f32[16,1,8,128]{3,2,1,0:T(8,128)S(1)} all-to-all(f32[16,1,8,128]{3,2,1,0:T(8,128)S(1)} %shard_map.100), channel_id=1, replica_groups=mesh['zh'=4,'zl'=2,'x'=4,'yh'=4,'yl'=2,'core'=2] {'zh','yh'}, dimensions={0} | all-to-all | bytes 131072 | tf_op jit(solution)/shard_map/all_to_all | solution.py:380
  103.3 11.4 %all_to_all.46 = f32[32,1,8,128]{3,2,1,0:T(8,128)S(1)} all-to-all(f32[32,1,8,128]{3,2,1,0:T(8,128)S(1)} %shard_map.101), channel_id=1, replica_groups=mesh['zh'=4,'zl'=2,'x'=4,'yh'=4,'yl'=2,'core'=2] {'zl','x','yl','core'}, dimensions={0} | all-to-all | bytes 262144 | tf_op jit(solution)/shard_map/all_to_all | solution.py:380
  114.7 1.3 shard_map.102
  116.0 20.2 %all_to_all.47 = f32[16,8,8,128]{3,2,1,0:T(8,128)S(1)} all-to-all(f32[16,8,8,128]{3,2,1,0:T(8,128)S(1)} %get-tuple-element.18), channel_id=1, replica_groups=mesh['zh'=4,'zl'=2,'x'=4,'yh'=4,'yl'=2,'core'=2] {'yh','yl','core'}, dimensions={0} | all-to-all | bytes 1048576 | tf_op jit(solution)/shard_map/all_to_all | solution.py:380
  136.2 1.0 shard_map.103
  (4 shorter events, 0.1 us)
Async XLA Ops:
  0.6 29.9 %copy-start = (bf16[1536,256]{1,0:T(8,128)(2,1)S(1)}, bf16[1536,256]{1,0:T(8,128)(2,1)}, u32[]{:S(2)}) copy-start(bf16[1536,256]{1,0:T(8,128)(2,1)} %constant.11.clone.sides_ref) | copy-start | bytes 2359300
  2.8 27.8 %copy-start.1 = (f32[2,128,128]{2,1,0:T(8,128)S(1)}, f32[2,128,128]{2,1,0:T(8,128)}, u32[]{:S(2)}) copy-start(f32[2,128,128]{2,1,0:T(8,128)} %constant.9.clone.twist_ref) | copy-start | bytes 393220
  2.8 27.7 %copy-start.2 = (bf16[256,192]{1,0:T(8,128)(2,1)S(1)}, bf16[256,192]{1,0:T(8,128)(2,1)}, u32[]{:S(2)}) copy-start(bf16[256,192]{1,0:T(8,128)(2,1)} %constant.10.clone.window_ref) | copy-start | bytes 294916
  2.8 27.7 %copy-start.3 = (s32[72,128]{1,0:T(8,128)S(1)}, s32[72,128]{1,0:T(8,128)}, u32[]{:S(2)}) copy-start(s32[72,128]{1,0:T(8,128)} %get-tuple-element.12.at_ref) | copy-start | bytes 110596
  65.5 11.8 %copy-start.4 = (f32[2,152,128]{2,1,0:T(8,128)S(1)}, f32[2,152,128]{2,1,0:T(8,128)}, u32[]{:S(2)}) copy-start(f32[2,152,128]{2,1,0:T(8,128)} %constant.8.clone.ring_ref) | copy-start | bytes 466948

commit v6 on v5

--- a/solution.py
+++ b/solution.py
@@ -135,9 +135,11 @@
     return within + (before[:1, :] + (before[16:17, :] + before[32:33, :]))
 
 
-def phase_of(sums_ref):
-    gradient = sums_ref[:TILES] / (sums_ref[TILES:] + EPSILON)
-    return running_sum(gradient.reshape(SIDE, SIDE))
+def phase_of(gradient_ref, whole_ref):
+    near, rows = gradient_ref.shape[:2]
+    for at in range(near):
+        whole_ref[at * rows : (at + 1) * rows, :] = gradient_ref[at]
+    return running_sum(whole_ref[...])
 
 
 def cosine_sine(angle):
@@ -187,8 +189,10 @@
         numerator = numerator + (before(real) * imag - before(imag) * real)
         denominator = denominator + (real * real + imag * imag)
     numerator = jnp.where((rows == 0) & (cols == 0), 0.0, numerator)
-    out_ref[:TILES] = numerator.reshape(TILES, SUB, SIDE)
-    out_ref[TILES:] = denominator.reshape(TILES, SUB, SIDE)
+    near, _, part = out_ref.shape[:3]
+    for at in range(near):
+        out_ref[at, 0] = numerator[at * part : (at + 1) * part, :]
+        out_ref[at, 1] = denominator[at * part : (at + 1) * part, :]
 
 
 def tile_at(bins, part, row):
@@ -321,11 +325,16 @@
     out_ref[...] = jnp.broadcast_to(jnp.sum(in_ref[...], axis=0)[None], out_ref.shape)
 
 
+def gradient_kernel(in_ref, out_ref):
+    sums = jnp.sum(in_ref[...], axis=0)
+    out_ref[...] = jnp.broadcast_to((sums[0] / (sums[1] + EPSILON))[None], out_ref.shape)
+
+
 def second_kernel(
-    at_ref, sums_ref, history_ref, window_ref, ring_ref, sides_ref, twist_ref,
-    out_ref, total_ref,
+    at_ref, gradient_ref, history_ref, window_ref, ring_ref, sides_ref, twist_ref,
+    out_ref, total_ref, whole_ref,
 ):
-    total = phase_of(sums_ref)
+    total = phase_of(gradient_ref, whole_ref)
     total_ref[...] = total
     lines = turn_back([(history_ref[at, 0], history_ref[at, 1]) for at in range(2)], total)
     centered = []
@@ -344,9 +353,9 @@
 
 
 def final_kernel(
-    sums_ref, total_ref, history_ref, sides_ref, twist_ref, out_ref, phase_ref, turned_ref
+    gradient_ref, total_ref, history_ref, sides_ref, twist_ref, out_ref, phase_ref, turned_ref
 ):
-    total = total_ref[...] + phase_of(sums_ref)
+    total = total_ref[...] + phase_of(gradient_ref, turned_ref)
     lines = turn_back([(history_ref[at, 0], history_ref[at, 1]) for at in range(4)], total)
     started = inverse_start(lines, sides_ref, twist_ref, 2)
     found = multiply(stacked_of(sides_ref, RIGHT, 2), split(jnp.concatenate(started, axis=1), 2))
@@ -392,6 +401,8 @@
     bins, pulses_local = sar_image.shape[1:]
     table = tables()
     tile = (SUB, SIDE)
+    part = SIDE // near
+    sums_shape = (near, 2, part, SIDE)
     moved_tiles = pltpu.VMEM((2 * bins * SUB, SIDE), f32)
 
     packed, places = call(
@@ -419,7 +430,7 @@
     rows = exchange(packed, AZ)
     sums, history = call(
         first_kernel,
-        [((2 * TILES,) + tile, f32), ((4, 2, SIDE, SIDE), f32)],
+        [(sums_shape, f32), ((4, 2, SIDE, SIDE), f32)],
         [VMEM] * 5,
         places,
         rows,
@@ -429,33 +440,33 @@
         scratch=[pltpu.VMEM((4, SIDE + LOAD, SIDE), f32)],
     )
 
-    def all_sums(sums):
-        each = 2 * TILES // near
-        scattered = exchange(sums.reshape((near, each) + tile), NEAR)
-        partial = call(share_kernel, [((far, each) + tile, f32)], [VMEM], scattered)
+    def all_gradients(sums):
+        scattered = exchange(sums, NEAR)
+        partial = call(share_kernel, [((far, 2, part, SIDE), f32)], [VMEM], scattered)
         everyone = exchange(partial, FAR)
-        whole = call(share_kernel, [((near, each) + tile, f32)], [VMEM], everyone)
-        return exchange(whole, NEAR).reshape((2 * TILES,) + tile)
-
-    summed = all_sums(sums)
+        gradient = call(gradient_kernel, [((near, part, SIDE), f32)], [VMEM], everyone)
+        return exchange(gradient, NEAR)
+
+    gradient = all_gradients(sums)
     sums, total = call(
         second_kernel,
-        [((2 * TILES,) + tile, f32), ((SIDE, SIDE), f32)],
+        [(sums_shape, f32), ((SIDE, SIDE), f32)],
         [VMEM] * 7,
         places,
-        summed,
+        gradient,
         history,
         table["window"],
         table["ring"],
         table["sides"],
         table["twist"],
-    )
-    summed = all_sums(sums)
+        scratch=[pltpu.VMEM((SIDE, SIDE), f32)],
+    )
+    gradient = all_gradients(sums)
     corrected, phase = call(
         final_kernel,
         [((az, 8) + tile, f32), (tile, f32)],
         [VMEM] * 5,
-        summed,
+        gradient,
         total,
         history,
         table["sides"],

time: 138 us -> 137 us (level)
  no operation moved by 1% of the time
where the time goes in v6:
time: 137 us; the launch traced here: 136 us
  blocking collectives  128 us (93%)
  Pallas kernels  7.54 us (6%)
    all_to_all x8, blocking collectives, exchange(): return lax.all_to_all(array, axes, split_axis=0, concat_axis=0, tiled=True)  128 us
    pallas_call x9, Pallas kernels, call(): pl.pallas_call(kernel, out_shape=[jax.ShapeDtypeStruct(*shape) for shape...  7.54 us

profile of v6, /device:TPU:1, one launch (start us, length us, event | category | flops | bytes accessed | tf_op | source)
XLA Modules:
  0.0 136.4 jit_solution(14351362367277496570)
XLA Ops:
  0.6 0.0 copy-start
  0.6 2.1 %shard_map.95 = (f32[16,8,8,128]{3,2,1,0:T(8,128)}, s32[72,128]{1,0:T(8,128)}) custom-call(s32[32]{0:T(128)} %strong_hbm.1, s32[32]{0:T(128)} %shifts_hbm.1, s32[32]{0:T(128)} %widths_hbm.1, f32[2,64,1024]{2,1,0:T(8,128)} %image_hbm.1), custom_call_target="tpu_custom_call" | custom-call | tf_op jit(solution)/shard_map/pallas_call | solution.py:377
  2.8 0.0 copy-start.1
  2.8 0.0 copy-start.2
  2.8 0.0 copy-start.3
  2.8 27.7 %all_to_all.40.rows_ref = f32[16,8,8,128]{3,2,1,0:T(8,128)S(1)} all-to-all(f32[16,8,8,128]{3,2,1,0:T(8,128)} %get-tuple-element.13), channel_id=1, replica_groups=mesh['zh'=4,'zl'=2,'x'=4,'yh'=4,'yl'=2,'core'=2] {'yh','yl','core'}, dimensions={0} | all-to-all | bytes 1048576 | tf_op jit(solution)/shard_map/all_to_all | solution.py:389
  30.5 0.0 copy-done
  30.5 0.0 copy-done.1
  30.5 0.0 copy-done.2
  30.5 0.0 copy-done.3
  30.5 1.2 shard_map.96
  31.8 11.5 %all_to_all.41.in_ref = f32[32,2,4,128]{3,2,1,0:T(4,128)S(1)} all-to-all(f32[32,2,4,128]{3,2,1,0:T(4,128)S(1)} %get-tuple-element.14), channel_id=1, replica_groups=mesh['zh'=4,'zl'=2,'x'=4,'yh'=4,'yl'=2,'core'=2] {'zl','x','yl','core'}, dimensions={0} | all-to-all | bytes 262144 | tf_op jit(solution)/shard_map/all_to_all | solution.py:389
  43.3 22.2 %all_to_all.42.in_ref = f32[16,2,4,128]{3,2,1,0:T(4,128)S(1)} all-to-all(f32[16,2,4,128]{3,2,1,0:T(4,128)S(1)} %shard_map.97), channel_id=1, replica_groups=mesh['zh'=4,'zl'=2,'x'=4,'yh'=4,'yl'=2,'core'=2] {'zh','yh'}, dimensions={0} | all-to-all | bytes 131072 | tf_op jit(solution)/shard_map/all_to_all | solution.py:389
  65.5 0.0 copy-start.4
  65.5 11.6 %all_to_all.43.gradient_ref = f32[32,4,128]{2,1,0:T(4,128)S(1)} all-to-all(f32[32,4,128]{2,1,0:T(4,128)S(1)} %shard_map.98), channel_id=1, replica_groups=mesh['zh'=4,'zl'=2,'x'=4,'yh'=4,'yl'=2,'core'=2] {'zl','x','yl','core'}, dimensions={0} | all-to-all | bytes 131072 | tf_op jit(solution)/shard_map/all_to_all | solution.py:389
  77.1 0.0 copy-done.4
  77.1 1.8 %shard_map.99 = (f32[32,2,4,128]{3,2,1,0:T(4,128)S(1)}, f32[128,128]{1,0:T(8,128)S(1)}) custom-call(s32[72,128]{1,0:T(8,128)S(1)} %copy-done.3, f32[32,4,128]{2,1,0:T(4,128)S(1)} %all_to_all.43.gradient_ref, f32[4,2,128,128]{3,2,1,0:T(8,128)S(1)} %get-tuple-element.15.history_ref, bf16[256,192]{1,0:T(8,128)(2,1)S(1)} %copy-done.2, ...), custom_call_target="tpu_custom_call" | custom-call | tf_op jit(solution)/shard_map/pallas_call | solution.py:377
  78.9 10.1 %all_to_all.44.in_ref = f32[32,2,4,128]{3,2,1,0:T(4,128)S(1)} all-to-all(f32[32,2,4,128]{3,2,1,0:T(4,128)S(1)} %get-tuple-element.16), channel_id=1, replica_groups=mesh['zh'=4,'zl'=2,'x'=4,'yh'=4,'yl'=2,'core'=2] {'zl','x','yl','core'}, dimensions={0} | all-to-all | bytes 262144 | tf_op jit(solution)/shard_map/all_to_all | solution.py:389
  89.0 13.9 %all_to_all.45.in_ref = f32[16,2,4,128]{3,2,1,0:T(4,128)S(1)} all-to-all(f32[16,2,4,128]{3,2,1,0:T(4,128)S(1)} %shard_map.100), channel_id=1, replica_groups=mesh['zh'=4,'zl'=2,'x'=4,'yh'=4,'yl'=2,'core'=2] {'zh','yh'}, dimensions={0} | all-to-all | bytes 131072 | tf_op jit(solution)/shard_map/all_to_all | solution.py:389
  102.9 11.2 %all_to_all.46.gradient_ref = f32[32,4,128]{2,1,0:T(4,128)S(1)} all-to-all(f32[32,4,128]{2,1,0:T(4,128)S(1)} %shard_map.101), channel_id=1, replica_groups=mesh['zh'=4,'zl'=2,'x'=4,'yh'=4,'yl'=2,'core'=2] {'zl','x','yl','core'}, dimensions={0} | all-to-all | bytes 131072 | tf_op jit(solution)/shard_map/all_to_all | solution.py:389
  114.0 1.3 shard_map.102
  115.3 20.2 %all_to_all.47 = f32[16,8,8,128]{3,2,1,0:T(8,128)S(1)} all-to-all(f32[16,8,8,128]{3,2,1,0:T(8,128)S(1)} %get-tuple-element.18), channel_id=1, replica_groups=mesh['zh'=4,'zl'=2,'x'=4,'yh'=4,'yl'=2,'core'=2] {'yh','yl','core'}, dimensions={0} | all-to-all | bytes 1048576 | tf_op jit(solution)/shard_map/all_to_all | solution.py:389
  135.5 1.0 shard_map.103
  (4 shorter events, 0.1 us)
Async XLA Ops:
  0.6 29.9 %copy-start = (bf16[1536,256]{1,0:T(8,128)(2,1)S(1)}, bf16[1536,256]{1,0:T(8,128)(2,1)}, u32[]{:S(2)}) copy-start(bf16[1536,256]{1,0:T(8,128)(2,1)} %constant.11.clone.sides_ref) | copy-start | bytes 2359300
  2.8 27.8 %copy-start.1 = (f32[2,128,128]{2,1,0:T(8,128)S(1)}, f32[2,128,128]{2,1,0:T(8,128)}, u32[]{:S(2)}) copy-start(f32[2,128,128]{2,1,0:T(8,128)} %constant.9.clone.twist_ref) | copy-start | bytes 393220
  2.8 27.7 %copy-start.2 = (bf16[256,192]{1,0:T(8,128)(2,1)S(1)}, bf16[256,192]{1,0:T(8,128)(2,1)}, u32[]{:S(2)}) copy-start(bf16[256,192]{1,0:T(8,128)(2,1)} %constant.10.clone.window_ref) | copy-start | bytes 294916
  2.8 27.7 %copy-start.3 = (s32[72,128]{1,0:T(8,128)S(1)}, s32[72,128]{1,0:T(8,128)}, u32[]{:S(2)}) copy-start(s32[72,128]{1,0:T(8,128)} %get-tuple-element.12.at_ref) | copy-start | bytes 110596
  65.5 11.6 %copy-start.4 = (f32[2,152,128]{2,1,0:T(8,128)S(1)}, f32[2,152,128]{2,1,0:T(8,128)}, u32[]{:S(2)}) copy-start(f32[2,152,128]{2,1,0:T(8,128)} %constant.8.clone.ring_ref) | copy-start | bytes 466948

commit v7 on v6

--- a/solution.py
+++ b/solution.py
@@ -200,8 +200,8 @@
 
 
 def pack_kernel(
-    strong_hbm, shifts_hbm, widths_hbm, image_hbm, out_hbm, at_hbm,
-    place_ref, strong_ref, shifts_ref, widths_ref, image_ref, tiles_ref, out_ref, at_ref, small_sems, sems, out_sems,
+    strong_hbm, shifts_hbm, widths_hbm, image_hbm, out_ref, at_ref,
+    place_ref, strong_ref, shifts_ref, widths_ref, image_ref, tiles_ref, small_sems, sems,
 ):
     bins = image_ref.shape[1]
     strong = strong_ref.shape[0]
@@ -241,8 +241,6 @@
         line = lax.axis_index(AZ) * 2 + at
         for where, value in enumerate(row_offset(shifts_ref[line]) + (widths_ref[line],)):
             at_ref[4 * at + where : 4 * at + where + 1, :] = jnp.full((1, SIDE), value, jnp.int32)
-    copies = [pltpu.make_async_copy(at_ref, at_hbm, out_sems.at[2])]
-    copies[0].start()
     for part in range(2):
         for at in range(2):
             chunks[part * 2 + at].wait()
@@ -253,15 +251,7 @@
                         part, group * SUB : (group + 1) * SUB, block * SIDE : (block + 1) * SIDE
                     ]
             for row in range(at * half, (at + 1) * half):
-                out_ref[part, places[row] >> 3, places[row] & 3] = tiles_ref[
-                    pl.ds(tile_at(bins, part, row), SUB, stride=SUB), :
-                ]
-        copies.append(
-            pltpu.make_async_copy(out_ref.at[part], out_hbm.at[:, pl.ds(part * 4, 4)], out_sems.at[part])
-        )
-        copies[-1].start()
-    for copy in copies:
-        copy.wait()
+                out_ref[places[row] + part * 4] = tiles_ref[pl.ds(tile_at(bins, part, row), SUB, stride=SUB), :]
 
 
 def unpack_kernel(at_ref, rows_ref, phase_ref, image_hbm, phase_hbm, image_ref, tiles_ref, sems):
@@ -370,17 +360,16 @@
 SMEM = pl.BlockSpec(memory_space=pltpu.SMEM)
 VMEM = pl.BlockSpec(memory_space=pltpu.VMEM)
 HBM = pl.BlockSpec(memory_space=pltpu.HBM)
-PACK_VMEM = 60 * 1024 * 1024
-
-
-def call(kernel, shapes, specs, *operands, scratch=(), out_specs=None, vmem=32 * 1024 * 1024):
+
+
+def call(kernel, shapes, specs, *operands, scratch=(), out_specs=None):
     out = pl.pallas_call(
         kernel,
         out_shape=[jax.ShapeDtypeStruct(*shape) for shape in shapes],
         in_specs=list(specs),
         out_specs=out_specs or [VMEM] * len(shapes),
         scratch_shapes=list(scratch),
-        compiler_params=pltpu.CompilerParams(vmem_limit_bytes=vmem),
+        compiler_params=pltpu.CompilerParams(vmem_limit_bytes=32 * 1024 * 1024),
     )(*operands)
     return out if len(out) > 1 else out[0]
 
@@ -407,27 +396,20 @@
 
     packed, places = call(
         pack_kernel,
-        [((az, 8) + tile, f32), ((SUB + bins, SIDE), i32)],
+        [((az * 8,) + tile, f32), ((SUB + bins, SIDE), i32)],
         [HBM] * 4,
-        strong_index,
-        shifts,
-        widths,
-        sar_image,
+        *(pltpu.with_memory_space_constraint(array, pltpu.HBM) for array in (strong_index, shifts, widths, sar_image)),
         scratch=[pltpu.SMEM((bins,), i32)]
         + [pltpu.SMEM(strong_index.shape, i32) for _ in range(3)]
         + [
             pltpu.VMEM(sar_image.shape, f32),
             moved_tiles,
-            pltpu.VMEM((2, az, 4) + tile, f32),
-            pltpu.VMEM((SUB + bins, SIDE), i32),
             pltpu.SemaphoreType.DMA((3,)),
             pltpu.SemaphoreType.DMA((4,)),
-            pltpu.SemaphoreType.DMA((3,)),
         ],
-        out_specs=[HBM, HBM],
-        vmem=PACK_VMEM,
-    )
-    rows = exchange(packed, AZ)
+        out_specs=[VMEM, VMEM],
+    )
+    rows = exchange(packed.reshape((az, 8) + tile), AZ)
     sums, history = call(
         first_kernel,
         [(sums_shape, f32), ((4, 2, SIDE, SIDE), f32)],

time: 137 us -> 136 us (level)
  no operation moved by 1% of the time
where the time goes in v7:
time: 136 us; the launch traced here: 135 us
  blocking collectives  128 us (94%)
  Pallas kernels  6.73 us (5%)
    all_to_all x8, blocking collectives, exchange(): return lax.all_to_all(array, axes, split_axis=0, concat_axis=0, tiled=True)  128 us
    pallas_call x9, Pallas kernels, call(): pl.pallas_call(kernel, out_shape=[jax.ShapeDtypeStruct(*shape) for shape...  6.73 us

profile of v7, /device:TPU:1, one launch (start us, length us, event | category | flops | bytes accessed | tf_op | source)
XLA Modules:
  0.0 135.4 jit_solution(17586916203754537599)
XLA Ops:
  0.6 0.0 copy-start
  0.6 1.3 shard_map.95
  1.9 0.0 copy-start.1
  2.0 0.0 copy-start.2
  2.0 26.8 %all_to_all.40.rows_ref = f32[16,8,8,128]{3,2,1,0:T(8,128)S(1)} all-to-all(f32[16,8,8,128]{3,2,1,0:T(8,128)S(1)} %bitcast.4), channel_id=1, replica_groups=mesh['zh'=4,'zl'=2,'x'=4,'yh'=4,'yl'=2,'core'=2] {'yh','yl','core'}, dimensions={0} | all-to-all | bytes 1048576 | tf_op jit(solution)/shard_map/all_to_all | solution.py:378
  28.8 0.0 copy-done
  28.8 0.0 copy-done.1
  28.8 0.0 copy-done.2
  28.8 1.3 shard_map.96
  30.0 12.2 %all_to_all.41.in_ref = f32[32,2,4,128]{3,2,1,0:T(4,128)S(1)} all-to-all(f32[32,2,4,128]{3,2,1,0:T(4,128)S(1)} %get-tuple-element.14), channel_id=1, replica_groups=mesh['zh'=4,'zl'=2,'x'=4,'yh'=4,'yl'=2,'core'=2] {'zl','x','yl','core'}, dimensions={0} | all-to-all | bytes 262144 | tf_op jit(solution)/shard_map/all_to_all | solution.py:378
  42.3 22.2 %all_to_all.42.in_ref = f32[16,2,4,128]{3,2,1,0:T(4,128)S(1)} all-to-all(f32[16,2,4,128]{3,2,1,0:T(4,128)S(1)} %shard_map.97), channel_id=1, replica_groups=mesh['zh'=4,'zl'=2,'x'=4,'yh'=4,'yl'=2,'core'=2] {'zh','yh'}, dimensions={0} | all-to-all | bytes 131072 | tf_op jit(solution)/shard_map/all_to_all | solution.py:378
  64.4 0.0 copy-start.3
  64.5 11.6 %all_to_all.43.gradient_ref = f32[32,4,128]{2,1,0:T(4,128)S(1)} all-to-all(f32[32,4,128]{2,1,0:T(4,128)S(1)} %shard_map.98), channel_id=1, replica_groups=mesh['zh'=4,'zl'=2,'x'=4,'yh'=4,'yl'=2,'core'=2] {'zl','x','yl','core'}, dimensions={0} | all-to-all | bytes 131072 | tf_op jit(solution)/shard_map/all_to_all | solution.py:378
  76.0 0.0 copy-done.3
  76.0 1.8 %shard_map.99 = (f32[32,2,4,128]{3,2,1,0:T(4,128)S(1)}, f32[128,128]{1,0:T(8,128)S(1)}) custom-call(s32[72,128]{1,0:T(8,128)S(1)} %get-tuple-element.12.at_ref, f32[32,4,128]{2,1,0:T(4,128)S(1)} %all_to_all.43.gradient_ref, f32[4,2,128,128]{3,2,1,0:T(8,128)S(1)} %get-tuple-element.15.history_ref, bf16[256,192]{1,0:T(8,128)(2,1)S(1)} %copy-done.2, ...), custom_call_target="tpu_custom_call" | custom-call | tf_op jit(solution)/shard_map/pallas_call | solution.py:366
  77.9 10.1 %all_to_all.44.in_ref = f32[32,2,4,128]{3,2,1,0:T(4,128)S(1)} all-to-all(f32[32,2,4,128]{3,2,1,0:T(4,128)S(1)} %get-tuple-element.16), channel_id=1, replica_groups=mesh['zh'=4,'zl'=2,'x'=4,'yh'=4,'yl'=2,'core'=2] {'zl','x','yl','core'}, dimensions={0} | all-to-all | bytes 262144 | tf_op jit(solution)/shard_map/all_to_all | solution.py:378
  88.0 13.9 %all_to_all.45.in_ref = f32[16,2,4,128]{3,2,1,0:T(4,128)S(1)} all-to-all(f32[16,2,4,128]{3,2,1,0:T(4,128)S(1)} %shard_map.100), channel_id=1, replica_groups=mesh['zh'=4,'zl'=2,'x'=4,'yh'=4,'yl'=2,'core'=2] {'zh','yh'}, dimensions={0} | all-to-all | bytes 131072 | tf_op jit(solution)/shard_map/all_to_all | solution.py:378
  101.9 11.2 %all_to_all.46.gradient_ref = f32[32,4,128]{2,1,0:T(4,128)S(1)} all-to-all(f32[32,4,128]{2,1,0:T(4,128)S(1)} %shard_map.101), channel_id=1, replica_groups=mesh['zh'=4,'zl'=2,'x'=4,'yh'=4,'yl'=2,'core'=2] {'zl','x','yl','core'}, dimensions={0} | all-to-all | bytes 131072 | tf_op jit(solution)/shard_map/all_to_all | solution.py:378
  113.0 1.3 shard_map.102
  114.3 20.2 %all_to_all.47 = f32[16,8,8,128]{3,2,1,0:T(8,128)S(1)} all-to-all(f32[16,8,8,128]{3,2,1,0:T(8,128)S(1)} %get-tuple-element.18), channel_id=1, replica_groups=mesh['zh'=4,'zl'=2,'x'=4,'yh'=4,'yl'=2,'core'=2] {'yh','yl','core'}, dimensions={0} | all-to-all | bytes 1048576 | tf_op jit(solution)/shard_map/all_to_all | solution.py:378
  134.4 1.0 shard_map.103
  (4 shorter events, 0.1 us)
Async XLA Ops:
  0.6 28.1 %copy-start = (bf16[1536,256]{1,0:T(8,128)(2,1)S(1)}, bf16[1536,256]{1,0:T(8,128)(2,1)}, u32[]{:S(2)}) copy-start(bf16[1536,256]{1,0:T(8,128)(2,1)} %constant.11.clone.sides_ref) | copy-start | bytes 2359300
  1.9 26.8 %copy-start.1 = (f32[2,128,128]{2,1,0:T(8,128)S(1)}, f32[2,128,128]{2,1,0:T(8,128)}, u32[]{:S(2)}) copy-start(f32[2,128,128]{2,1,0:T(8,128)} %constant.9.clone.twist_ref) | copy-start | bytes 393220
  2.0 26.8 %copy-start.2 = (bf16[256,192]{1,0:T(8,128)(2,1)S(1)}, bf16[256,192]{1,0:T(8,128)(2,1)}, u32[]{:S(2)}) copy-start(bf16[256,192]{1,0:T(8,128)(2,1)} %constant.10.clone.window_ref) | copy-start | bytes 294916
  64.4 11.6 %copy-start.3 = (f32[2,152,128]{2,1,0:T(8,128)S(1)}, f32[2,152,128]{2,1,0:T(8,128)}, u32[]{:S(2)}) copy-start(f32[2,152,128]{2,1,0:T(8,128)} %constant.8.clone.ring_ref) | copy-start | bytes 466948

commit v8 on v7

--- a/solution.py
+++ b/solution.py
@@ -201,21 +201,18 @@
 
 def pack_kernel(
     strong_hbm, shifts_hbm, widths_hbm, image_hbm, out_ref, at_ref,
-    place_ref, strong_ref, shifts_ref, widths_ref, image_ref, tiles_ref, small_sems, sems,
+    place_ref, strong_ref, shifts_ref, widths_ref, tiles_ref, small_sems, sems,
 ):
-    bins = image_ref.shape[1]
+    bins = image_hbm.shape[0] // (2 * SUB)
     strong = strong_ref.shape[0]
-    half = bins // 2
     indices = pltpu.make_async_copy(strong_hbm, strong_ref, small_sems.at[0])
     indices.start()
-    chunks = []
-    for part in range(2):
-        for at in range(2):
-            span = slice(at * half, (at + 1) * half)
-            chunks.append(
-                pltpu.make_async_copy(image_hbm.at[part, span], image_ref.at[part, span], sems.at[part * 2 + at])
-            )
-            chunks[-1].start()
+    parts = [
+        pltpu.make_async_copy(image_hbm.at[pl.ds(part * SUB * bins, SUB * bins)], tiles_ref.at[pl.ds(part * SUB * bins, SUB * bins)], sems.at[part])
+        for part in range(2)
+    ]
+    for copy in parts:
+        copy.start()
     others_in = [
         pltpu.make_async_copy(shifts_hbm, shifts_ref, small_sems.at[1]),
         pltpu.make_async_copy(widths_hbm, widths_ref, small_sems.at[2]),
@@ -228,60 +225,41 @@
     for at in range(strong):
         place_ref[strong_ref[at] & (bins - 1)] = at // 2 * 8 + at % 2
     others = jnp.int32(0)
-    places = []
     for row in range(bins):
         held = place_ref[row]
         place = jnp.where(held < 0, ((others >> 1) << 3) + (others & 1) + 2, held)
-        others = others + jnp.where(held < 0, 1, 0)
-        places.append(place)
-        at_ref[SUB + row : SUB + row + 1, :] = jnp.full((1, SIDE), place, jnp.int32)
+        others = others + (held < 0).astype(jnp.int32)
+        at_ref[SUB + row] = place
     for copy in others_in:
         copy.wait()
     for at in range(2):
         line = lax.axis_index(AZ) * 2 + at
         for where, value in enumerate(row_offset(shifts_ref[line]) + (widths_ref[line],)):
-            at_ref[4 * at + where : 4 * at + where + 1, :] = jnp.full((1, SIDE), value, jnp.int32)
+            at_ref[4 * at + where] = value
     for part in range(2):
-        for at in range(2):
-            chunks[part * 2 + at].wait()
-            for group in range(at * half // SUB, (at + 1) * half // SUB):
-                for block in range(SUB):
-                    tile = ((part * (bins // SUB) + group) * SUB + block) * SUB
-                    tiles_ref[tile : tile + SUB, :] = image_ref[
-                        part, group * SUB : (group + 1) * SUB, block * SIDE : (block + 1) * SIDE
-                    ]
-            for row in range(at * half, (at + 1) * half):
-                out_ref[places[row] + part * 4] = tiles_ref[pl.ds(tile_at(bins, part, row), SUB, stride=SUB), :]
-
-
-def unpack_kernel(at_ref, rows_ref, phase_ref, image_hbm, phase_hbm, image_ref, tiles_ref, sems):
-    bins = image_ref.shape[1]
+        parts[part].wait()
+        for row in range(bins):
+            out_ref[at_ref[SUB + row] + part * 4] = tiles_ref[pl.ds(tile_at(bins, part, row), SUB, stride=SUB), :]
+
+
+def unpack_kernel(at_ref, rows_ref, phase_ref, image_hbm, phase_hbm, tiles_ref, sems):
+    bins = image_hbm.shape[0] // (2 * SUB)
     copies = [pltpu.make_async_copy(phase_ref, phase_hbm, sems.at[4])]
     copies[0].start()
-    places = [at_ref[SUB + row, 0] for row in range(bins)]
+    places = [at_ref[SUB + row] for row in range(bins)]
     for part in range(2):
-        for row in range(bins):
-            tiles_ref[pl.ds(tile_at(bins, part, row), SUB, stride=SUB), :] = rows_ref[places[row] + part * 4]
         for half in range(2):
-            span = slice(half * bins // 2, (half + 1) * bins // 2)
-            for group in range(half * bins // 2 // SUB, (half + 1) * bins // 2 // SUB):
-                for block in range(SUB):
-                    at = ((part * (bins // SUB) + group) * SUB + block) * SUB
-                    image_ref[part, group * SUB : (group + 1) * SUB, block * SIDE : (block + 1) * SIDE] = tiles_ref[
-                        at : at + SUB, :
-                    ]
-            copies.append(
-                pltpu.make_async_copy(
-                    image_ref.at[part, span], image_hbm.at[part, span], sems.at[part * 2 + half]
-                )
-            )
+            for row in range(half * bins // 2, (half + 1) * bins // 2):
+                tiles_ref[pl.ds(tile_at(bins, part, row), SUB, stride=SUB), :] = rows_ref[places[row] + part * 4]
+            span = pl.ds((part * 2 + half) * SUB * bins // 2, SUB * bins // 2)
+            copies.append(pltpu.make_async_copy(tiles_ref.at[span], image_hbm.at[span], sems.at[part * 2 + half]))
             copies[-1].start()
     for copy in copies:
         copy.wait()
 
 
 def offsets(at_ref, line):
-    return [at_ref[4 * line + where, 0] for where in range(3)]
+    return [at_ref[4 * line + where] for where in range(3)]
 
 
 def first_kernel(
@@ -365,7 +343,7 @@
 def call(kernel, shapes, specs, *operands, scratch=(), out_specs=None):
     out = pl.pallas_call(
         kernel,
-        out_shape=[jax.ShapeDtypeStruct(*shape) for shape in shapes],
+        out_shape=[shape if isinstance(shape, pl.MemoryRef) else jax.ShapeDtypeStruct(*shape) for shape in shapes],
         in_specs=list(specs),
         out_specs=out_specs or [VMEM] * len(shapes),
         scratch_shapes=list(scratch),
@@ -390,30 +368,32 @@
     bins, pulses_local = sar_image.shape[1:]
     table = tables()
     tile = (SUB, SIDE)
+    tiles = (2, bins // SUB, SUB, pulses_local // SIDE, SIDE)
+    image = sar_image.reshape(tiles).transpose(0, 1, 3, 2, 4).reshape(2 * bins * SUB, SIDE)
     part = SIDE // near
     sums_shape = (near, 2, part, SIDE)
     moved_tiles = pltpu.VMEM((2 * bins * SUB, SIDE), f32)
 
     packed, places = call(
         pack_kernel,
-        [((az * 8,) + tile, f32), ((SUB + bins, SIDE), i32)],
+        [((az * 8,) + tile, f32), pltpu.SMEM((SUB + bins,), i32)],
         [HBM] * 4,
-        *(pltpu.with_memory_space_constraint(array, pltpu.HBM) for array in (strong_index, shifts, widths, sar_image)),
+        *(pltpu.with_memory_space_constraint(array, pltpu.HBM) for array in (strong_index, shifts, widths, image)),
         scratch=[pltpu.SMEM((bins,), i32)]
         + [pltpu.SMEM(strong_index.shape, i32) for _ in range(3)]
         + [
-            pltpu.VMEM(sar_image.shape, f32),
             moved_tiles,
             pltpu.SemaphoreType.DMA((3,)),
-            pltpu.SemaphoreType.DMA((4,)),
+            pltpu.SemaphoreType.DMA((2,)),
         ],
-        out_specs=[VMEM, VMEM],
-    )
+        out_specs=[VMEM, SMEM],
+    )
+    places = pltpu.with_memory_space_constraint(places, pltpu.SMEM)
     rows = exchange(packed.reshape((az, 8) + tile), AZ)
     sums, history = call(
         first_kernel,
         [(sums_shape, f32), ((4, 2, SIDE, SIDE), f32)],
-        [VMEM] * 5,
+        [SMEM] + [VMEM] * 4,
         places,
         rows,
         table["window"],
@@ -433,7 +413,7 @@
     sums, total = call(
         second_kernel,
         [(sums_shape, f32), ((SIDE, SIDE), f32)],
-        [VMEM] * 7,
+        [SMEM] + [VMEM] * 6,
         places,
         gradient,
         history,
@@ -458,15 +438,16 @@
     returned = exchange(corrected, AZ)
     focused, phase = call(
         unpack_kernel,
-        [(sar_image.shape, f32), (tile, f32)],
-        [VMEM, VMEM, VMEM],
+        [(image.shape, f32), (tile, f32)],
+        [SMEM, VMEM, VMEM],
         places,
         returned.reshape((az * 8,) + tile),
         phase,
-        scratch=[pltpu.VMEM(sar_image.shape, f32), moved_tiles, pltpu.SemaphoreType.DMA((5,))],
+        scratch=[moved_tiles, pltpu.SemaphoreType.DMA((5,))],
         out_specs=[HBM, HBM],
     )
-    return focused, phase.reshape(pulses_local)
+    focused = focused.reshape(2, bins // SUB, pulses_local // SIDE, SUB, SIDE).transpose(0, 1, 3, 2, 4)
+    return focused.reshape(sar_image.shape), phase.reshape(pulses_local)
 
 
 def solution(mesh):

time: 136 us -> 136 us (level)
  no operation moved by 1% of the time
where the time goes in v8:
time: 136 us; the launch traced here: 135 us
  blocking collectives  128 us (94%)
  Pallas kernels  6.65 us (5%)
    all_to_all x8, blocking collectives, exchange(): return lax.all_to_all(array, axes, split_axis=0, concat_axis=0, tiled=True)  128 us
    pallas_call x9, Pallas kernels, call(): pl.pallas_call(kernel, out_shape=[shape if isinstance(shape, pl.MemoryRef...  6.65 us

profile of v8, /device:TPU:1, one launch (start us, length us, event | category | flops | bytes accessed | tf_op | source)
XLA Modules:
  0.0 135.3 jit_solution(13619084776369342404)
XLA Ops:
  0.6 0.0 copy-start
  0.6 1.3 shard_map.95
  2.0 0.0 copy-start.1
  2.0 0.0 copy-start.2
  2.0 26.8 %all_to_all.40.rows_ref = f32[16,8,8,128]{3,2,1,0:T(8,128)S(1)} all-to-all(f32[16,8,8,128]{3,2,1,0:T(8,128)S(1)} %bitcast.14), channel_id=1, replica_groups=mesh['zh'=4,'zl'=2,'x'=4,'yh'=4,'yl'=2,'core'=2] {'yh','yl','core'}, dimensions={0} | all-to-all | bytes 1048576 | tf_op jit(solution)/shard_map/all_to_all | solution.py:356
  28.8 0.0 copy-done
  28.8 0.0 copy-done.1
  28.8 0.0 copy-done.2
  28.8 1.2 shard_map.96
  30.0 12.2 %all_to_all.41.in_ref = f32[32,2,4,128]{3,2,1,0:T(4,128)S(1)} all-to-all(f32[32,2,4,128]{3,2,1,0:T(4,128)S(1)} %get-tuple-element.14), channel_id=1, replica_groups=mesh['zh'=4,'zl'=2,'x'=4,'yh'=4,'yl'=2,'core'=2] {'zl','x','yl','core'}, dimensions={0} | all-to-all | bytes 262144 | tf_op jit(solution)/shard_map/all_to_all | solution.py:356
  42.3 22.2 %all_to_all.42.in_ref = f32[16,2,4,128]{3,2,1,0:T(4,128)S(1)} all-to-all(f32[16,2,4,128]{3,2,1,0:T(4,128)S(1)} %shard_map.97), channel_id=1, replica_groups=mesh['zh'=4,'zl'=2,'x'=4,'yh'=4,'yl'=2,'core'=2] {'zh','yh'}, dimensions={0} | all-to-all | bytes 131072 | tf_op jit(solution)/shard_map/all_to_all | solution.py:356
  64.4 0.0 copy-start.3
  64.5 11.6 %all_to_all.43.gradient_ref = f32[32,4,128]{2,1,0:T(4,128)S(1)} all-to-all(f32[32,4,128]{2,1,0:T(4,128)S(1)} %shard_map.98), channel_id=1, replica_groups=mesh['zh'=4,'zl'=2,'x'=4,'yh'=4,'yl'=2,'core'=2] {'zl','x','yl','core'}, dimensions={0} | all-to-all | bytes 131072 | tf_op jit(solution)/shard_map/all_to_all | solution.py:356
  76.0 0.0 copy-done.3
  76.0 1.8 %shard_map.99 = (f32[32,2,4,128]{3,2,1,0:T(4,128)S(1)}, f32[128,128]{1,0:T(8,128)S(1)}) custom-call(s32[72]{0:T(128)S(4)} %get-tuple-element.12.at_ref, f32[32,4,128]{2,1,0:T(4,128)S(1)} %all_to_all.43.gradient_ref, f32[4,2,128,128]{3,2,1,0:T(8,128)S(1)} %get-tuple-element.15.history_ref, bf16[256,192]{1,0:T(8,128)(2,1)S(1)} %copy-done.2, ...), custom_call_target="tpu_custom_call" | custom-call | tf_op jit(solution)/shard_map/pallas_call | solution.py:344
  77.8 10.1 %all_to_all.44.in_ref = f32[32,2,4,128]{3,2,1,0:T(4,128)S(1)} all-to-all(f32[32,2,4,128]{3,2,1,0:T(4,128)S(1)} %get-tuple-element.16), channel_id=1, replica_groups=mesh['zh'=4,'zl'=2,'x'=4,'yh'=4,'yl'=2,'core'=2] {'zl','x','yl','core'}, dimensions={0} | all-to-all | bytes 262144 | tf_op jit(solution)/shard_map/all_to_all | solution.py:356
  87.9 13.9 %all_to_all.45.in_ref = f32[16,2,4,128]{3,2,1,0:T(4,128)S(1)} all-to-all(f32[16,2,4,128]{3,2,1,0:T(4,128)S(1)} %shard_map.100), channel_id=1, replica_groups=mesh['zh'=4,'zl'=2,'x'=4,'yh'=4,'yl'=2,'core'=2] {'zh','yh'}, dimensions={0} | all-to-all | bytes 131072 | tf_op jit(solution)/shard_map/all_to_all | solution.py:356
  101.8 11.2 %all_to_all.46.gradient_ref = f32[32,4,128]{2,1,0:T(4,128)S(1)} all-to-all(f32[32,4,128]{2,1,0:T(4,128)S(1)} %shard_map.101), channel_id=1, replica_groups=mesh['zh'=4,'zl'=2,'x'=4,'yh'=4,'yl'=2,'core'=2] {'zl','x','yl','core'}, dimensions={0} | all-to-all | bytes 131072 | tf_op jit(solution)/shard_map/all_to_all | solution.py:356
  113.0 1.3 shard_map.102
  114.2 20.2 %all_to_all.47 = f32[16,8,8,128]{3,2,1,0:T(8,128)S(1)} all-to-all(f32[16,8,8,128]{3,2,1,0:T(8,128)S(1)} %get-tuple-element.18), channel_id=1, replica_groups=mesh['zh'=4,'zl'=2,'x'=4,'yh'=4,'yl'=2,'core'=2] {'yh','yl','core'}, dimensions={0} | all-to-all | bytes 1048576 | tf_op jit(solution)/shard_map/all_to_all | solution.py:356
  134.4 0.9 shard_map.103
  (4 shorter events, 0.1 us)
Async XLA Ops:
  0.6 28.2 %copy-start = (bf16[1536,256]{1,0:T(8,128)(2,1)S(1)}, bf16[1536,256]{1,0:T(8,128)(2,1)}, u32[]{:S(2)}) copy-start(bf16[1536,256]{1,0:T(8,128)(2,1)} %constant.11.clone.sides_ref) | copy-start | bytes 2359300
  2.0 26.8 %copy-start.1 = (f32[2,128,128]{2,1,0:T(8,128)S(1)}, f32[2,128,128]{2,1,0:T(8,128)}, u32[]{:S(2)}) copy-start(f32[2,128,128]{2,1,0:T(8,128)} %constant.9.clone.twist_ref) | copy-start | bytes 393220
  2.0 26.8 %copy-start.2 = (bf16[256,192]{1,0:T(8,128)(2,1)S(1)}, bf16[256,192]{1,0:T(8,128)(2,1)}, u32[]{:S(2)}) copy-start(bf16[256,192]{1,0:T(8,128)(2,1)} %constant.10.clone.window_ref) | copy-start | bytes 294916
  64.4 11.6 %copy-start.3 = (f32[2,152,128]{2,1,0:T(8,128)S(1)}, f32[2,152,128]{2,1,0:T(8,128)}, u32[]{:S(2)}) copy-start(f32[2,152,128]{2,1,0:T(8,128)} %constant.8.clone.ring_ref) | copy-start | bytes 466948

commit v9 on v8

--- a/solution.py
+++ b/solution.py
@@ -183,7 +183,8 @@
 
     def before(part):
         down = pltpu.roll(part, 1, 0)
-        return jnp.where(rows == 0, pltpu.roll(down, 1, 1), down)
+        top = jnp.where(rows[:SUB] == 0, pltpu.roll(down[:SUB], 1, 1), down[:SUB])
+        return jnp.concatenate([top, down[SUB:]], axis=0)
 
     for real, imag in lines:
         numerator = numerator + (before(real) * imag - before(imag) * real)
@@ -225,28 +226,30 @@
     for at in range(strong):
         place_ref[strong_ref[at] & (bins - 1)] = at // 2 * 8 + at % 2
     others = jnp.int32(0)
+    places = []
     for row in range(bins):
         held = place_ref[row]
         place = jnp.where(held < 0, ((others >> 1) << 3) + (others & 1) + 2, held)
-        others = others + (held < 0).astype(jnp.int32)
-        at_ref[SUB + row] = place
+        others = others + jnp.where(held < 0, 1, 0)
+        places.append(place)
+        at_ref[SUB + row : SUB + row + 1, :] = jnp.full((1, SIDE), place, jnp.int32)
     for copy in others_in:
         copy.wait()
     for at in range(2):
         line = lax.axis_index(AZ) * 2 + at
         for where, value in enumerate(row_offset(shifts_ref[line]) + (widths_ref[line],)):
-            at_ref[4 * at + where] = value
+            at_ref[4 * at + where : 4 * at + where + 1, :] = jnp.full((1, SIDE), value, jnp.int32)
     for part in range(2):
         parts[part].wait()
         for row in range(bins):
-            out_ref[at_ref[SUB + row] + part * 4] = tiles_ref[pl.ds(tile_at(bins, part, row), SUB, stride=SUB), :]
+            out_ref[places[row] + part * 4] = tiles_ref[pl.ds(tile_at(bins, part, row), SUB, stride=SUB), :]
 
 
 def unpack_kernel(at_ref, rows_ref, phase_ref, image_hbm, phase_hbm, tiles_ref, sems):
     bins = image_hbm.shape[0] // (2 * SUB)
     copies = [pltpu.make_async_copy(phase_ref, phase_hbm, sems.at[4])]
     copies[0].start()
-    places = [at_ref[SUB + row] for row in range(bins)]
+    places = [at_ref[SUB + row, 0] for row in range(bins)]
     for part in range(2):
         for half in range(2):
             for row in range(half * bins // 2, (half + 1) * bins // 2):
@@ -259,7 +262,7 @@
 
 
 def offsets(at_ref, line):
-    return [at_ref[4 * line + where] for where in range(3)]
+    return [at_ref[4 * line + where, 0] for where in range(3)]
 
 
 def first_kernel(
@@ -343,7 +346,7 @@
 def call(kernel, shapes, specs, *operands, scratch=(), out_specs=None):
     out = pl.pallas_call(
         kernel,
-        out_shape=[shape if isinstance(shape, pl.MemoryRef) else jax.ShapeDtypeStruct(*shape) for shape in shapes],
+        out_shape=[jax.ShapeDtypeStruct(*shape) for shape in shapes],
         in_specs=list(specs),
         out_specs=out_specs or [VMEM] * len(shapes),
         scratch_shapes=list(scratch),
@@ -376,7 +379,7 @@
 
     packed, places = call(
         pack_kernel,
-        [((az * 8,) + tile, f32), pltpu.SMEM((SUB + bins,), i32)],
+        [((az * 8,) + tile, f32), ((SUB + bins, SIDE), i32)],
         [HBM] * 4,
         *(pltpu.with_memory_space_constraint(array, pltpu.HBM) for array in (strong_index, shifts, widths, image)),
         scratch=[pltpu.SMEM((bins,), i32)]
@@ -386,14 +389,13 @@
             pltpu.SemaphoreType.DMA((3,)),
             pltpu.SemaphoreType.DMA((2,)),
         ],
-        out_specs=[VMEM, SMEM],
-    )
-    places = pltpu.with_memory_space_constraint(places, pltpu.SMEM)
+        out_specs=[VMEM, VMEM],
+    )
     rows = exchange(packed.reshape((az, 8) + tile), AZ)
     sums, history = call(
         first_kernel,
         [(sums_shape, f32), ((4, 2, SIDE, SIDE), f32)],
-        [SMEM] + [VMEM] * 4,
+        [VMEM] * 5,
         places,
         rows,
         table["window"],
@@ -413,7 +415,7 @@
     sums, total = call(
         second_kernel,
         [(sums_shape, f32), ((SIDE, SIDE), f32)],
-        [SMEM] + [VMEM] * 6,
+        [VMEM] * 7,
         places,
         gradient,
         history,
@@ -439,7 +441,7 @@
     focused, phase = call(
         unpack_kernel,
         [(image.shape, f32), (tile, f32)],
-        [SMEM, VMEM, VMEM],
+        [VMEM, VMEM, VMEM],
         places,
         returned.reshape((az * 8,) + tile),
         phase,

time: 136 us -> 136 us (level)
  no operation moved by 1% of the time
where the time goes in v9:
time: 136 us; the launch traced here: 135 us
  blocking collectives  128 us (94%)
  Pallas kernels  6.68 us (5%)
    all_to_all x8, blocking collectives, exchange(): return lax.all_to_all(array, axes, split_axis=0, concat_axis=0, tiled=True)  128 us
    pallas_call x9, Pallas kernels, call(): pl.pallas_call(kernel, out_shape=[jax.ShapeDtypeStruct(*shape) for shape...  6.68 us

profile of v9, /device:TPU:1, one launch (start us, length us, event | category | flops | bytes accessed | tf_op | source)
XLA Modules:
  0.0 135.3 jit_solution(6545950283213597306)
XLA Ops:
  0.6 0.0 copy-start
  0.6 1.2 shard_map.95
  1.9 0.0 copy-start.1
  1.9 0.0 copy-start.2
  1.9 26.8 %all_to_all.40.rows_ref = f32[16,8,8,128]{3,2,1,0:T(8,128)S(1)} all-to-all(f32[16,8,8,128]{3,2,1,0:T(8,128)S(1)} %bitcast.14), channel_id=1, replica_groups=mesh['zh'=4,'zl'=2,'x'=4,'yh'=4,'yl'=2,'core'=2] {'yh','yl','core'}, dimensions={0} | all-to-all | bytes 1048576 | tf_op jit(solution)/shard_map/all_to_all | solution.py:359
  28.7 0.0 copy-done
  28.7 0.0 copy-done.1
  28.7 0.0 copy-done.2
  28.7 1.3 shard_map.96
  30.0 12.2 %all_to_all.41.in_ref = f32[32,2,4,128]{3,2,1,0:T(4,128)S(1)} all-to-all(f32[32,2,4,128]{3,2,1,0:T(4,128)S(1)} %get-tuple-element.14), channel_id=1, replica_groups=mesh['zh'=4,'zl'=2,'x'=4,'yh'=4,'yl'=2,'core'=2] {'zl','x','yl','core'}, dimensions={0} | all-to-all | bytes 262144 | tf_op jit(solution)/shard_map/all_to_all | solution.py:359
  42.2 22.2 %all_to_all.42.in_ref = f32[16,2,4,128]{3,2,1,0:T(4,128)S(1)} all-to-all(f32[16,2,4,128]{3,2,1,0:T(4,128)S(1)} %shard_map.97), channel_id=1, replica_groups=mesh['zh'=4,'zl'=2,'x'=4,'yh'=4,'yl'=2,'core'=2] {'zh','yh'}, dimensions={0} | all-to-all | bytes 131072 | tf_op jit(solution)/shard_map/all_to_all | solution.py:359
  64.4 0.0 copy-start.3
  64.4 11.6 %all_to_all.43.gradient_ref = f32[32,4,128]{2,1,0:T(4,128)S(1)} all-to-all(f32[32,4,128]{2,1,0:T(4,128)S(1)} %shard_map.98), channel_id=1, replica_groups=mesh['zh'=4,'zl'=2,'x'=4,'yh'=4,'yl'=2,'core'=2] {'zl','x','yl','core'}, dimensions={0} | all-to-all | bytes 131072 | tf_op jit(solution)/shard_map/all_to_all | solution.py:359
  76.0 0.0 copy-done.3
  76.0 1.8 %shard_map.99 = (f32[32,2,4,128]{3,2,1,0:T(4,128)S(1)}, f32[128,128]{1,0:T(8,128)S(1)}) custom-call(s32[72,128]{1,0:T(8,128)S(1)} %get-tuple-element.12.at_ref, f32[32,4,128]{2,1,0:T(4,128)S(1)} %all_to_all.43.gradient_ref, f32[4,2,128,128]{3,2,1,0:T(8,128)S(1)} %get-tuple-element.15.history_ref, bf16[256,192]{1,0:T(8,128)(2,1)S(1)} %copy-done.2, ...), custom_call_target="tpu_custom_call" | custom-call | tf_op jit(solution)/shard_map/pallas_call | solution.py:347
  77.8 10.1 %all_to_all.44.in_ref = f32[32,2,4,128]{3,2,1,0:T(4,128)S(1)} all-to-all(f32[32,2,4,128]{3,2,1,0:T(4,128)S(1)} %get-tuple-element.16), channel_id=1, replica_groups=mesh['zh'=4,'zl'=2,'x'=4,'yh'=4,'yl'=2,'core'=2] {'zl','x','yl','core'}, dimensions={0} | all-to-all | bytes 262144 | tf_op jit(solution)/shard_map/all_to_all | solution.py:359
  87.9 13.9 %all_to_all.45.in_ref = f32[16,2,4,128]{3,2,1,0:T(4,128)S(1)} all-to-all(f32[16,2,4,128]{3,2,1,0:T(4,128)S(1)} %shard_map.100), channel_id=1, replica_groups=mesh['zh'=4,'zl'=2,'x'=4,'yh'=4,'yl'=2,'core'=2] {'zh','yh'}, dimensions={0} | all-to-all | bytes 131072 | tf_op jit(solution)/shard_map/all_to_all | solution.py:359
  101.8 11.2 %all_to_all.46.gradient_ref = f32[32,4,128]{2,1,0:T(4,128)S(1)} all-to-all(f32[32,4,128]{2,1,0:T(4,128)S(1)} %shard_map.101), channel_id=1, replica_groups=mesh['zh'=4,'zl'=2,'x'=4,'yh'=4,'yl'=2,'core'=2] {'zl','x','yl','core'}, dimensions={0} | all-to-all | bytes 131072 | tf_op jit(solution)/shard_map/all_to_all | solution.py:359
  113.0 1.3 shard_map.102
  114.2 20.2 %all_to_all.47 = f32[16,8,8,128]{3,2,1,0:T(8,128)S(1)} all-to-all(f32[16,8,8,128]{3,2,1,0:T(8,128)S(1)} %get-tuple-element.18), channel_id=1, replica_groups=mesh['zh'=4,'zl'=2,'x'=4,'yh'=4,'yl'=2,'core'=2] {'yh','yl','core'}, dimensions={0} | all-to-all | bytes 1048576 | tf_op jit(solution)/shard_map/all_to_all | solution.py:359
  134.4 0.9 shard_map.103
  (4 shorter events, 0.1 us)
Async XLA Ops:
  0.6 28.1 %copy-start = (bf16[1536,256]{1,0:T(8,128)(2,1)S(1)}, bf16[1536,256]{1,0:T(8,128)(2,1)}, u32[]{:S(2)}) copy-start(bf16[1536,256]{1,0:T(8,128)(2,1)} %constant.11.clone.sides_ref) | copy-start | bytes 2359300
  1.9 26.8 %copy-start.1 = (f32[2,128,128]{2,1,0:T(8,128)S(1)}, f32[2,128,128]{2,1,0:T(8,128)}, u32[]{:S(2)}) copy-start(f32[2,128,128]{2,1,0:T(8,128)} %constant.9.clone.twist_ref) | copy-start | bytes 393220
  1.9 26.8 %copy-start.2 = (bf16[256,192]{1,0:T(8,128)(2,1)S(1)}, bf16[256,192]{1,0:T(8,128)(2,1)}, u32[]{:S(2)}) copy-start(bf16[256,192]{1,0:T(8,128)(2,1)} %constant.10.clone.window_ref) | copy-start | bytes 294916
  64.4 11.6 %copy-start.3 = (f32[2,152,128]{2,1,0:T(8,128)S(1)}, f32[2,152,128]{2,1,0:T(8,128)}, u32[]{:S(2)}) copy-start(f32[2,152,128]{2,1,0:T(8,128)} %constant.8.clone.ring_ref) | copy-start | bytes 466948

commit v10 on v9

--- a/solution.py
+++ b/solution.py
@@ -80,7 +80,7 @@
     return dot(left, jnp.concatenate([first, second, first, third, second, first], axis=0))
 
 
-def forward(lines, first_stage, sides_ref, twist_ref, count=3):
+def forward_start(lines, first_stage, twist_ref):
     cosine, sine = twist_ref[0], twist_ref[1]
     first = first_stage(jnp.concatenate([jnp.concatenate(line, axis=0) for line in lines], axis=1))
     turned = []
@@ -88,11 +88,30 @@
         real = first[:SIDE, at * SIDE : (at + 1) * SIDE]
         imag = first[SIDE:, at * SIDE : (at + 1) * SIDE]
         turned.append(jnp.concatenate([real * cosine + imag * sine, imag * cosine - real * sine], axis=1))
-    second = multiply(stack(jnp.concatenate(turned, axis=0), count), parts_of(sides_ref, RIGHT, count))
-    return [
-        (second[at * SIDE : (at + 1) * SIDE, :SIDE], second[at * SIDE : (at + 1) * SIDE, SIDE:])
-        for at in range(len(lines))
-    ]
+    return jnp.concatenate(turned, axis=0)
+
+
+def forward_end(started, sides_ref):
+    parts = [split(lines, count) for lines, count in started]
+    totals = [[] for _ in started]
+    for at, right in enumerate(parts_of(sides_ref, RIGHT)):
+        used = [(group, part) for group in range(len(started)) for part in range(started[group][1] - at)]
+        product = dot(jnp.concatenate([parts[group][part] for group, part in used], axis=0), right)
+        begin = 0
+        for group, part in used:
+            rows = started[group][0].shape[0]
+            totals[group].append((at + part, product[begin : begin + rows]))
+            begin += rows
+    found = []
+    for terms in totals:
+        terms = [term for _, term in sorted(terms, key=lambda pair: -pair[0])]
+        total = terms[0]
+        for term in terms[1:]:
+            total = total + term
+        found.append(
+            [(total[at : at + SIDE, :SIDE], total[at : at + SIDE, SIDE:]) for at in range(0, total.shape[0], SIDE)]
+        )
+    return found
 
 
 def inverse_start(lines, sides_ref, twist_ref, count=3):
@@ -278,11 +297,14 @@
             ring[SIDE:, :] = rows_ref[: LOAD // SUB, part * 4 + at].reshape(LOAD, SIDE)
             parts.append(center(ring[pl.ds(row, WINDOW), :], ring[pl.ds(row + 1, WINDOW), :], lane, width))
         lines.append(parts)
-    gradient_sums(forward(lines, lambda lines: multiply_window(window_ref[...], lines), sides_ref, twist_ref), out_ref)
+    started = [(forward_start(lines, lambda lines: multiply_window(window_ref[...], lines), twist_ref), 3)]
     for begin, count in ((0, 3), (2, 2)):
         lines = [[square(rows_ref, part * 4 + begin + at) for part in range(2)] for at in range(2)]
         whole = stacked_of(sides_ref, RIGHT_T, count)
-        spectra = forward(lines, lambda lines: multiply(whole, split(lines, count)), sides_ref, twist_ref, count)
+        started.append((forward_start(lines, lambda lines: multiply(whole, split(lines, count)), twist_ref), count))
+    windowed, *history = forward_end(started, sides_ref)
+    gradient_sums(windowed, out_ref)
+    for begin, spectra in zip((0, 2), history):
         for at in range(2):
             for part in range(2):
                 history_ref[begin + at, part] = spectra[at][part]
@@ -320,7 +342,8 @@
                 for from_row in (0, LOAD)
             ]
         )
-    gradient_sums(forward(centered, lambda lines: multiply_window(window_ref[...], lines), sides_ref, twist_ref), out_ref)
+    started = forward_start(centered, lambda lines: multiply_window(window_ref[...], lines), twist_ref)
+    gradient_sums(forward_end([(started, 3)], sides_ref)[0], out_ref)
 
 
 def final_kernel(

time: 136 us -> 136 us (level)
  no operation moved by 1% of the time
where the time goes in v10:
time: 136 us; the launch traced here: 135 us
  blocking collectives  128 us (94%)
  Pallas kernels  6.6 us (5%)
    all_to_all x8, blocking collectives, exchange(): return lax.all_to_all(array, axes, split_axis=0, concat_axis=0, tiled=True)  128 us
    pallas_call x9, Pallas kernels, call(): pl.pallas_call(kernel, out_shape=[jax.ShapeDtypeStruct(*shape) for shape...  6.6 us

profile of v10, /device:TPU:1, one launch (start us, length us, event | category | flops | bytes accessed | tf_op | source)
XLA Modules:
  0.0 135.3 jit_solution(507700676012287601)
XLA Ops:
  0.6 0.0 copy-start
  0.6 1.2 shard_map.95
  1.9 0.0 copy-start.1
  1.9 0.0 copy-start.2
  1.9 26.8 %all_to_all.40.rows_ref = f32[16,8,8,128]{3,2,1,0:T(8,128)S(1)} all-to-all(f32[16,8,8,128]{3,2,1,0:T(8,128)S(1)} %bitcast.14), channel_id=1, replica_groups=mesh['zh'=4,'zl'=2,'x'=4,'yh'=4,'yl'=2,'core'=2] {'yh','yl','core'}, dimensions={0} | all-to-all | bytes 1048576 | tf_op jit(solution)/shard_map/all_to_all | solution.py:382
  28.7 0.0 copy-done
  28.7 0.0 copy-done.1
  28.7 0.0 copy-done.2
  28.7 1.2 shard_map.96
  29.9 12.2 %all_to_all.41.in_ref = f32[32,2,4,128]{3,2,1,0:T(4,128)S(1)} all-to-all(f32[32,2,4,128]{3,2,1,0:T(4,128)S(1)} %get-tuple-element.14), channel_id=1, replica_groups=mesh['zh'=4,'zl'=2,'x'=4,'yh'=4,'yl'=2,'core'=2] {'zl','x','yl','core'}, dimensions={0} | all-to-all | bytes 262144 | tf_op jit(solution)/shard_map/all_to_all | solution.py:382
  42.2 22.2 %all_to_all.42.in_ref = f32[16,2,4,128]{3,2,1,0:T(4,128)S(1)} all-to-all(f32[16,2,4,128]{3,2,1,0:T(4,128)S(1)} %shard_map.97), channel_id=1, replica_groups=mesh['zh'=4,'zl'=2,'x'=4,'yh'=4,'yl'=2,'core'=2] {'zh','yh'}, dimensions={0} | all-to-all | bytes 131072 | tf_op jit(solution)/shard_map/all_to_all | solution.py:382
  64.3 0.0 copy-start.3
  64.4 11.6 %all_to_all.43.gradient_ref = f32[32,4,128]{2,1,0:T(4,128)S(1)} all-to-all(f32[32,4,128]{2,1,0:T(4,128)S(1)} %shard_map.98), channel_id=1, replica_groups=mesh['zh'=4,'zl'=2,'x'=4,'yh'=4,'yl'=2,'core'=2] {'zl','x','yl','core'}, dimensions={0} | all-to-all | bytes 131072 | tf_op jit(solution)/shard_map/all_to_all | solution.py:382
  75.9 0.0 copy-done.3
  75.9 1.8 %shard_map.99 = (f32[32,2,4,128]{3,2,1,0:T(4,128)S(1)}, f32[128,128]{1,0:T(8,128)S(1)}) custom-call(s32[72,128]{1,0:T(8,128)S(1)} %get-tuple-element.12.at_ref, f32[32,4,128]{2,1,0:T(4,128)S(1)} %all_to_all.43.gradient_ref, f32[4,2,128,128]{3,2,1,0:T(8,128)S(1)} %get-tuple-element.15.history_ref, bf16[256,192]{1,0:T(8,128)(2,1)S(1)} %copy-done.2, ...), custom_call_target="tpu_custom_call" | custom-call | tf_op jit(solution)/shard_map/pallas_call | solution.py:370
  77.8 10.1 %all_to_all.44.in_ref = f32[32,2,4,128]{3,2,1,0:T(4,128)S(1)} all-to-all(f32[32,2,4,128]{3,2,1,0:T(4,128)S(1)} %get-tuple-element.16), channel_id=1, replica_groups=mesh['zh'=4,'zl'=2,'x'=4,'yh'=4,'yl'=2,'core'=2] {'zl','x','yl','core'}, dimensions={0} | all-to-all | bytes 262144 | tf_op jit(solution)/shard_map/all_to_all | solution.py:382
  87.9 13.9 %all_to_all.45.in_ref = f32[16,2,4,128]{3,2,1,0:T(4,128)S(1)} all-to-all(f32[16,2,4,128]{3,2,1,0:T(4,128)S(1)} %shard_map.100), channel_id=1, replica_groups=mesh['zh'=4,'zl'=2,'x'=4,'yh'=4,'yl'=2,'core'=2] {'zh','yh'}, dimensions={0} | all-to-all | bytes 131072 | tf_op jit(solution)/shard_map/all_to_all | solution.py:382
  101.7 11.2 %all_to_all.46.gradient_ref = f32[32,4,128]{2,1,0:T(4,128)S(1)} all-to-all(f32[32,4,128]{2,1,0:T(4,128)S(1)} %shard_map.101), channel_id=1, replica_groups=mesh['zh'=4,'zl'=2,'x'=4,'yh'=4,'yl'=2,'core'=2] {'zl','x','yl','core'}, dimensions={0} | all-to-all | bytes 131072 | tf_op jit(solution)/shard_map/all_to_all | solution.py:382
  112.9 1.3 shard_map.102
  114.2 20.2 %all_to_all.47 = f32[16,8,8,128]{3,2,1,0:T(8,128)S(1)} all-to-all(f32[16,8,8,128]{3,2,1,0:T(8,128)S(1)} %get-tuple-element.18), channel_id=1, replica_groups=mesh['zh'=4,'zl'=2,'x'=4,'yh'=4,'yl'=2,'core'=2] {'yh','yl','core'}, dimensions={0} | all-to-all | bytes 1048576 | tf_op jit(solution)/shard_map/all_to_all | solution.py:382
  134.3 0.9 shard_map.103
  (4 shorter events, 0.1 us)
Async XLA Ops:
  0.6 28.1 %copy-start = (bf16[1536,256]{1,0:T(8,128)(2,1)S(1)}, bf16[1536,256]{1,0:T(8,128)(2,1)}, u32[]{:S(2)}) copy-start(bf16[1536,256]{1,0:T(8,128)(2,1)} %constant.11.clone.sides_ref) | copy-start | bytes 2359300
  1.9 26.8 %copy-start.1 = (f32[2,128,128]{2,1,0:T(8,128)S(1)}, f32[2,128,128]{2,1,0:T(8,128)}, u32[]{:S(2)}) copy-start(f32[2,128,128]{2,1,0:T(8,128)} %constant.9.clone.twist_ref) | copy-start | bytes 393220
  1.9 26.8 %copy-start.2 = (bf16[256,192]{1,0:T(8,128)(2,1)S(1)}, bf16[256,192]{1,0:T(8,128)(2,1)}, u32[]{:S(2)}) copy-start(bf16[256,192]{1,0:T(8,128)(2,1)} %constant.10.clone.window_ref) | copy-start | bytes 294916
  64.3 11.6 %copy-start.3 = (f32[2,152,128]{2,1,0:T(8,128)S(1)}, f32[2,152,128]{2,1,0:T(8,128)}, u32[]{:S(2)}) copy-start(f32[2,152,128]{2,1,0:T(8,128)} %constant.8.clone.ring_ref) | copy-start | bytes 466948

commit v11 on v7

--- a/solution.py
+++ b/solution.py
@@ -380,7 +380,7 @@
 
 RNG = ("zh", "zl", "x")
 AZ = ("yh", "yl", "core")
-NEAR = ("zl", "x", "yl", "core")
+NEAR = ("zl", "yl", "core", "x")
 FAR = ("zh", "yh")
 
 

time: 136 us -> 136 us (level)
  no operation moved by 1% of the time
where the time goes in v11:
time: 136 us
  blocking collectives  128 us (94%)
  Pallas kernels  6.73 us (5%)
    all_to_all x8, blocking collectives, exchange(): return lax.all_to_all(array, axes, split_axis=0, concat_axis=0, tiled=True)  128 us
    pallas_call x9, Pallas kernels, call(): pl.pallas_call(kernel, out_shape=[jax.ShapeDtypeStruct(*shape) for shape...  6.73 us

profile of v11, /device:TPU:1, one launch (start us, length us, event | category | flops | bytes accessed | tf_op | source)
XLA Modules:
  0.0 135.6 jit_solution(1137861373010510420)
XLA Ops:
  0.6 0.0 copy-start
  0.6 1.3 shard_map.95
  1.9 0.0 copy-start.1
  2.0 0.0 copy-start.2
  2.0 26.8 %all_to_all.40.rows_ref = f32[16,8,8,128]{3,2,1,0:T(8,128)S(1)} all-to-all(f32[16,8,8,128]{3,2,1,0:T(8,128)S(1)} %bitcast.4), channel_id=1, replica_groups=mesh['zh'=4,'zl'=2,'x'=4,'yh'=4,'yl'=2,'core'=2] {'yh','yl','core'}, dimensions={0} | all-to-all | bytes 1048576 | tf_op jit(solution)/shard_map/all_to_all | solution.py:378
  28.8 0.0 copy-done
  28.8 0.0 copy-done.1
  28.8 0.0 copy-done.2
  28.8 1.3 shard_map.96
  30.0 12.3 %all_to_all.41.in_ref = f32[32,2,4,128]{3,2,1,0:T(4,128)S(1)} all-to-all(f32[32,2,4,128]{3,2,1,0:T(4,128)S(1)} %get-tuple-element.14), channel_id=1, replica_groups=mesh['zh'=4,'zl'=2,'x'=4,'yh'=4,'yl'=2,'core'=2] {'zl','yl','core','x'}, dimensions={0} | all-to-all | bytes 262144 | tf_op jit(solution)/shard_map/all_to_all | solution.py:378
  42.4 22.2 %all_to_all.42.in_ref = f32[16,2,4,128]{3,2,1,0:T(4,128)S(1)} all-to-all(f32[16,2,4,128]{3,2,1,0:T(4,128)S(1)} %shard_map.97), channel_id=1, replica_groups=mesh['zh'=4,'zl'=2,'x'=4,'yh'=4,'yl'=2,'core'=2] {'zh','yh'}, dimensions={0} | all-to-all | bytes 131072 | tf_op jit(solution)/shard_map/all_to_all | solution.py:378
  64.6 0.0 copy-start.3
  64.6 11.5 %all_to_all.43.gradient_ref = f32[32,4,128]{2,1,0:T(4,128)S(1)} all-to-all(f32[32,4,128]{2,1,0:T(4,128)S(1)} %shard_map.98), channel_id=1, replica_groups=mesh['zh'=4,'zl'=2,'x'=4,'yh'=4,'yl'=2,'core'=2] {'zl','yl','core','x'}, dimensions={0} | all-to-all | bytes 131072 | tf_op jit(solution)/shard_map/all_to_all | solution.py:378
  76.1 0.0 copy-done.3
  76.1 1.8 %shard_map.99 = (f32[32,2,4,128]{3,2,1,0:T(4,128)S(1)}, f32[128,128]{1,0:T(8,128)S(1)}) custom-call(s32[72,128]{1,0:T(8,128)S(1)} %get-tuple-element.12.at_ref, f32[32,4,128]{2,1,0:T(4,128)S(1)} %all_to_all.43.gradient_ref, f32[4,2,128,128]{3,2,1,0:T(8,128)S(1)} %get-tuple-element.15.history_ref, bf16[256,192]{1,0:T(8,128)(2,1)S(1)} %copy-done.2, ...), custom_call_target="tpu_custom_call" | custom-call | tf_op jit(solution)/shard_map/pallas_call | solution.py:366
  77.9 10.2 %all_to_all.44.in_ref = f32[32,2,4,128]{3,2,1,0:T(4,128)S(1)} all-to-all(f32[32,2,4,128]{3,2,1,0:T(4,128)S(1)} %get-tuple-element.16), channel_id=1, replica_groups=mesh['zh'=4,'zl'=2,'x'=4,'yh'=4,'yl'=2,'core'=2] {'zl','yl','core','x'}, dimensions={0} | all-to-all | bytes 262144 | tf_op jit(solution)/shard_map/all_to_all | solution.py:378
  88.1 13.9 %all_to_all.45.in_ref = f32[16,2,4,128]{3,2,1,0:T(4,128)S(1)} all-to-all(f32[16,2,4,128]{3,2,1,0:T(4,128)S(1)} %shard_map.100), channel_id=1, replica_groups=mesh['zh'=4,'zl'=2,'x'=4,'yh'=4,'yl'=2,'core'=2] {'zh','yh'}, dimensions={0} | all-to-all | bytes 131072 | tf_op jit(solution)/shard_map/all_to_all | solution.py:378
  102.0 11.1 %all_to_all.46.gradient_ref = f32[32,4,128]{2,1,0:T(4,128)S(1)} all-to-all(f32[32,4,128]{2,1,0:T(4,128)S(1)} %shard_map.101), channel_id=1, replica_groups=mesh['zh'=4,'zl'=2,'x'=4,'yh'=4,'yl'=2,'core'=2] {'zl','yl','core','x'}, dimensions={0} | all-to-all | bytes 131072 | tf_op jit(solution)/shard_map/all_to_all | solution.py:378
  113.2 1.3 shard_map.102
  114.4 20.2 %all_to_all.47 = f32[16,8,8,128]{3,2,1,0:T(8,128)S(1)} all-to-all(f32[16,8,8,128]{3,2,1,0:T(8,128)S(1)} %get-tuple-element.18), channel_id=1, replica_groups=mesh['zh'=4,'zl'=2,'x'=4,'yh'=4,'yl'=2,'core'=2] {'yh','yl','core'}, dimensions={0} | all-to-all | bytes 1048576 | tf_op jit(solution)/shard_map/all_to_all | solution.py:378
  134.6 1.0 shard_map.103
  (4 shorter events, 0.1 us)
Async XLA Ops:
  0.6 28.1 %copy-start = (bf16[1536,256]{1,0:T(8,128)(2,1)S(1)}, bf16[1536,256]{1,0:T(8,128)(2,1)}, u32[]{:S(2)}) copy-start(bf16[1536,256]{1,0:T(8,128)(2,1)} %constant.11.clone.sides_ref) | copy-start | bytes 2359300
  1.9 26.8 %copy-start.1 = (f32[2,128,128]{2,1,0:T(8,128)S(1)}, f32[2,128,128]{2,1,0:T(8,128)}, u32[]{:S(2)}) copy-start(f32[2,128,128]{2,1,0:T(8,128)} %constant.9.clone.twist_ref) | copy-start | bytes 393220
  2.0 26.8 %copy-start.2 = (bf16[256,192]{1,0:T(8,128)(2,1)S(1)}, bf16[256,192]{1,0:T(8,128)(2,1)}, u32[]{:S(2)}) copy-start(bf16[256,192]{1,0:T(8,128)(2,1)} %constant.10.clone.window_ref) | copy-start | bytes 294916
  64.6 11.6 %copy-start.3 = (f32[2,152,128]{2,1,0:T(8,128)S(1)}, f32[2,152,128]{2,1,0:T(8,128)}, u32[]{:S(2)}) copy-start(f32[2,152,128]{2,1,0:T(8,128)} %constant.8.clone.ring_ref) | copy-start | bytes 466948

commit v12 on v7

--- a/solution.py
+++ b/solution.py
@@ -260,9 +260,9 @@
     copies[0].start()
     places = [at_ref[SUB + row, 0] for row in range(bins)]
     for part in range(2):
-        for row in range(bins):
-            tiles_ref[pl.ds(tile_at(bins, part, row), SUB, stride=SUB), :] = rows_ref[places[row] + part * 4]
         for half in range(2):
+            for row in range(half * bins // 2, (half + 1) * bins // 2):
+                tiles_ref[pl.ds(tile_at(bins, part, row), SUB, stride=SUB), :] = rows_ref[places[row] + part * 4]
             span = slice(half * bins // 2, (half + 1) * bins // 2)
             for group in range(half * bins // 2 // SUB, (half + 1) * bins // 2 // SUB):
                 for block in range(SUB):

time: 136 us -> 136 us (level)
  no operation moved by 1% of the time
where the time goes in v12:
time: 136 us; the launch traced here: 135 us
  blocking collectives  128 us (94%)
  Pallas kernels  6.73 us (5%)
    all_to_all x8, blocking collectives, exchange(): return lax.all_to_all(array, axes, split_axis=0, concat_axis=0, tiled=True)  128 us
    pallas_call x9, Pallas kernels, call(): pl.pallas_call(kernel, out_shape=[jax.ShapeDtypeStruct(*shape) for shape...  6.73 us

profile of v12, /device:TPU:1, one launch (start us, length us, event | category | flops | bytes accessed | tf_op | source)
XLA Modules:
  0.0 135.4 jit_solution(17586916203754537599)
XLA Ops:
  0.6 0.0 copy-start
  0.6 1.3 shard_map.95
  1.9 0.0 copy-start.1
  2.0 0.0 copy-start.2
  2.0 26.8 %all_to_all.40.rows_ref = f32[16,8,8,128]{3,2,1,0:T(8,128)S(1)} all-to-all(f32[16,8,8,128]{3,2,1,0:T(8,128)S(1)} %bitcast.4), channel_id=1, replica_groups=mesh['zh'=4,'zl'=2,'x'=4,'yh'=4,'yl'=2,'core'=2] {'yh','yl','core'}, dimensions={0} | all-to-all | bytes 1048576 | tf_op jit(solution)/shard_map/all_to_all | solution.py:378
  28.8 0.0 copy-done
  28.8 0.0 copy-done.1
  28.8 0.0 copy-done.2
  28.8 1.3 shard_map.96
  30.0 12.2 %all_to_all.41.in_ref = f32[32,2,4,128]{3,2,1,0:T(4,128)S(1)} all-to-all(f32[32,2,4,128]{3,2,1,0:T(4,128)S(1)} %get-tuple-element.14), channel_id=1, replica_groups=mesh['zh'=4,'zl'=2,'x'=4,'yh'=4,'yl'=2,'core'=2] {'zl','x','yl','core'}, dimensions={0} | all-to-all | bytes 262144 | tf_op jit(solution)/shard_map/all_to_all | solution.py:378
  42.3 22.2 %all_to_all.42.in_ref = f32[16,2,4,128]{3,2,1,0:T(4,128)S(1)} all-to-all(f32[16,2,4,128]{3,2,1,0:T(4,128)S(1)} %shard_map.97), channel_id=1, replica_groups=mesh['zh'=4,'zl'=2,'x'=4,'yh'=4,'yl'=2,'core'=2] {'zh','yh'}, dimensions={0} | all-to-all | bytes 131072 | tf_op jit(solution)/shard_map/all_to_all | solution.py:378
  64.5 0.0 copy-start.3
  64.5 11.6 %all_to_all.43.gradient_ref = f32[32,4,128]{2,1,0:T(4,128)S(1)} all-to-all(f32[32,4,128]{2,1,0:T(4,128)S(1)} %shard_map.98), channel_id=1, replica_groups=mesh['zh'=4,'zl'=2,'x'=4,'yh'=4,'yl'=2,'core'=2] {'zl','x','yl','core'}, dimensions={0} | all-to-all | bytes 131072 | tf_op jit(solution)/shard_map/all_to_all | solution.py:378
  76.0 0.0 copy-done.3
  76.0 1.8 %shard_map.99 = (f32[32,2,4,128]{3,2,1,0:T(4,128)S(1)}, f32[128,128]{1,0:T(8,128)S(1)}) custom-call(s32[72,128]{1,0:T(8,128)S(1)} %get-tuple-element.12.at_ref, f32[32,4,128]{2,1,0:T(4,128)S(1)} %all_to_all.43.gradient_ref, f32[4,2,128,128]{3,2,1,0:T(8,128)S(1)} %get-tuple-element.15.history_ref, bf16[256,192]{1,0:T(8,128)(2,1)S(1)} %copy-done.2, ...), custom_call_target="tpu_custom_call" | custom-call | tf_op jit(solution)/shard_map/pallas_call | solution.py:366
  77.9 10.1 %all_to_all.44.in_ref = f32[32,2,4,128]{3,2,1,0:T(4,128)S(1)} all-to-all(f32[32,2,4,128]{3,2,1,0:T(4,128)S(1)} %get-tuple-element.16), channel_id=1, replica_groups=mesh['zh'=4,'zl'=2,'x'=4,'yh'=4,'yl'=2,'core'=2] {'zl','x','yl','core'}, dimensions={0} | all-to-all | bytes 262144 | tf_op jit(solution)/shard_map/all_to_all | solution.py:378
  88.0 13.9 %all_to_all.45.in_ref = f32[16,2,4,128]{3,2,1,0:T(4,128)S(1)} all-to-all(f32[16,2,4,128]{3,2,1,0:T(4,128)S(1)} %shard_map.100), channel_id=1, replica_groups=mesh['zh'=4,'zl'=2,'x'=4,'yh'=4,'yl'=2,'core'=2] {'zh','yh'}, dimensions={0} | all-to-all | bytes 131072 | tf_op jit(solution)/shard_map/all_to_all | solution.py:378
  101.9 11.2 %all_to_all.46.gradient_ref = f32[32,4,128]{2,1,0:T(4,128)S(1)} all-to-all(f32[32,4,128]{2,1,0:T(4,128)S(1)} %shard_map.101), channel_id=1, replica_groups=mesh['zh'=4,'zl'=2,'x'=4,'yh'=4,'yl'=2,'core'=2] {'zl','x','yl','core'}, dimensions={0} | all-to-all | bytes 131072 | tf_op jit(solution)/shard_map/all_to_all | solution.py:378
  113.0 1.3 shard_map.102
  114.3 20.2 %all_to_all.47 = f32[16,8,8,128]{3,2,1,0:T(8,128)S(1)} all-to-all(f32[16,8,8,128]{3,2,1,0:T(8,128)S(1)} %get-tuple-element.18), channel_id=1, replica_groups=mesh['zh'=4,'zl'=2,'x'=4,'yh'=4,'yl'=2,'core'=2] {'yh','yl','core'}, dimensions={0} | all-to-all | bytes 1048576 | tf_op jit(solution)/shard_map/all_to_all | solution.py:378
  134.4 1.0 shard_map.103
  (4 shorter events, 0.1 us)
Async XLA Ops:
  0.6 28.1 %copy-start = (bf16[1536,256]{1,0:T(8,128)(2,1)S(1)}, bf16[1536,256]{1,0:T(8,128)(2,1)}, u32[]{:S(2)}) copy-start(bf16[1536,256]{1,0:T(8,128)(2,1)} %constant.11.clone.sides_ref) | copy-start | bytes 2359300
  1.9 26.8 %copy-start.1 = (f32[2,128,128]{2,1,0:T(8,128)S(1)}, f32[2,128,128]{2,1,0:T(8,128)}, u32[]{:S(2)}) copy-start(f32[2,128,128]{2,1,0:T(8,128)} %constant.9.clone.twist_ref) | copy-start | bytes 393220
  2.0 26.8 %copy-start.2 = (bf16[256,192]{1,0:T(8,128)(2,1)S(1)}, bf16[256,192]{1,0:T(8,128)(2,1)}, u32[]{:S(2)}) copy-start(bf16[256,192]{1,0:T(8,128)(2,1)} %constant.10.clone.window_ref) | copy-start | bytes 294916
  64.5 11.6 %copy-start.3 = (f32[2,152,128]{2,1,0:T(8,128)S(1)}, f32[2,152,128]{2,1,0:T(8,128)}, u32[]{:S(2)}) copy-start(f32[2,152,128]{2,1,0:T(8,128)} %constant.8.clone.ring_ref) | copy-start | bytes 466948
